TPU v7x, 256 devices: a whole 4x4x8 slice. The times are simulated.
256 devices in a mesh: pool: 32 (over x, z), ctx: 8 (over y, core).
Axes of the slice: x: 4, y: 4, z: 8, core: 2. Of those that a mesh axis runs over, the one named last changes fastest.
Arguments:
- query_nope: bfloat16 [32, 512, 4096], P('pool', 'ctx'), may hold values from -6 to 6
- query_rope: bfloat16 [32, 512, 2048], P('pool', 'ctx'), may hold values from -600 to 600
- suffix_latent: bfloat16 [32, 512, 512], P('pool', 'ctx'), may hold values from -6 to 6
- suffix_rope: bfloat16 [32, 32768], P('pool', 'ctx'), may hold values from -6 to 6
- absorb_key: bfloat16 [32, 128, 512], replicated, may hold values from -0.5 to 0.5
- absorb_value: bfloat16 [32, 512, 128], replicated, may hold values from -0.25 to 0.25
- pool_latent: bfloat16 [32, 8, 32, 8, 512], P('pool', 'ctx'), may hold values from -6 to 6
- pool_rope: bfloat16 [32, 8, 32, 512], P('pool', 'ctx'), may hold values from -6 to 6
- pool_scale: bfloat16 [32, 8, 32, 8], P('pool', 'ctx'), may hold values from 0.25 to 2
- prefix_tokens: int32 [32], replicated, may hold values from 256 to 2048, as said below
- block_owner: int32 [32, 8, 32], replicated, may hold values from 0 to 31, as said below
- block_slot: int32 [32, 8, 32], replicated, may hold values from 0 to 31, as said below
- write_owner: int32 [32, 8, 8], replicated, may hold values from 0 to 31, as said below
- write_slot: int32 [32, 8, 8], replicated, may hold values from 0 to 7, as said below
Outputs:
- attended: bfloat16 [32, 512, 4096], P('pool', 'ctx')
- written_latent: bfloat16 [32, 8, 8, 8, 512], P('pool', 'ctx')
- written_rope: bfloat16 [32, 8, 8, 512], P('pool', 'ctx')
- written_scale: bfloat16 [32, 8, 8, 8], P('pool', 'ctx')
Inputs may be any that keep to these rules, and one draw needn't show every extreme that they name: `prefix_tokens`: multiples of 8; some request has the longest prefix and some the shortest. `block_owner`: for one request and ctx index, every owner keeps exactly 1 of the 32 blocks. `block_slot`: different blocks at one owner and ctx index have different slots. `write_owner`: the 8 new blocks of one request at one ctx index go to different owners; every owner receives exactly 8 new blocks at each ctx index. `write_slot`: new blocks at one owner and ctx index have different slots.
All inputs are finite; a program needn't handle non-finite values.
Results may differ from a plain program's by a relative error of at most 0.011.
Values may be sent and summed in bfloat16 or wider, within the bound.
No kernel may reach another device: no remote copies, remote signals or barrier semaphores. Data moves between devices by JAX's collectives and lax.ppermute only.
A program may use at most 128 MiB of HBM per device.

v0:
```python
import jax
import jax.numpy as jnp
from jax import lax
from jax.sharding import PartitionSpec as P

neg_large = -1e30
quant_top = 4.0
quant_eps = 1e-06


def owner_ranks(owners):
    count = owners.shape[-1]
    same = owners[..., :, None] == owners[..., None, :]
    earlier = jnp.arange(count)[None, :] < jnp.arange(count)[:, None]
    return jnp.sum(same & earlier, axis=-1)


def dequantize(values, ropes, scales, rope_width):
    block = scales.shape[-1]
    latent = values.shape[-1]
    factor = scales.astype(jnp.float32)[..., None]
    keys = (values.astype(jnp.float32) * factor).astype(jnp.bfloat16)
    shaped = ropes.reshape(ropes.shape[:-1] + (block, rope_width)).astype(jnp.float32)
    key_rope = (shaped * factor).astype(jnp.bfloat16)
    return (keys.reshape(-1, latent), key_rope.reshape(-1, rope_width))


def body(
    query_nope,
    query_rope,
    suffix_latent,
    suffix_rope,
    absorb_key,
    absorb_value,
    pool_latent,
    pool_rope,
    pool_scale,
    prefix_tokens,
    block_owner,
    block_slot,
    write_owner,
    write_slot,
):
    pool_count = lax.axis_size("pool")
    ctx_count = lax.axis_size("ctx")
    own_index = lax.axis_index("pool")
    column = lax.axis_index("ctx")
    heads, nope, latent = absorb_key.shape
    tokens = query_nope.shape[1]
    rope = query_rope.shape[2] // heads
    per_column = block_owner.shape[2]
    block = pool_scale.shape[3]
    capacity = per_column // pool_count
    new_blocks = write_owner.shape[2]
    score_scale = (nope + rope) ** (-0.5)
    absorbed = jnp.einsum(
        "thn,hnl->thl",
        query_nope[0].reshape(tokens, heads, nope),
        absorb_key,
        preferred_element_type=jnp.float32,
    ).astype(jnp.bfloat16)
    rotary = query_rope[0].reshape(tokens, heads, rope)
    group_latent = suffix_latent[0]
    group_rope = suffix_rope[0].reshape(tokens, rope)
    query_place = column * tokens + jnp.arange(tokens)

    def attend(carry, keys, key_rope, visible):
        row_top, row_total, mixed_sum = carry
        scores = jnp.einsum("thl,kl->thk", absorbed, keys, preferred_element_type=jnp.float32)
        scores = scores + jnp.einsum(
            "thr,kr->thk", rotary, key_rope, preferred_element_type=jnp.float32
        )
        scores = jnp.where(visible, scores * score_scale, neg_large)
        new_top = jnp.maximum(row_top, jnp.max(scores, axis=2))
        fade = jnp.exp(row_top - new_top)
        weights_full = jnp.where(visible, jnp.exp(scores - new_top[:, :, None]), 0.0)
        row_total = row_total * fade + jnp.sum(weights_full, axis=2)
        mixed_sum = mixed_sum * fade[:, :, None] + jnp.einsum(
            "thk,kl->thl",
            weights_full.astype(jnp.bfloat16),
            keys,
            preferred_element_type=jnp.float32,
        )
        return (new_top, row_total, mixed_sum)

    begin = (
        jnp.full((tokens, heads), neg_large, jnp.float32),
        jnp.zeros((tokens, heads), jnp.float32),
        jnp.zeros((tokens, heads, latent), jnp.float32),
    )
    piece = (
        lax.all_gather(group_latent[None], "ctx", axis=0, tiled=True),
        lax.all_gather(group_rope[None], "ctx", axis=0, tiled=True),
    )
    count = piece[0].shape[0]
    key_place = jnp.arange(count * tokens)
    visible = (key_place[None, :] <= query_place[:, None])[:, None, :]
    carry = attend(begin, piece[0].reshape(-1, latent), piece[1].reshape(-1, rope), visible)
    whole = (
        lax.all_gather(pool_latent[0], "ctx", axis=0, tiled=True),
        lax.all_gather(pool_rope[0], "ctx", axis=0, tiled=True),
        lax.all_gather(pool_scale[0], "ctx", axis=0, tiled=True),
    )
    every = jnp.arange(ctx_count)
    owners = jnp.take(block_owner, every, axis=1)
    slot_ids = jnp.take(block_slot, every, axis=1)
    ranks = owner_ranks(owners)
    starts = (jnp.arange(per_column)[None, None, :] * ctx_count + every[None, :, None]) * block
    live = (starts < prefix_tokens[:, None, None]) & (owners == own_index)
    matches = live[..., None] & (ranks[..., None] == jnp.arange(capacity))
    found = jnp.any(matches, axis=2)
    index = jnp.sum(jnp.where(matches, slot_ids[..., None], 0), axis=2) + jnp.where(
        found, 0, per_column
    )
    lanes = every[None, :, None]
    padded = [
        jnp.concatenate(
            [member, jnp.zeros((ctx_count, 1) + member.shape[2:], member.dtype)], axis=1
        )
        for member in whole
    ]
    arrived = (
        lax.all_to_all(padded[0][lanes, index], "pool", split_axis=0, concat_axis=0, tiled=True),
        lax.all_to_all(padded[1][lanes, index], "pool", split_axis=0, concat_axis=0, tiled=True),
        lax.all_to_all(padded[2][lanes, index], "pool", split_axis=0, concat_axis=0, tiled=True),
    )
    keys, key_rope = dequantize(arrived[0], arrived[1], arrived[2], rope)
    owners = jnp.take(block_owner[own_index], every, axis=0)
    ranks = owner_ranks(owners)
    starts = (jnp.arange(per_column)[None, :] * ctx_count + every[:, None]) * block
    live = starts < prefix_tokens[own_index]
    matches = (
        (owners[:, :, None, None] == jnp.arange(pool_count)[None, None, :, None])
        & (ranks[:, :, None, None] == jnp.arange(capacity)[None, None, None, :])
        & live[:, :, None, None]
    )
    valid = jnp.transpose(jnp.any(matches, axis=1), (1, 0, 2))
    visible = jnp.repeat(valid.reshape(-1), block)[None, None, :]
    carry = attend(carry, keys, key_rope, visible)
    row_top, row_total, mixed_sum = carry
    mixed = (mixed_sum / row_total[:, :, None]).astype(jnp.bfloat16)
    attended = (
        jnp.einsum("thl,hlv->thv", mixed, absorb_value, preferred_element_type=jnp.float32)
        .astype(jnp.bfloat16)
        .reshape(1, tokens, -1)
    )
    latent_full = group_latent.astype(jnp.float32)
    rotary_full = group_rope.astype(jnp.float32)
    magnitude = jnp.maximum(
        jnp.max(jnp.abs(latent_full), axis=1), jnp.max(jnp.abs(rotary_full), axis=1)
    )
    token_scale = ((magnitude + quant_eps) / quant_top).astype(jnp.bfloat16)
    factor = token_scale.astype(jnp.float32)[:, None]
    code_latent = jnp.concatenate(
        [
            (latent_full / factor).astype(jnp.bfloat16).reshape(new_blocks, block, latent),
            jnp.zeros((1, block, latent), jnp.bfloat16),
        ],
        axis=0,
    )
    code_rotary = jnp.concatenate(
        [
            (rotary_full / factor).astype(jnp.bfloat16).reshape(new_blocks, block * rope),
            jnp.zeros((1, block * rope), jnp.bfloat16),
        ],
        axis=0,
    )
    code_scale = jnp.concatenate(
        [token_scale.reshape(new_blocks, block), jnp.zeros((1, block), jnp.bfloat16)], axis=0
    )
    targets = write_owner[own_index, column]
    chosen = targets[None, :] == jnp.arange(pool_count)[:, None]
    pick = jnp.sum(jnp.where(chosen, jnp.arange(new_blocks)[None, :], 0), axis=1) + jnp.where(
        jnp.any(chosen, axis=1), 0, new_blocks
    )
    returned = (
        lax.all_to_all(code_latent[pick], "pool", split_axis=0, concat_axis=0, tiled=True),
        lax.all_to_all(code_rotary[pick], "pool", split_axis=0, concat_axis=0, tiled=True),
        lax.all_to_all(code_scale[pick], "pool", split_axis=0, concat_axis=0, tiled=True),
    )
    column_owner = write_owner[:, column]
    column_slot = write_slot[:, column]
    lands = (column_owner == own_index)[:, :, None] & (
        column_slot[:, :, None] == jnp.arange(new_blocks)[None, None, :]
    )
    source = jnp.sum(jnp.where(lands, jnp.arange(pool_count)[:, None, None], 0), axis=(0, 1))
    written_latent = returned[0][source][None, None]
    written_rope = returned[1][source][None, None]
    written_scale = returned[2][source][None, None]
    return (attended, written_latent, written_rope, written_scale)


def solution(mesh):
    placed = (
        P("pool", "ctx", None),
        P("pool", "ctx", None),
        P("pool", "ctx", None),
        P("pool", "ctx"),
        P(),
        P(),
        P("pool", "ctx", None, None, None),
        P("pool", "ctx", None, None),
        P("pool", "ctx", None, None),
        P(),
        P(),
        P(),
        P(),
        P(),
    )
    return jax.shard_map(
        body,
        mesh=mesh,
        in_specs=placed,
        out_specs=(
            P("pool", "ctx", None),
            P("pool", "ctx", None, None, None),
            P("pool", "ctx", None, None),
            P("pool", "ctx", None, None),
        ),
        check_vma=False,
    )
```

profile of v0, /device:TPU:1, one launch (start us, length us, event | category | flops | bytes accessed | tf_op | source)
XLA Modules:
  0.0 238.5 jit_solution(16151136266853707019)
XLA Ops:
  7.2 0.7 all-gather.5.cloned.1.call-update
  7.9 0.9 dynamic-slice_reduce_fusion
  9.0 0.8 convert_reduce_fusion.2
  9.9 1.0 fusion.26
  12.4 11.9 %all-to-all-start.5 = ((bf16[32,1,8]{2,1,0:T(2,128)(2,1)}), bf16[32,1,8]{2,1,0:T(2,128)(2,1)S(1)}, u32[]{:S(2)}, u32[]{:S(2)}) async-start(bf16[32,1,8]{2,1,0:T(2,128)(2,1)} %copy.160), calls=%async_computation.5 | async-start | bytes 32768 | tf_op jit(solution)/shard_map/all_to_all | solution.py:179
  24.3 0.7 gather_fusion.10
  25.0 1.7 gather_fusion.11
  26.8 5.8 %convert_reduce_fusion = s32[32,8,32]{2,1,0:T(8,128)S(1)} fusion(s32[32,8,32]{2,1,0:T(8,128)S(1)} %select_bitcast_fusion, pred[32,32]{1,0:T(8,128)(4,1)S(1)} %iota_compare_fusion.4), kind=kLoop, calls=%fused_computation.22 | loop fusion | flops 1040384 | bytes 66560 | tf_op jit(solution)/shard_map/reduce_sum | solution.py:15
  32.7 1.4 fusion.40
  34.0 0.7 fusion.27
  34.8 12.9 %all-gather.1 = bf16[8,1,32,8]{2,3,1,0:T(8,128)(2,1)S(1)} all-gather(bf16[1,1,32,8]{2,3,1,0:T(8,128)(2,1)S(1)} %copy-done.17), channel_id=3, replica_groups=mesh['pool'=32,'ctx'=8] {'ctx'}, dimensions={0}, use_global_device_ids=true | all-gather | bytes 4608 | tf_op jit(solution)/shard_map/all_gather | solution.py:102
  48.1 2.2 gather_fusion.2
  50.3 9.5 %all-to-all-start.1 = ((bf16[32,8,1,8]{3,1,2,0:T(8,128)(2,1)}), bf16[32,8,1,8]{3,1,2,0:T(8,128)(2,1)S(1)}, u32[]{:S(2)}, u32[]{:S(2)}) async-start(bf16[32,8,1,8]{3,1,2,0:T(8,128)(2,1)} %bitcast.19), calls=%async_computation.1 | async-start | bytes 131072 | tf_op jit(solution)/shard_map/all_to_all | solution.py:125
  62.3 6.4 %all-to-all-done.1 = bf16[32,8,1,8]{3,1,2,0:T(8,128)(2,1)S(1)} async-done(((bf16[32,8,1,8]{3,1,2,0:T(8,128)(2,1)}), bf16[32,8,1,8]{3,1,2,0:T(8,128)(2,1)S(1)}, u32[]{:S(2)}, u32[]{:S(2)}) %all-to-all-start.1) | async-done | bytes 4128 | tf_op jit(solution)/shard_map/all_to_all | solution.py:125
  68.7 3.9 %all-to-all-start.4 = ((bf16[32,2,256]{2,1,0:T(2,128)(2,1)}), bf16[32,2,256]{2,1,0:T(2,128)(2,1)S(1)}, u32[]{:S(2)}, u32[]{:S(2)}) async-start(bf16[32,2,256]{2,1,0:T(2,128)(2,1)} %reshape.534), calls=%async_computation.4 | async-start | bytes 65536 | tf_op jit(solution)/shard_map/all_to_all | solution.py:178
  72.6 14.3 %all-gather.2 = bf16[8,1,32,512]{3,2,1,0:T(8,128)(2,1)S(1)} all-gather(bf16[1,1,32,512]{3,2,1,0:T(8,128)(2,1)S(1)} %copy-done.15), channel_id=4, replica_groups=mesh['pool'=32,'ctx'=8] {'ctx'}, dimensions={0}, use_global_device_ids=true | all-gather | bytes 294912 | tf_op jit(solution)/shard_map/all_gather | solution.py:101
  87.0 2.7 %gather_fusion.3 = bf16[256,512]{1,0:T(8,128)(2,1)} fusion(bf16[8,33,512]{2,0,1:T(8,128)(2,1)S(1)} %concatenate.26, s32[256]{0:T(256)S(1)} %reshape.434), kind=kCustom, calls=%fused_computation.5 | custom fusion | bytes 526336 | tf_op jit(solution)/shard_map/gather | solution.py:124
  89.8 9.5 %all-to-all-start.2 = ((bf16[32,8,1,512]{3,1,2,0:T(8,128)(2,1)}), bf16[32,8,1,512]{3,1,2,0:T(8,128)(2,1)S(1)}, u32[]{:S(2)}, u32[]{:S(2)}) async-start(bf16[32,8,1,512]{3,1,2,0:T(8,128)(2,1)} %bitcast.25), calls=%async_computation.2 | async-start | bytes 524288 | tf_op jit(solution)/shard_map/all_to_all | solution.py:124
  99.4 1.3 gather_fusion.4
  100.7 8.7 %all-to-all-done.2 = bf16[32,8,1,512]{3,1,2,0:T(8,128)(2,1)S(1)} async-done(((bf16[32,8,1,512]{3,1,2,0:T(8,128)(2,1)}), bf16[32,8,1,512]{3,1,2,0:T(8,128)(2,1)S(1)}, u32[]{:S(2)}, u32[]{:S(2)}) %all-to-all-start.2) | async-done | bytes 262176 | tf_op jit(solution)/shard_map/all_to_all | solution.py:124
  109.4 6.5 %all-to-all-start.3 = ((bf16[32,8,512]{2,1,0:T(8,128)(2,1)}), bf16[32,8,512]{2,1,0:T(8,128)(2,1)S(1)}, u32[]{:S(2)}, u32[]{:S(2)}) async-start(bf16[32,8,512]{2,1,0:T(8,128)(2,1)} %gather_fusion.4), calls=%async_computation.3 | async-start | bytes 524288 | tf_op jit(solution)/shard_map/all_to_all | solution.py:177
  116.0 1.7 concatenate.23
  117.7 2.5 %gather_fusion.1 = bf16[256,8,512]{2,1,0:T(8,128)(2,1)} fusion(bf16[8,33,8,512]{3,2,1,0:T(8,128)(2,1)S(1)} %concatenate.23, s32[256]{0:T(256)S(1)} %reshape.434), kind=kCustom, calls=%fused_computation.3 | custom fusion | bytes 4196352 | tf_op jit(solution)/shard_map/gather | solution.py:123
  120.2 5.4 %all-to-all-done.3 = bf16[32,8,512]{2,1,0:T(8,128)(2,1)S(1)} async-done(((bf16[32,8,512]{2,1,0:T(8,128)(2,1)}), bf16[32,8,512]{2,1,0:T(8,128)(2,1)S(1)}, u32[]{:S(2)}, u32[]{:S(2)}) %all-to-all-start.3) | async-done | bytes 262176 | tf_op jit(solution)/shard_map/all_to_all | solution.py:177
  125.6 6.2 %all-to-all-start = ((bf16[32,8,1,8,512]{4,3,1,2,0:T(8,128)(2,1)}), bf16[32,8,1,8,512]{4,3,1,2,0:T(8,128)(2,1)S(1)}, u32[]{:S(2)}, u32[]{:S(2)}) async-start(bf16[32,8,1,8,512]{4,3,1,2,0:T(8,128)(2,1)} %bitcast.112), calls=%async_computation | async-start | bytes 4194304 | tf_op jit(solution)/shard_map/all_to_all | solution.py:123
  134.6 0.7 broadcast_in_dim.121
  135.4 1.5 reshape_squeeze.8
  137.0 14.7 %all_gather.16 = bf16[8,64,64]{2,1,0:T(8,128)(2,1)S(1)} all-gather(bf16[1,64,64]{2,1,0:T(8,128)(2,1)S(1)} %broadcast_in_dim_reshape_squeeze.3), channel_id=1, replica_groups=mesh['pool'=32,'ctx'=8] {'ctx'}, dimensions={0}, use_global_device_ids=true | all-gather | bytes 73728 | tf_op jit(solution)/shard_map/all_gather | solution.py:93
  151.7 13.1 %all_gather.15 = bf16[8,64,512]{2,1,0:T(8,128)(2,1)S(1)} all-gather(bf16[1,64,512]{2,1,0:T(8,128)(2,1)S(1)} %copy-done.8), channel_id=1, replica_groups=mesh['pool'=32,'ctx'=8] {'ctx'}, dimensions={0}, use_global_device_ids=true | all-gather | bytes 589824 | tf_op jit(solution)/shard_map/all_gather | solution.py:92
  164.9 3.1 %convert_bitcast_fusion = bf16[64,32,512]{2,0,1:T(8,128)(2,1)S(1)} fusion(bf16[32,128,512]{2,1,0:T(8,128)(2,1)} %param.20, bf16[64,32,128]{2,1,0:T(8,128)(2,1)S(1)} %bitcast.118), kind=kOutput, calls=%fused_computation.28 | convolution fusion | flops 269484032 | bytes 6815744 | tf_op jit(solution)/shard_map/thn,hnl->thl/dot_general | solution.py:56
  168.0 1.7 fusion.11
  169.7 2.8 %fusion.41 = (f32[64,32]{1,0:T(8,128)S(1)}, f32[64,32,512]{2,1,0:T(8,128)}) fusion(f32[64,32,512]{2,1,0:T(8,128)S(1)} %fusion.11, bf16[64,32,64]{2,1,0:T(8,128)(2,1)S(1)} %reshape_squeeze.8, bf16[512,64,1]{1,0,2:T(8,128)(2,1)S(1)} %bitcast.120, pred[64,512]{1,0:T(8,128)(4,1)S(1)} %iota_compare_fusion.1), kind=kOutput, calls=%fused_computation.102 | convolution fusion | flops 138409984 | bytes 8757248 | tf_op jit(solution)/shard_map/thr,kr->thk/dot_general | solution.py:70
  172.6 0.7 fusion.36
  173.3 0.7 dynamic-slice_bitcast_fusion
  174.1 1.1 gather_fusion.9
  175.3 1.3 mul.112
  176.6 1.5 mul.113
  178.2 1.2 gather_fusion.7
  179.3 1.0 multiply_convert_fusion.1
  180.6 2.3 gather_fusion.5
  183.4 1.4 copy-done.4
  184.8 5.4 %fusion.9 = f32[64,32,2048]{2,1,0:T(8,128)S(1)} fusion(bf16[2048,512,1]{1,0,2:T(8,128)(2,1)S(1)} %bitcast.114, bf16[64,32,512]{2,0,1:T(8,128)(2,1)S(1)} %copy-done.3), kind=kOutput, calls=%fused_computation.29 | convolution fusion | flops 4294967296 | bytes 20971520 | tf_op jit(solution)/shard_map/thl,kl->thk/dot_general | solution.py:69
  190.2 7.5 %fusion.42 = (f32[64,32]{1,0:T(8,128)S(1)}, f32[64,32,2048]{2,1,0:T(8,128)}) fusion(f32[64,32,2048]{2,1,0:T(8,128)S(1)} %fusion.9, bf16[64,32,64]{2,1,0:T(8,128)(2,1)S(1)} %reshape_squeeze.8, bf16[2048,64]{1,0:T(8,128)(2,1)S(1)} %convert_element_type.109, pred[2048]{0:T(1024)(128)(4,1)S(1)} %copy-done.14), kind=kOutput, calls=%fused_computation.103 | convolution fusion | flops 553646080 | bytes 34088960 | tf_op jit(solution)/shard_map/thr,kr->thk/dot_general | solution.py:70
  197.9 3.0 %fusion.6 = (f32[64,32]{1,0:T(8,128)S(1)}, bf16[64,32,512]{2,1,0:T(8,128)(2,1)S(1)}) fusion(f32[64,32,512]{2,1,0:T(8,128)} %get-tuple-element.19, f32[64,32]{1,0:T(8,128)S(1)} %copy.141, pred[64,512]{1,0:T(8,128)(4,1)S(1)} %copy-done.12), kind=kLoop, calls=%fused_computation.25 | loop fusion | flops 4192256 | bytes 6340608 | tf_op jit(solution)/shard_map/reduce_sum | solution.py:77
  201.1 10.1 %fusion.2 = (f32[64,32]{1,0:T(8,128)S(1)}, bf16[64,32,2048]{2,1,0:T(8,128)(2,1)}) fusion(f32[64,32,2048]{2,1,0:T(8,128)} %get-tuple-element.21, f32[64,32]{1,0:T(8,128)S(1)} %copy.154, pred[2048]{0:T(1024)(128)(4,1)S(1)} %copy-done.14), kind=kLoop, calls=%fused_computation.16 | loop fusion | flops 16775168 | bytes 25184256 | tf_op jit(solution)/shard_map/reduce_sum | solution.py:77
  211.3 12.6 %fusion.4 = f32[64,32,512]{2,0,1:T(8,128)} fusion(bf16[2048,512,1]{1,0,2:T(8,128)(2,1)} %bitcast.115, bf16[64,32,2048]{2,1,0:T(8,128)(2,1)} %get-tuple-element.12), kind=kOutput, calls=%fused_computation.18 | convolution fusion | flops 4294967296 | bytes 14680064 | tf_op jit(solution)/shard_map/thk,kl->thl/dot_general | solution.py:78
  223.9 6.4 %fusion.19 = bf16[64,32,128]{2,0,1:T(8,128)(2,1)S(1)} fusion(bf16[32,512,128]{2,1,0:T(8,128)(2,1)} %param.21, f32[64,32,512]{2,0,1:T(8,128)} %fusion.4, bf16[512,512,1]{1,0,2:T(8,128)(2,1)S(1)} %bitcast.117, bf16[64,32,512]{2,1,0:T(8,128)(2,1)S(1)} %get-tuple-element.14, f32[64,32]{0,1:T(8,128)S(1)} %get-tuple-element.7, ...), kind=kOutput, calls=%fused_computation.35 | convolution fusion | flops 1347682304 | bytes 11558912 | tf_op jit(solution)/shard_map/thl,hlv->thv/dot_general | solution.py:143
  230.6 1.0 reshape.404
  (117 shorter events, 10.0 us)
Async XLA Ops:
  7.2 17.1 %copy-start = (s32[32,8,32]{2,1,0:T(8,128)S(1)}, s32[32,8,32]{2,1,0:T(8,128)}, u32[]{:S(2)}) copy-start(s32[32,8,32]{2,1,0:T(8,128)} %param.26) | copy-start | bytes 98308
  7.2 27.6 %copy-start.17 = (bf16[1,1,32,8]{2,3,1,0:T(8,128)(2,1)S(1)}, bf16[1,1,32,8]{2,3,1,0:T(8,128)(2,1)}, u32[]{:S(2)}) copy-start(bf16[1,1,32,8]{2,3,1,0:T(8,128)(2,1)} %param.24) | copy-start | bytes 1540
  7.2 65.4 %copy-start.15 = (bf16[1,1,32,512]{3,2,1,0:T(8,128)(2,1)S(1)}, bf16[1,1,32,512]{3,2,1,0:T(8,128)(2,1)}, u32[]{:S(2)}) copy-start(bf16[1,1,32,512]{3,2,1,0:T(8,128)(2,1)} %param.23) | copy-start | bytes 98308
  7.2 108.7 %all-gather.5.cloned.1.call-start = ((), (), s32[]{:S(2)}) async-start(), calls=%async_computation.6 | async-start | bytes 2359296 | tf_op jit(solution)/shard_map/all_gather | solution.py:100
  12.4 37.9 %all-to-all-start.5 = ((bf16[32,1,8]{2,1,0:T(2,128)(2,1)}), bf16[32,1,8]{2,1,0:T(2,128)(2,1)S(1)}, u32[]{:S(2)}, u32[]{:S(2)}) async-start(bf16[32,1,8]{2,1,0:T(2,128)(2,1)} %copy.160), calls=%async_computation.5 | async-start | bytes 32768 | tf_op jit(solution)/shard_map/all_to_all | solution.py:179
  25.0 74.3 %copy-start.8 = (bf16[1,64,512]{2,1,0:T(8,128)(2,1)S(1)}, bf16[1,64,512]{2,1,0:T(8,128)(2,1)}, u32[]{:S(2)}) copy-start(bf16[1,64,512]{2,1,0:T(8,128)(2,1)} %param.18) | copy-start | bytes 196612
  50.3 18.4 %all-to-all-start.1 = ((bf16[32,8,1,8]{3,1,2,0:T(8,128)(2,1)}), bf16[32,8,1,8]{3,1,2,0:T(8,128)(2,1)S(1)}, u32[]{:S(2)}, u32[]{:S(2)}) async-start(bf16[32,8,1,8]{3,1,2,0:T(8,128)(2,1)} %bitcast.19), calls=%async_computation.1 | async-start | bytes 131072 | tf_op jit(solution)/shard_map/all_to_all | solution.py:125
  68.7 21.1 %all-to-all-start.4 = ((bf16[32,2,256]{2,1,0:T(2,128)(2,1)}), bf16[32,2,256]{2,1,0:T(2,128)(2,1)S(1)}, u32[]{:S(2)}, u32[]{:S(2)}) async-start(bf16[32,2,256]{2,1,0:T(2,128)(2,1)} %reshape.534), calls=%async_computation.4 | async-start | bytes 65536 | tf_op jit(solution)/shard_map/all_to_all | solution.py:178
  89.8 19.6 %all-to-all-start.2 = ((bf16[32,8,1,512]{3,1,2,0:T(8,128)(2,1)}), bf16[32,8,1,512]{3,1,2,0:T(8,128)(2,1)S(1)}, u32[]{:S(2)}, u32[]{:S(2)}) async-start(bf16[32,8,1,512]{3,1,2,0:T(8,128)(2,1)} %bitcast.25), calls=%async_computation.2 | async-start | bytes 524288 | tf_op jit(solution)/shard_map/all_to_all | solution.py:124
  109.4 6.6 %copy-start.7 = (bf16[32,8,1,512]{3,1,2,0:T(8,128)(2,1)}, bf16[32,8,1,512]{3,1,2,0:T(8,128)(2,1)S(1)}, u32[]{:S(2)}) copy-start(bf16[32,8,1,512]{3,1,2,0:T(8,128)(2,1)S(1)} %all-to-all-done.2) | copy-start | bytes 786436
  109.4 16.2 %all-to-all-start.3 = ((bf16[32,8,512]{2,1,0:T(8,128)(2,1)}), bf16[32,8,512]{2,1,0:T(8,128)(2,1)S(1)}, u32[]{:S(2)}, u32[]{:S(2)}) async-start(bf16[32,8,512]{2,1,0:T(8,128)(2,1)} %gather_fusion.4), calls=%async_computation.3 | async-start | bytes 524288 | tf_op jit(solution)/shard_map/all_to_all | solution.py:177
  117.7 14.1 %copy-start.18 = (s32[32]{0:T(128)S(1)}, s32[32]{0:T(128)}, u32[]{:S(2)}) copy-start(s32[32]{0:T(128)} %param.25) | copy-start | bytes 388
  117.7 14.7 %copy-start.13 = (bf16[1,4096]{1,0:T(2,128)(2,1)S(1)}, bf16[1,4096]{1,0:T(2,128)(2,1)}, u32[]{:S(2)}) copy-start(bf16[1,4096]{1,0:T(2,128)(2,1)} %param.19) | copy-start | bytes 24580
  120.2 15.1 %copy-start.9 = (bf16[1,64,4096]{2,1,0:T(8,128)(2,1)S(1)}, bf16[1,64,4096]{2,1,0:T(8,128)(2,1)}, u32[]{:S(2)}) copy-start(bf16[1,64,4096]{2,1,0:T(8,128)(2,1)} %param.16) | copy-start | bytes 1572868
  125.6 9.7 %copy-start.10 = (bf16[32,8,512]{2,1,0:T(8,128)(2,1)}, bf16[32,8,512]{2,1,0:T(8,128)(2,1)S(1)}, u32[]{:S(2)}) copy-start(bf16[32,8,512]{2,1,0:T(8,128)(2,1)S(1)} %all-to-all-done.3) | copy-start | bytes 786436
  125.6 57.3 %all-to-all-start = ((bf16[32,8,1,8,512]{4,3,1,2,0:T(8,128)(2,1)}), bf16[32,8,1,8,512]{4,3,1,2,0:T(8,128)(2,1)S(1)}, u32[]{:S(2)}, u32[]{:S(2)}) async-start(bf16[32,8,1,8,512]{4,3,1,2,0:T(8,128)(2,1)} %bitcast.112), calls=%async_computation | async-start | bytes 4194304 | tf_op jit(solution)/shard_map/all_to_all | solution.py:123
  151.7 18.0 %copy-start.11 = (pred[64,512]{1,0:T(8,128)(4,1)}, pred[64,512]{1,0:T(8,128)(4,1)S(1)}, u32[]{:S(2)}) copy-start(pred[64,512]{1,0:T(8,128)(4,1)S(1)} %iota_compare_fusion.1) | copy-start | bytes 98308
  164.9 4.8 %copy-start.5 = (bf16[8,64,512]{2,1,0:T(8,128)(2,1)}, bf16[8,64,512]{2,1,0:T(8,128)(2,1)S(1)}, u32[]{:S(2)}) copy-start(bf16[8,64,512]{2,1,0:T(8,128)(2,1)S(1)} %all_gather.15) | copy-start | bytes 1572868
  168.0 4.6 %copy-start.2 = (bf16[64,32,512]{2,0,1:T(8,128)(2,1)}, bf16[64,32,512]{2,0,1:T(8,128)(2,1)S(1)}, u32[]{:S(2)}) copy-start(bf16[64,32,512]{2,0,1:T(8,128)(2,1)S(1)} %convert_bitcast_fusion) | copy-start | bytes 6291460
  174.1 4.0 %copy-start.16 = (s32[1024]{0:T(1024)}, s32[1024]{0:T(1024)S(1)}, u32[]{:S(2)}) copy-start(s32[1024]{0:T(1024)S(1)} %pad_clamp_fusion) | copy-start | bytes 12292
  182.9 1.9 copy-start.3
  183.4 1.4 copy-start.4
  184.8 5.4 %copy-start.14 = (pred[2048]{0:T(1024)(128)(4,1)S(1)}, pred[2048]{0:T(1024)(128)(4,1)}, u32[]{:S(2)}) copy-start(pred[2048]{0:T(1024)(128)(4,1)} %broadcast_in_dim.121) | copy-start | bytes 6148
  190.2 7.7 %copy-start.12 = (pred[64,512]{1,0:T(8,128)(4,1)S(1)}, pred[64,512]{1,0:T(8,128)(4,1)}, u32[]{:S(2)}) copy-start(pred[64,512]{1,0:T(8,128)(4,1)} %copy-done.11) | copy-start | bytes 98308
  211.3 12.6 %copy-start.6 = (bf16[8,64,512]{2,1,0:T(8,128)(2,1)S(1)}, bf16[8,64,512]{2,1,0:T(8,128)(2,1)}, u32[]{:S(2)}) copy-start(bf16[8,64,512]{2,1,0:T(8,128)(2,1)} %copy-done.5) | copy-start | bytes 1572868
  223.9 7.8 %copy-start.1 = (s32[32,8,32]{2,1,0:T(8,128)S(1)}, s32[32,8,32]{2,1,0:T(8,128)}, u32[]{:S(2)}) copy-start(s32[32,8,32]{2,1,0:T(8,128)} %param.26) | copy-start | bytes 98308
Sparse Core Ops, SparseCore 0:
  9.9 31.9 all-gather.4
where the time goes:
time: 240 us; the launch traced here: 239 us
  blocking collectives  55 us (23%)
  starting transfers between devices  47.5 us (20%)
  matrix products  39.5 us (16%)
  local copies, waits for them, and re-layouts  33 us (14%)
  other arithmetic  27.7 us (12%)
  waiting for transfers between devices  21.2 us (9%)
  between operations  14.7 us (6%)
    all_gather x1, blocking collectives, body(): lax.all_gather(group_rope[None], 'ctx', axis=0, tiled=True)  14.7 us
    all_gather x1, blocking collectives, body(): lax.all_gather(pool_rope[0], 'ctx', axis=0, tiled=True)  14.3 us
    all_gather x1, blocking collectives, body(): lax.all_gather(group_latent[None], 'ctx', axis=0, tiled=True)  13.1 us
    reduce_sum x2, other arithmetic, attend(): row_total = row_total * fade + jnp.sum(weights_full, axis=2)  13.1 us
    all_gather x1, blocking collectives, body(): lax.all_gather(pool_scale[0], 'ctx', axis=0, tiled=True)  12.9 us
    dot_general x1, matrix products, attend(): jnp.einsum('thk,kl->thl', weights_full.astype(jnp.bfloat16), keys, prefer...  12.6 us
    all_to_all x1, starting transfers between devices, body(): lax.all_to_all(code_scale[pick], 'pool', split_axis=0, concat_axis=0, til...  11.9 us
    dot_general x2, matrix products, attend(): jnp.einsum('thr,kr->thk', rotary, key_rope, preferred_element_type=jnp.fl...  10.4 us
  transfers between devices with their start and end apart: 7, of which 3 were waited for; matrix products, arithmetic and copies ran while one was open for 22% of the time, Pallas kernels for 0%

commit v1 on v0

v1 whole, which is shorter than its diff:
```python
import functools

import jax
import jax.numpy as jnp
from jax import lax
from jax.experimental import pallas as pl
from jax.experimental.pallas import tpu as pltpu
from jax.sharding import PartitionSpec as P

HIDDEN = -1e30
QUANT_TOP = 4.0
QUANT_EPS = 1e-06
MIB = 1 << 20

F32 = jnp.float32
BF16 = jnp.bfloat16
VMEM = pl.BlockSpec(memory_space=pltpu.VMEM)
SMEM = pl.BlockSpec(memory_space=pltpu.SMEM)


def iota(shape, axis):
    return lax.broadcasted_iota(jnp.int32, shape, axis)


def dot(a, b):
    return jnp.dot(a, b, preferred_element_type=F32)


def dot_nt(a, b):
    return lax.dot_general(a, b, (((1,), (1,)), ((), ())), preferred_element_type=F32)


def fold_matrix(block, rope, lanes):
    shape = (block * rope, lanes)
    return (iota(shape, 0) % rope == iota(shape, 1)).astype(F32).astype(BF16)


def pick_column(table, column):
    return jnp.sum(jnp.where(iota(table.shape, 1) == column, table, 0), axis=1)


def pack_kernel(
    ids, latent, ropes, scales, sfx_latent, sfx_rope, prefix, owners, slots, targets, message, suffix
):
    own, column = ids[0], ids[1]
    count, block, width = latent.shape
    rope = ropes.shape[1] // block
    ctx = owners.shape[1]
    tokens = sfx_latent.shape[0]
    tail = message.shape[2] - width
    rows = 2 * block * count
    fold = fold_matrix(block, rope, tail)

    cube = (count, block, block)
    factor = jnp.broadcast_to(scales[...].astype(F32)[:, None, :], cube)
    factor = jnp.sum(jnp.where(iota(cube, 1) == iota(cube, 2), factor, 0.0), axis=2, keepdims=True)
    keys = (latent[...].astype(F32) * factor).reshape(count * block, width).astype(BF16)
    wide = (count, block, block * rope)
    spread = jnp.broadcast_to(ropes[...].astype(F32)[:, None, :], wide) * factor
    spread = jnp.where(iota(wide, 2) // rope == iota(wide, 1), spread, 0.0)
    key_tail = dot(spread.reshape(count * block, block * rope).astype(BF16), fold).astype(BF16)

    own_latent = sfx_latent[...].astype(F32)
    pieces = []
    for g in range(tokens // block):
        piece = sfx_rope[:, g * block * rope : (g + 1) * block * rope].astype(F32)
        piece = jnp.broadcast_to(piece, (block, block * rope))
        pieces.append(jnp.where(iota(piece.shape, 1) // rope == iota(piece.shape, 0), piece, 0.0))
    own_tail = dot(jnp.concatenate(pieces, axis=0).astype(BF16), fold)
    suffix[:, :width] = sfx_latent[...]
    suffix[:, width:] = own_tail.astype(BF16)
    magnitude = jnp.maximum(
        jnp.max(jnp.abs(own_latent), axis=1, keepdims=True),
        jnp.max(jnp.abs(own_tail), axis=1, keepdims=True),
    )
    token_scale = ((magnitude + QUANT_EPS) / QUANT_TOP).astype(BF16).astype(F32)
    code = (own_latent / token_scale).astype(BF16)
    code_tail = jnp.where(iota(own_tail.shape, 1) == rope, token_scale, own_tail / token_scale)
    code_tail = code_tail.astype(BF16)

    def by_row(table):
        table = pick_column(table, column)[:, None, :]
        return jnp.broadcast_to(table, (count, 2 * block, table.shape[2])).reshape(rows, table.shape[2])

    owner_rows = by_row(owners[...])
    mine = owner_rows == own
    slot = jnp.sum(jnp.where(mine, by_row(slots[...]), 0), axis=1, keepdims=True)
    place = jnp.sum(jnp.where(mine, iota(mine.shape, 1), 0), axis=1, keepdims=True)
    row = iota((rows, 1), 0)
    unit = row % (2 * block)
    limit_shape = (rows, count)
    limit = jnp.where(
        iota(limit_shape, 1) == iota(limit_shape, 0) // (2 * block),
        jnp.broadcast_to(prefix[...], limit_shape),
        0,
    )
    limit = jnp.sum(limit, axis=1, keepdims=True)
    read = unit < block
    bias = jnp.where(read & ((place * ctx + column) * block >= limit), HIDDEN, 0.0)
    source = jnp.where(read, slot * block + unit, -1)
    take_read = (iota((rows, count * block), 1) == source).astype(F32).astype(BF16)
    mark = jnp.sum(jnp.where(iota(targets.shape, 0) == own, targets[...], 0), axis=0)
    mark = jnp.sum(jnp.where(iota(mark.shape, 0) == column, mark, 0), axis=0, keepdims=True)
    new = mark.shape[1]
    mark = jnp.broadcast_to(mark, (tokens, new))
    mark = jnp.sum(jnp.where(iota(mark.shape, 1) == iota(mark.shape, 0) // block, mark, 0), axis=1, keepdims=True)
    mark = mark * (2 * block) + block + iota((tokens, 1), 0) % block
    square = (tokens, tokens)
    mark = jnp.where(iota(square, 0) == iota(square, 1), jnp.broadcast_to(mark, square), 0)
    mark = jnp.sum(mark, axis=0, keepdims=True)
    take_new = (iota((rows, tokens), 0) == mark).astype(F32).astype(BF16)

    body = dot(take_read, keys) + dot(take_new, code)
    end = dot(take_read, key_tail) + dot(take_new, code_tail)
    end = end + jnp.where(iota(end.shape, 1) == rope, bias, 0.0)
    message[:, :, :width] = body.astype(BF16).reshape(count, 2 * block, width)
    message[:, :, width:] = end.astype(BF16).reshape(count, 2 * block, tail)


def shard_kernel(arrived, suffix, shard):
    count, double, width = arrived.shape
    block = double // 2
    shard[: count * block, :] = (
        arrived[...].astype(F32)[:, :block, :].reshape(count * block, width).astype(BF16)
    )
    shard[count * block :, :] = suffix[...]


def land_kernel(ids, arrived, targets, slots, out_latent, out_rope, out_scale):
    own, column = ids[0], ids[1]
    new, block, width = out_latent.shape
    count = arrived.shape[0]
    rope = out_rope.shape[1] // block
    tail = arrived.shape[2] - width
    target = pick_column(targets[...], column)
    slot = pick_column(slots[...], column)
    cube = (new,) + target.shape
    hit = (jnp.broadcast_to(target[None], cube) == own) & (jnp.broadcast_to(slot[None], cube) == iota(cube, 0))
    source = jnp.sum(jnp.where(hit, iota(cube, 1), 0), axis=2, keepdims=True)
    source = jnp.sum(source, axis=1, keepdims=True)
    source = jnp.broadcast_to(source, (new, block, 1)).reshape(new * block, 1)
    rows = new * block
    source = source * (2 * block) + block + iota((rows, 1), 0) % block
    take = (iota((rows, count * 2 * block), 1) == source).astype(F32).astype(BF16)
    flat = arrived[...].reshape(count * 2 * block, width + tail)
    out_latent[...] = dot(take, flat[:, :width]).astype(BF16).reshape(new, block, width)
    end = dot(take, flat[:, width:])
    fold = fold_matrix(block, rope, tail)
    wide = dot_nt(end.astype(BF16), fold)
    wide = jnp.where(iota(wide.shape, 1) // rope == iota(wide.shape, 0) % block, wide, 0.0)
    out_rope[...] = jnp.sum(wide.reshape(new, block, block * rope), axis=1).astype(BF16)
    scale = jnp.sum(jnp.where(iota(end.shape, 1) == rope, end, 0.0), axis=1, keepdims=True)
    scale = jnp.broadcast_to(scale, (rows, block))
    scale = jnp.where(iota(scale.shape, 1) == iota(scale.shape, 0) % block, scale, 0.0)
    out_scale[...] = jnp.sum(scale.reshape(new, block, block), axis=1).astype(BF16)


def absorb_kernel(nope, rotary, weight, out):
    heads, depth, width = weight.shape
    tokens = nope.shape[0]
    rope = rotary.shape[1] // heads
    tail = out.shape[2] - width
    filler = (iota((tokens, tail - rope), 1) == 0).astype(F32).astype(BF16)
    for h in range(heads):
        out[h, :, :width] = dot(nope[:, h * depth : (h + 1) * depth], weight[h]).astype(BF16)
        out[h, :, width:] = jnp.concatenate([rotary[:, h * rope : (h + 1) * rope], filler], axis=1)


def attend_kernel(shards, first, last, sub, scale, *refs):
    refs = list(refs)
    query = refs.pop(0)
    key_refs = [refs.pop(0) for _ in range(shards)]
    if not first:
        acc_in, stat_in = refs.pop(0), refs.pop(0)
    if last:
        ids, all_refs, value = refs.pop(0), refs[:8], refs[8]
        del refs[:9]
        (out,) = refs
    else:
        acc_out, stat_out = refs
    heads, tokens, wide = query.shape
    group = tokens
    prefix = key_refs[0].shape[0] - group
    width = value.shape[1] if last else acc_out.shape[2]
    step = sub // tokens
    keys = [ref[:prefix, :] for ref in key_refs]
    if last:
        suffix = jnp.concatenate([ref[prefix:, :] for ref in all_refs], axis=0)
        shape = (1, suffix.shape[0])
        where = iota(shape, 1) % group
        for i in range(len(all_refs)):
            where = where + jnp.where(iota(shape, 1) // group == i, ids[2 + i] * group, 0)
        seen = where <= ids[1] * group + iota((sub, 1), 0) % tokens
    for part in range(heads // step):
        q = query[part * step : (part + 1) * step].reshape(sub, wide)
        scores = [dot_nt(q, k) for k in keys]
        held = list(keys)
        if last:
            scores.append(jnp.where(seen, dot_nt(q, suffix), HIDDEN))
            held.append(suffix)
        tops = [jnp.max(s, axis=1, keepdims=True) for s in scores]
        if not first:
            stat = stat_in[part * step : (part + 1) * step].reshape(sub, 128)
            old_top, old_total = stat[:, 0:1], stat[:, 64:65]
            tops.append(old_top)
        top = functools.reduce(jnp.maximum, tops)
        weights = [jnp.exp((s - top) * scale) for s in scores]
        total = sum(jnp.sum(w, axis=1, keepdims=True) for w in weights)
        mixed = sum(dot(w.astype(BF16), k[:, :width]) for w, k in zip(weights, held))
        if not first:
            fade = jnp.exp((old_top - top) * scale)
            total = total + old_total * fade
            mixed = mixed + acc_in[part * step : (part + 1) * step].reshape(sub, width) * fade
        if last:
            mixed = (mixed / total).astype(BF16)
            for h in range(step):
                at = part * step + h
                out[:, at * value.shape[2] : (at + 1) * value.shape[2]] = dot(
                    mixed[h * tokens : (h + 1) * tokens], value[at]
                ).astype(BF16)
        else:
            acc_out[part * step : (part + 1) * step] = mixed.reshape(step, tokens, width)
            stat = jnp.where(iota((sub, 128), 1) < 64, top, total)
            stat_out[part * step : (part + 1) * step] = stat.reshape(step, tokens, 128)


def attend(query, shards, state=None, final=None, width=512, tile=8, sub=256, scale=1.0):
    heads, tokens, wide = query.shape
    first, last = state is None, final is not None

    def by_tile(*dims):
        return pl.BlockSpec((tile,) + dims, lambda i: (i,) + (0,) * len(dims))

    def whole(array):
        return pl.BlockSpec(array.shape, lambda i: (0,) * array.ndim)

    operands, specs = [query, *shards], [by_tile(tokens, wide)] + [whole(s) for s in shards]
    if not first:
        operands += list(state)
        specs += [by_tile(tokens, width), by_tile(tokens, 128)]
    keys = sum(s.shape[0] - tokens for s in shards)
    if last:
        ids, every, value = final
        operands += [ids, *every, value]
        specs += [SMEM] + [whole(s) for s in every] + [by_tile(*value.shape[1:])]
        lanes = value.shape[2]
        out_shape = jax.ShapeDtypeStruct((tokens, heads * lanes), BF16)
        out_specs = pl.BlockSpec((tokens, tile * lanes), lambda i: (0, i))
        keys += tokens * len(every)
    else:
        out_shape = (
            jax.ShapeDtypeStruct((heads, tokens, width), F32),
            jax.ShapeDtypeStruct((heads, tokens, 128), F32),
        )
        out_specs = (by_tile(tokens, width), by_tile(tokens, 128))
    rows = heads * tokens
    return pl.pallas_call(
        functools.partial(attend_kernel, len(shards), first, last, sub, scale),
        grid=(heads // tile,),
        in_specs=specs,
        out_specs=out_specs,
        out_shape=out_shape,
        compiler_params=pltpu.CompilerParams(vmem_limit_bytes=40 * MIB),
        cost_estimate=pl.CostEstimate(
            flops=2 * rows * keys * (wide + width), bytes_accessed=8 * MIB, transcendentals=rows * keys
        ),
    )(*operands)


def body(
    query_nope,
    query_rope,
    suffix_latent,
    suffix_rope,
    absorb_key,
    absorb_value,
    pool_latent,
    pool_rope,
    pool_scale,
    prefix_tokens,
    block_owner,
    block_slot,
    write_owner,
    write_slot,
):
    own = lax.axis_index("pool")
    column = lax.axis_index("ctx")
    count = lax.axis_size("pool")
    ctx = lax.axis_size("ctx")
    heads, nope, latent = absorb_key.shape
    tokens = query_nope.shape[1]
    rope = query_rope.shape[2] // heads
    block = pool_scale.shape[3]
    slots = pool_scale.shape[2]
    new_blocks = write_owner.shape[2]
    wide = latent + 128
    scale = (nope + rope) ** -0.5
    core = column % 2
    turn = jnp.where(core == 0, -2, 2)
    a, c = (column + turn) % ctx, (column + 2 * turn) % ctx
    a_swap = ((column ^ 1) - turn) % ctx
    c_swap = ((column ^ 1) - 2 * turn) % ctx
    order = [column, column ^ 1, a, a_swap, a ^ 1, a_swap ^ 1, c, c_swap]
    ids = jnp.stack([own, column] + order).astype(jnp.int32)

    message, suffix = pl.pallas_call(
        pack_kernel,
        in_specs=[SMEM] + [VMEM] * 9,
        out_specs=(VMEM, VMEM),
        out_shape=(
            jax.ShapeDtypeStruct((count, 2 * block, wide), BF16),
            jax.ShapeDtypeStruct((tokens, wide), BF16),
        ),
        compiler_params=pltpu.CompilerParams(vmem_limit_bytes=32 * MIB),
    )(
        ids,
        pool_latent[0, 0],
        pool_rope[0, 0],
        pool_scale[0, 0],
        suffix_latent[0],
        suffix_rope,
        prefix_tokens[None],
        block_owner,
        block_slot,
        write_owner,
    )
    arrived = lax.all_to_all(message, "pool", split_axis=0, concat_axis=0, tiled=True)

    tile = 4
    query = pl.pallas_call(
        absorb_kernel,
        grid=(heads // tile,),
        in_specs=[
            pl.BlockSpec((tokens, tile * nope), lambda i: (0, i)),
            pl.BlockSpec((tokens, tile * rope), lambda i: (0, i)),
            pl.BlockSpec((tile, nope, latent), lambda i: (i, 0, 0)),
        ],
        out_specs=pl.BlockSpec((tile, tokens, wide), lambda i: (i, 0, 0)),
        out_shape=jax.ShapeDtypeStruct((heads, tokens, wide), BF16),
        compiler_params=pltpu.CompilerParams(vmem_limit_bytes=16 * MIB),
        cost_estimate=pl.CostEstimate(
            flops=2 * heads * tokens * nope * latent, bytes_accessed=8 * MIB, transcendentals=0
        ),
    )(query_nope[0], query_rope[0], absorb_key)

    shard = pl.pallas_call(
        shard_kernel,
        in_specs=[VMEM, VMEM],
        out_specs=VMEM,
        out_shape=jax.ShapeDtypeStruct((slots * block + tokens, wide), BF16),
    )(arrived, suffix)

    ring = [(s, (s + (2 if s % 2 == 0 else -2)) % ctx) for s in range(ctx)]
    swap = [(s, s ^ 1) for s in range(ctx)]
    first = lax.ppermute(shard, "ctx", ring)
    sibling = lax.ppermute(shard, "ctx", swap)
    second = lax.ppermute(sibling, "ctx", ring)
    third = lax.ppermute(first, "ctx", ring)
    first_swap = lax.ppermute(first, "ctx", swap)
    second_swap = lax.ppermute(second, "ctx", swap)
    third_swap = lax.ppermute(third, "ctx", swap)

    run = functools.partial(attend, query, width=latent, scale=scale)
    state = run([shard, sibling])
    state = run([first, first_swap], state)
    state = run([second, second_swap], state)
    every = [shard, sibling, first, first_swap, second, second_swap, third, third_swap]
    attended = run([third, third_swap], state, (ids, every, absorb_value))

    written_latent, written_rope, written_scale = pl.pallas_call(
        land_kernel,
        in_specs=[SMEM] + [VMEM] * 3,
        out_specs=(VMEM, VMEM, VMEM),
        out_shape=(
            jax.ShapeDtypeStruct((new_blocks, block, latent), BF16),
            jax.ShapeDtypeStruct((new_blocks, block * rope), BF16),
            jax.ShapeDtypeStruct((new_blocks, block), BF16),
        ),
    )(ids, arrived, write_owner, write_slot)
    return (attended[None], written_latent[None, None], written_rope[None, None], written_scale[None, None])


def solution(mesh):
    placed = (
        P("pool", "ctx", None),
        P("pool", "ctx", None),
        P("pool", "ctx", None),
        P("pool", "ctx"),
        P(),
        P(),
        P("pool", "ctx", None, None, None),
        P("pool", "ctx", None, None),
        P("pool", "ctx", None, None),
        P(),
        P(),
        P(),
        P(),
        P(),
    )
    return jax.shard_map(
        body,
        mesh=mesh,
        in_specs=placed,
        out_specs=(
            P("pool", "ctx", None),
            P("pool", "ctx", None, None, None),
            P("pool", "ctx", None, None),
            P("pool", "ctx", None, None),
        ),
        check_vma=False,
    )
```

time: 240 us -> 103 us (0.43)
  Pallas kernels: 0 us -> 42.8 us
  matrix products: 39.5 us -> 0 us
  starting transfers between devices: 47.5 us -> 13.4 us
  other arithmetic: 27.7 us -> 0 us
  blocking collectives: 55 us -> 28.2 us
  local copies, waits for them, and re-layouts: 33 us -> 13.2 us
  waiting for transfers between devices: 21.2 us -> 3.51 us
  between operations: 14.7 us -> 0.86 us
    all_gather x4 -> x0, blocking collectives: 55 us -> none  [the longest x1 14.7 us: body(): lax.all_gather(group_rope[None], 'ctx', axis=0, tiled=True)]
    all_to_all x6 -> x0, starting transfers between devices: 47.5 us -> none  [the longest x1 11.9 us: body(): lax.all_to_all(code_scale[pick], 'pool', split_axis=0, concat_axis=0, til...]
    pallas_call x0 -> x8, Pallas kernels: none -> 42.8 us  [the longest x4 34.9 us: attend(): pl.pallas_call(functools.partial(attend_kernel, len(shards), first, last,...]
    dot_general x7 -> x0, matrix products: 39.5 us -> none  [the longest x1 12.6 us: attend(): jnp.einsum('thk,kl->thl', weights_full.astype(jnp.bfloat16), keys, prefer...]
    all_to_all x0 -> x1, blocking collectives: none -> 28.2 us  [body(): lax.all_to_all(message, 'pool', split_axis=0, concat_axis=0, tiled=True)]
    all_to_all x6 -> x0, waiting for transfers between devices: 20.5 us -> none  [the longest x1 8.68 us: body(): lax.all_to_all(padded[1][lanes, index], 'pool', split_axis=0, concat_axis...]
    reduce_sum x7 -> x0, other arithmetic: 20.1 us -> none  [the longest x2 13.1 us: attend(): row_total = row_total * fade + jnp.sum(weights_full, axis=2)]
    gather x12 -> x0, local copies, waits for them, and re-layouts: 17.4 us -> none  [the longest x1 2.71 us: body(): padded[1][lanes, index]]
  transfers between devices with their start and end apart: 7 -> 7, of which waited for: 3 -> 1; matrix products, arithmetic and copies ran while one was open for 22% -> 1% of each run, Pallas kernels for 0% -> 25%
where the time goes in v1:
time: 103 us; the launch traced here: 102 us
  Pallas kernels  42.8 us (42%)
  blocking collectives  28.2 us (27%)
  starting transfers between devices  13.4 us (13%)
  local copies, waits for them, and re-layouts  13.2 us (13%)
  waiting for transfers between devices  3.51 us (3%)
    pallas_call x4, Pallas kernels, attend(): pl.pallas_call(functools.partial(attend_kernel, len(shards), first, last,...  34.9 us
    all_to_all x1, blocking collectives, body(): lax.all_to_all(message, 'pool', split_axis=0, concat_axis=0, tiled=True)  28.2 us
    unnamed x33, local copies, waits for them, and re-layouts  13.1 us
    ppermute x1, starting transfers between devices, body(): sibling = lax.ppermute(shard, 'ctx', swap)  5.01 us
    ppermute x1, waiting for transfers between devices, body(): first = lax.ppermute(shard, 'ctx', ring)  3.5 us
    ppermute x1, starting transfers between devices, body(): third = lax.ppermute(first, 'ctx', ring)  3.12 us
    ppermute x1, starting transfers between devices, body(): first = lax.ppermute(shard, 'ctx', ring)  2.73 us
    pallas_call x1, Pallas kernels, body(): pl.pallas_call(land_kernel, in_specs=[SMEM] + [VMEM] * 3, out_specs=(VMEM...  2.52 us
  transfers between devices with their start and end apart: 7, of which 1 were waited for; matrix products, arithmetic and copies ran while one was open for 1% of the time, Pallas kernels for 25%

profile of v1, /device:TPU:1, one launch (start us, length us, event | category | flops | bytes accessed | tf_op | source)
XLA Modules:
  0.0 101.8 jit_solution(15121994121203605455)
XLA Ops:
  0.7 0.9 copy.19.targets
  1.6 0.0 copy-start.1
  1.6 0.8 copy.18
  2.4 0.1 stack.40.ids.refs_5_
  2.5 0.0 copy-start.4
  2.5 0.9 copy-done.4
  3.4 0.0 copy-start.6
  3.4 0.9 copy-done.6
  4.3 0.0 copy-start.7
  4.3 0.9 copy-done.7
  5.2 0.8 copy-done.9
  6.1 0.8 copy-done.10
  6.8 0.7 copy-done.11
  7.6 0.7 copy-done.14
  8.2 1.6 %shard_map.166 = (bf16[32,16,640]{2,1,0:T(8,128)(2,1)S(1)}, bf16[64,640]{1,0:T(8,128)(2,1)S(1)}) custom-call(s32[10]{0:T(128)S(1)} %stack.40.ids.refs_5_, bf16[32,8,512]{2,1,0:T(8,128)(2,1)S(1)} %bitcast.21, bf16[32,512]{1,0:T(8,128)(2,1)S(1)} %bitcast.25, bf16[32,8]{1,0:T(8,128)(2,1)S(1)} %bitcast.24, bf16[64,512]{1,0:T(8,128)(2,1)S(1)} %bitcast.23, ...), custom_call_target="tpu_custom_call" | custom-call | tf_op jit(solution)/shard_map/pallas_call | solution.py:306
  9.8 0.0 copy-start.8
  9.8 28.2 %all_to_all.5.arrived = bf16[32,16,640]{2,1,0:T(8,128)(2,1)} all-to-all(bf16[32,16,640]{2,1,0:T(8,128)(2,1)S(1)} %get-tuple-element.15), channel_id=1, replica_groups=mesh['pool'=32,'ctx'=8] {'pool'}, dimensions={0} | all-to-all | bytes 1310720 | tf_op jit(solution)/shard_map/all_to_all | solution.py:327
  37.9 0.0 copy-done.8
  37.9 1.9 %shard_map.167.refs_1_.refs_6_ = bf16[320,640]{1,0:T(8,128)(2,1)} custom-call(bf16[32,16,640]{2,1,0:T(8,128)(2,1)} %all_to_all.5.arrived, bf16[64,640]{1,0:T(8,128)(2,1)} %copy-done.8), custom_call_target="tpu_custom_call" | custom-call | tf_op jit(solution)/shard_map/pallas_call | solution.py:346
  39.8 5.0 %collective-permute-start.3 = (bf16[320,640]{1,0:T(8,128)(2,1)}, bf16[320,640]{1,0:T(8,128)(2,1)}, u32[]{:S(2)}, u32[]{:S(2)}) collective-permute-start(bf16[320,640]{1,0:T(8,128)(2,1)} %shard_map.167.refs_1_.refs_6_), channel_id=1, source_target_pairs={{0,1},{1,0},{2,3},{3,2},{4,5},{5,4},{6,7},{7,6},{8,9},{9,8},{10,11... | collective-permute-start | bytes 1228808 | tf_op jit(solution)/shard_map/ppermute | solution.py:356
  44.8 2.7 %collective-permute-start = (bf16[320,640]{1,0:T(8,128)(2,1)}, bf16[320,640]{1,0:T(8,128)(2,1)}, u32[]{:S(2)}, u32[]{:S(2)}) collective-permute-start(bf16[320,640]{1,0:T(8,128)(2,1)} %shard_map.167.refs_1_.refs_6_), channel_id=1, source_target_pairs={{0,2},{1,7},{2,4},{3,1},{4,6},{5,3},{6,0},{7,5},{8,10},{9,15},{10,... | collective-permute-start | bytes 1228808 | tf_op jit(solution)/shard_map/ppermute | solution.py:355
  47.6 0.0 collective-permute-done.3.refs_2_.refs_7_
  47.6 1.7 %collective-permute-start.4 = (bf16[320,640]{1,0:T(8,128)(2,1)}, bf16[320,640]{1,0:T(8,128)(2,1)}, u32[]{:S(2)}, u32[]{:S(2)}) collective-permute-start(bf16[320,640]{1,0:T(8,128)(2,1)} %collective-permute-done.3.refs_2_.refs_7_), channel_id=1, source_target_pairs={{0,2},{1,7},{2,4},{3,1},{4,6},{5,3},{6,0},{7,5},{8,10},{9,15},{10,... | collective-permute-start | bytes 1228808 | tf_op jit(solution)/shard_map/ppermute | solution.py:357
  49.3 3.5 %collective-permute-done.refs_1_.refs_8_ = bf16[320,640]{1,0:T(8,128)(2,1)} collective-permute-done((bf16[320,640]{1,0:T(8,128)(2,1)}, bf16[320,640]{1,0:T(8,128)(2,1)}, u32[]{:S(2)}, u32[]{:S(2)}) %collective-permute-start) | collective-permute-done | bytes 409632 | tf_op jit(solution)/shard_map/ppermute | solution.py:355
  52.8 3.1 %collective-permute-start.1 = (bf16[320,640]{1,0:T(8,128)(2,1)}, bf16[320,640]{1,0:T(8,128)(2,1)}, u32[]{:S(2)}, u32[]{:S(2)}) collective-permute-start(bf16[320,640]{1,0:T(8,128)(2,1)} %collective-permute-done.refs_1_.refs_8_), channel_id=1, source_target_pairs={{0,2},{1,7},{2,4},{3,1},{4,6},{5,3},{6,0},{7,5},{8,10},{9,15},{10,... | collective-permute-start | bytes 1228808 | tf_op jit(solution)/shard_map/ppermute | solution.py:358
  55.9 0.0 collective-permute-start.6
  55.9 1.5 %copy.21.slots = s32[32,8,8]{2,1,0:T(8,128)} copy(s32[32,8,8]{0,2,1:T(8,128)} %param.27) | data formatting | bytes 16384 | tf_op args[13]
  57.4 2.2 %copy-done = bf16[32,128,512]{2,1,0:T(8,128)(2,1)S(1)} copy-done((bf16[32,128,512]{2,1,0:T(8,128)(2,1)S(1)}, bf16[32,128,512]{2,1,0:T(8,128)(2,1)}, u32[]{:S(2)}) %copy-start) | copy-done | bytes 4194328
  59.6 1.0 %copy-done.2 = bf16[1,64,4096]{2,1,0:T(8,128)(2,1)S(1)} copy-done((bf16[1,64,4096]{2,1,0:T(8,128)(2,1)S(1)}, bf16[1,64,4096]{2,1,0:T(8,128)(2,1)}, u32[]{:S(2)}) %copy-start.2) | copy-done | bytes 524312
  60.6 0.9 copy-done.5
  61.6 1.9 %shard_map.165.refs_0_ = bf16[32,64,640]{2,1,0:T(8,128)(2,1)S(1)} custom-call(bf16[64,4096]{1,0:T(8,128)(2,1)S(1)} %bitcast.20, bf16[64,2048]{1,0:T(8,128)(2,1)S(1)} %bitcast.22, bf16[32,128,512]{2,1,0:T(8,128)(2,1)S(1)} %copy-done), custom_call_target="tpu_custom_call" | custom-call | flops 268435456 | bytes 8388608 | tf_op jit(solution)/shard_map/pallas_call | solution.py:330
  63.5 0.0 copy-done.1
  63.5 0.0 copy-done.12
  63.5 2.5 %shard_map.172 = (bf16[8,8,512]{2,1,0:T(8,128)(2,1)}, bf16[8,512]{1,0:T(8,128)(2,1)}, bf16[8,8]{1,0:T(8,128)(2,1)}) custom-call(s32[10]{0:T(128)} %copy-done.12, bf16[32,16,640]{2,1,0:T(8,128)(2,1)} %all_to_all.5.arrived, s32[32,8,8]{2,1,0:T(8,128)} %copy-done.1, s32[32,8,8]{2,1,0:T(8,128)} %copy.21.slots), custom_call_target="tpu_custom_call" | custom-call | tf_op jit(solution)/shard_map/pallas_call | solution.py:370
  66.0 0.0 collective-permute-done.4.refs_1_.refs_10_
  66.0 0.5 collective-permute-start.5
  66.6 0.0 copy-done.3
  66.6 6.0 %shard_map.168 = (f32[32,64,512]{2,1,0:T(8,128)S(1)}, f32[32,64,128]{2,1,0:T(8,128)S(1)}) custom-call(bf16[32,64,640]{2,1,0:T(8,128)(2,1)S(1)} %shard_map.165.refs_0_, bf16[320,640]{1,0:T(8,128)(2,1)S(1)} %copy-done.3, bf16[320,640]{1,0:T(8,128)(2,1)} %collective-permute-done.3.refs_2_.refs_7_), custom_call_target="tpu_custom_call" | custom-call | flops 2415919104 | bytes 8388608 | tf_op jit(solution)/shard_map/pallas_call | solution.py:257
  72.6 0.0 collective-permute-done.1.refs_1_.refs_12_
  72.6 0.3 collective-permute-start.2
  72.9 0.0 collective-permute-done.6.refs_2_.refs_9_
  72.9 7.5 %shard_map.169 = (f32[32,64,512]{2,1,0:T(8,128)S(1)}, f32[32,64,128]{2,1,0:T(8,128)S(1)}) custom-call(bf16[32,64,640]{2,1,0:T(8,128)(2,1)S(1)} %shard_map.165.refs_0_, bf16[320,640]{1,0:T(8,128)(2,1)} %collective-permute-done.refs_1_.refs_8_, bf16[320,640]{1,0:T(8,128)(2,1)} %collective-permute-done.6.refs_2_.refs_9_, ...), custom_call_target="tpu_custom_call" | custom-call | flops 2415919104 | bytes 8388608 | tf_op jit(solution)/shard_map/pallas_call | solution.py:257
  80.4 0.0 collective-permute-done.5.refs_2_.refs_11_
  80.4 0.0 copy-start.13
  80.4 7.5 %shard_map.170 = (f32[32,64,512]{2,1,0:T(8,128)S(1)}, f32[32,64,128]{2,1,0:T(8,128)S(1)}) custom-call(bf16[32,64,640]{2,1,0:T(8,128)(2,1)S(1)} %shard_map.165.refs_0_, bf16[320,640]{1,0:T(8,128)(2,1)} %collective-permute-done.4.refs_1_.refs_10_, bf16[320,640]{1,0:T(8,128)(2,1)S(1)} %collective-permute-done.5.refs_2_.refs_11_, ...), custom_call_target="tpu_custom_call" | custom-call | flops 2415919104 | bytes 8388608 | tf_op jit(solution)/shard_map/pallas_call | solution.py:257
  88.0 0.0 collective-permute-done.2.refs_2_.refs_13_
  88.0 0.0 copy-done.13
  88.0 13.8 %shard_map.171 = bf16[64,4096]{1,0:T(8,128)(2,1)} custom-call(bf16[32,64,640]{2,1,0:T(8,128)(2,1)S(1)} %shard_map.165.refs_0_, bf16[320,640]{1,0:T(8,128)(2,1)} %collective-permute-done.1.refs_1_.refs_12_, bf16[320,640]{1,0:T(8,128)(2,1)S(1)} %collective-permute-done.2.refs_2_.refs_13_, f32[32,64,512]{2,1,0:T(8,128)S(1)} %get-tuple-element.21.refs_3_, ...), custom_call_target="tpu_custom_call" | custom-call | flops 4831838208 | bytes 8388608 | tf_op jit(solution)/shard_map/pallas_call | solution.py:257
  (9 shorter events, 0.0 us)
Async XLA Ops:
  1.6 61.9 %copy-start.1 = (s32[32,8,8]{2,1,0:T(8,128)}, s32[32,8,8]{2,1,0:T(8,128)S(1)}, u32[]{:S(2)}) copy-start(s32[32,8,8]{2,1,0:T(8,128)S(1)} %copy.19.targets) | copy-start | bytes 24580
  2.5 61.0 %copy-start.12 = (s32[10]{0:T(128)}, s32[10]{0:T(128)S(1)}, u32[]{:S(2)}) copy-start(s32[10]{0:T(128)S(1)} %stack.40.ids.refs_5_) | copy-start | bytes 124
  2.5 1.0 copy-start.4
  3.4 0.9 copy-start.6
  4.3 0.9 copy-start.7
  5.2 0.8 copy-start.9
  6.1 0.8 copy-start.10
  6.8 0.7 copy-start.11
  7.6 0.7 copy-start.14
  9.8 28.2 %copy-start.8 = (bf16[64,640]{1,0:T(8,128)(2,1)}, bf16[64,640]{1,0:T(8,128)(2,1)S(1)}, u32[]{:S(2)}) copy-start(bf16[64,640]{1,0:T(8,128)(2,1)S(1)} %get-tuple-element.16.suffix) | copy-start | bytes 245764
  39.8 7.7 %collective-permute-start.3 = (bf16[320,640]{1,0:T(8,128)(2,1)}, bf16[320,640]{1,0:T(8,128)(2,1)}, u32[]{:S(2)}, u32[]{:S(2)}) collective-permute-start(bf16[320,640]{1,0:T(8,128)(2,1)} %shard_map.167.refs_1_.refs_6_), channel_id=1, source_target_pairs={{0,1},{1,0},{2,3},{3,2},{4,5},{5,4},{6,7},{7,6},{8,9},{9,8},{10,11... | collective-permute-start | bytes 1228808 | tf_op jit(solution)/shard_map/ppermute | solution.py:356
  44.8 7.9 %collective-permute-start = (bf16[320,640]{1,0:T(8,128)(2,1)}, bf16[320,640]{1,0:T(8,128)(2,1)}, u32[]{:S(2)}, u32[]{:S(2)}) collective-permute-start(bf16[320,640]{1,0:T(8,128)(2,1)} %shard_map.167.refs_1_.refs_6_), channel_id=1, source_target_pairs={{0,2},{1,7},{2,4},{3,1},{4,6},{5,3},{6,0},{7,5},{8,10},{9,15},{10,... | collective-permute-start | bytes 1228808 | tf_op jit(solution)/shard_map/ppermute | solution.py:355
  47.6 18.5 %collective-permute-start.4 = (bf16[320,640]{1,0:T(8,128)(2,1)}, bf16[320,640]{1,0:T(8,128)(2,1)}, u32[]{:S(2)}, u32[]{:S(2)}) collective-permute-start(bf16[320,640]{1,0:T(8,128)(2,1)} %collective-permute-done.3.refs_2_.refs_7_), channel_id=1, source_target_pairs={{0,2},{1,7},{2,4},{3,1},{4,6},{5,3},{6,0},{7,5},{8,10},{9,15},{10,... | collective-permute-start | bytes 1228808 | tf_op jit(solution)/shard_map/ppermute | solution.py:357
  52.8 19.8 %collective-permute-start.1 = (bf16[320,640]{1,0:T(8,128)(2,1)}, bf16[320,640]{1,0:T(8,128)(2,1)}, u32[]{:S(2)}, u32[]{:S(2)}) collective-permute-start(bf16[320,640]{1,0:T(8,128)(2,1)} %collective-permute-done.refs_1_.refs_8_), channel_id=1, source_target_pairs={{0,2},{1,7},{2,4},{3,1},{4,6},{5,3},{6,0},{7,5},{8,10},{9,15},{10,... | collective-permute-start | bytes 1228808 | tf_op jit(solution)/shard_map/ppermute | solution.py:358
  55.9 17.0 %collective-permute-start.6 = (bf16[320,640]{1,0:T(8,128)(2,1)}, bf16[320,640]{1,0:T(8,128)(2,1)}, u32[]{:S(2)}, u32[]{:S(2)}) collective-permute-start(bf16[320,640]{1,0:T(8,128)(2,1)} %collective-permute-done.refs_1_.refs_8_), channel_id=1, source_target_pairs={{0,1},{1,0},{2,3},{3,2},{4,5},{5,4},{6,7},{7,6},{8,9},{9,8},{10,11... | collective-permute-start | bytes 1228808 | tf_op jit(solution)/shard_map/ppermute | solution.py:359
  57.4 2.2 %copy-start = (bf16[32,128,512]{2,1,0:T(8,128)(2,1)S(1)}, bf16[32,128,512]{2,1,0:T(8,128)(2,1)}, u32[]{:S(2)}) copy-start(bf16[32,128,512]{2,1,0:T(8,128)(2,1)} %weight.1) | copy-start | bytes 12582916
  59.6 1.0 %copy-start.2 = (bf16[1,64,4096]{2,1,0:T(8,128)(2,1)S(1)}, bf16[1,64,4096]{2,1,0:T(8,128)(2,1)}, u32[]{:S(2)}) copy-start(bf16[1,64,4096]{2,1,0:T(8,128)(2,1)} %param.14) | copy-start | bytes 1572868
  60.6 0.9 copy-start.5
  61.6 5.0 %copy-start.3 = (bf16[320,640]{1,0:T(8,128)(2,1)S(1)}, bf16[320,640]{1,0:T(8,128)(2,1)}, u32[]{:S(2)}) copy-start(bf16[320,640]{1,0:T(8,128)(2,1)} %shard_map.167.refs_1_.refs_6_) | copy-start | bytes 1228804
  66.0 14.4 %collective-permute-start.5 = (bf16[320,640]{1,0:T(8,128)(2,1)}, bf16[320,640]{1,0:T(8,128)(2,1)S(1)}, u32[]{:S(2)}, u32[]{:S(2)}) collective-permute-start(bf16[320,640]{1,0:T(8,128)(2,1)} %collective-permute-done.4.refs_1_.refs_10_), channel_id=1, source_target_pairs={{0,1},{1,0},{2,3},{3,2},{4,5},{5,4},{6,7},{7,6},{8,9},{9,8},{10,11... | collective-permute-start | bytes 1228808 | tf_op jit(solution)/shard_map/ppermute | solution.py:360
  72.6 15.4 %collective-permute-start.2 = (bf16[320,640]{1,0:T(8,128)(2,1)}, bf16[320,640]{1,0:T(8,128)(2,1)S(1)}, u32[]{:S(2)}, u32[]{:S(2)}) collective-permute-start(bf16[320,640]{1,0:T(8,128)(2,1)} %collective-permute-done.1.refs_1_.refs_12_), channel_id=1, source_target_pairs={{0,1},{1,0},{2,3},{3,2},{4,5},{5,4},{6,7},{7,6},{8,9},{9,8},{10,11... | collective-permute-start | bytes 1228808 | tf_op jit(solution)/shard_map/ppermute | solution.py:361
  80.4 7.5 %copy-start.13 = (s32[10]{0:T(128)S(1)}, s32[10]{0:T(128)}, u32[]{:S(2)}) copy-start(s32[10]{0:T(128)} %copy-done.12) | copy-start | bytes 124

commit v2 on v1

v2 whole, which is shorter than its diff:
```python
import functools

import jax
import jax.numpy as jnp
from jax import lax
from jax.experimental import pallas as pl
from jax.experimental.pallas import tpu as pltpu
from jax.sharding import PartitionSpec as P

HIDDEN = -1e30
QUANT_TOP = 4.0
QUANT_EPS = 1e-06
MIB = 1 << 20

F32 = jnp.float32
BF16 = jnp.bfloat16
VMEM = pl.BlockSpec(memory_space=pltpu.VMEM)
SMEM = pl.BlockSpec(memory_space=pltpu.SMEM)
ANY = pl.BlockSpec(memory_space=pl.ANY)


def iota(shape, axis):
    return lax.broadcasted_iota(jnp.int32, shape, axis)


def dot(a, b):
    return jnp.dot(a, b, preferred_element_type=F32)


def dot_nt(a, b):
    return lax.dot_general(a, b, (((1,), (1,)), ((), ())), preferred_element_type=F32)


def fold_matrix(block, rope, lanes):
    shape = (block * rope, lanes)
    return (iota(shape, 0) % rope == iota(shape, 1)).astype(F32).astype(BF16)


def pick_column(table, column):
    return jnp.sum(jnp.where(iota(table.shape, 1) == column, table, 0), axis=1)


def pack_kernel(ids, latent, ropes, scales, prefix, owners, slots, message):
    own, column = ids[0], ids[1]
    count, block, width = latent.shape
    rope = ropes.shape[1] // block
    ctx = owners.shape[1]
    tail = message.shape[2] - width
    rows = block * count
    fold = fold_matrix(block, rope, tail)

    cube = (count, block, count)
    factor = jnp.broadcast_to(scales[...].astype(F32)[None], cube)
    factor = jnp.sum(jnp.where(iota(cube, 0) == iota(cube, 2), factor, 0.0), axis=2, keepdims=True)
    keys = (latent[...].astype(F32) * factor).reshape(rows, width).astype(BF16)
    wide = (count, block, block * rope)
    spread = jnp.broadcast_to(ropes[...].astype(F32)[:, None, :], wide) * factor
    spread = jnp.where(iota(wide, 2) // rope == iota(wide, 1), spread, 0.0)
    key_tail = dot(spread.reshape(rows, block * rope).astype(BF16), fold).astype(BF16)

    def by_row(table):
        table = pick_column(table, column)[:, None, :]
        return jnp.broadcast_to(table, (count, block, table.shape[2])).reshape(rows, table.shape[2])

    mine = by_row(owners[...]) == own
    slot = jnp.sum(jnp.where(mine, by_row(slots[...]), 0), axis=1, keepdims=True)
    place = jnp.sum(jnp.where(mine, iota(mine.shape, 1), 0), axis=1, keepdims=True)
    unit = iota((rows, 1), 0) % block
    limit_shape = (rows, count)
    limit = jnp.where(
        iota(limit_shape, 1) == iota(limit_shape, 0) // block,
        jnp.broadcast_to(prefix[...], limit_shape),
        0,
    )
    limit = jnp.sum(limit, axis=1, keepdims=True)
    bias = jnp.where((place * ctx + column) * block >= limit, HIDDEN, 0.0)
    take = (iota((rows, rows), 1) == slot * block + unit).astype(F32).astype(BF16)

    message[:, :, :width] = dot(take, keys).astype(BF16).reshape(count, block, width)
    end = dot(take, key_tail)
    end = end + jnp.where(iota(end.shape, 1) == rope, bias, 0.0)
    message[:, :, width:] = end.astype(BF16).reshape(count, block, tail)


def code_kernel(ids, after, sfx_latent, sfx_rope, targets, suffix, message):
    own, column = ids[0], ids[1]
    tokens, width = sfx_latent.shape
    count, block, lanes = message.shape
    rope = sfx_rope.shape[1] // tokens
    tail = lanes - width
    rows = count * block
    fold = fold_matrix(block, rope, tail)
    own_latent = sfx_latent[...].astype(F32)
    pieces = []
    for g in range(tokens // block):
        piece = sfx_rope[:, g * block * rope : (g + 1) * block * rope].astype(F32)
        piece = jnp.broadcast_to(piece, (block, block * rope))
        pieces.append(jnp.where(iota(piece.shape, 1) // rope == iota(piece.shape, 0), piece, 0.0))
    own_tail = dot(jnp.concatenate(pieces, axis=0).astype(BF16), fold)
    suffix[:, :width] = sfx_latent[...]
    suffix[:, width:] = own_tail.astype(BF16)
    magnitude = jnp.maximum(
        jnp.max(jnp.abs(own_latent), axis=1, keepdims=True),
        jnp.max(jnp.abs(own_tail), axis=1, keepdims=True),
    )
    token_scale = ((magnitude + QUANT_EPS) / QUANT_TOP).astype(BF16).astype(F32)
    code = (own_latent / token_scale).astype(BF16)
    code_tail = jnp.where(iota(own_tail.shape, 1) == rope, token_scale, own_tail / token_scale)
    code_tail = code_tail.astype(BF16)

    table = targets[...]
    mark = jnp.sum(jnp.where(iota(table.shape, 0) == column, table, 0), axis=0)
    mark = jnp.sum(jnp.where(iota(mark.shape, 1) == own, mark, 0), axis=1, keepdims=True)
    new = mark.shape[0]
    mark = jnp.broadcast_to(mark, (new, tokens))
    mark = jnp.sum(jnp.where(iota(mark.shape, 0) == iota(mark.shape, 1) // block, mark, 0), axis=0, keepdims=True)
    mark = mark * block + iota((1, tokens), 1) % block
    take = (iota((rows, tokens), 0) == mark).astype(F32).astype(BF16)
    message[:, :, :width] = dot(take, code).astype(BF16).reshape(count, block, width)
    message[:, :, width:] = dot(take, code_tail).astype(BF16).reshape(count, block, tail)


def shard_kernel(arrived, suffix, after, shard):
    rows = arrived.shape[0]
    shard[:rows, :] = arrived[...]
    shard[rows:, :] = suffix[...]


def land_kernel(ids, arrived, targets, slots, out_latent, out_rope, out_scale):
    own, column = ids[0], ids[1]
    new, block, width = out_latent.shape
    count = arrived.shape[0]
    rope = out_rope.shape[1] // block
    tail = arrived.shape[2] - width

    def pick(table):
        return jnp.sum(jnp.where(iota(table.shape, 0) == column, table, 0), axis=0)

    target, slot = pick(targets[...]), pick(slots[...])
    cube = (new,) + target.shape
    hit = (jnp.broadcast_to(target[None], cube) == own) & (jnp.broadcast_to(slot[None], cube) == iota(cube, 0))
    source = jnp.sum(jnp.where(hit, iota(cube, 2), 0), axis=2, keepdims=True)
    source = jnp.sum(source, axis=1, keepdims=True)
    rows = new * block
    source = jnp.broadcast_to(source, (new, block, 1)).reshape(rows, 1)
    source = source * block + iota((rows, 1), 0) % block
    take = (iota((rows, count * block), 1) == source).astype(F32).astype(BF16)
    flat = arrived[...].astype(F32).reshape(count * block, width + tail).astype(BF16)
    out_latent[...] = dot(take, flat[:, :width]).astype(BF16).reshape(new, block, width)
    end = dot(take, flat[:, width:])
    fold = fold_matrix(block, rope, tail)
    wide = dot_nt(end.astype(BF16), fold)
    wide = jnp.where(iota(wide.shape, 1) // rope == iota(wide.shape, 0) % block, wide, 0.0)
    out_rope[...] = jnp.sum(wide.reshape(new, block, block * rope), axis=1).astype(BF16)
    scale = jnp.sum(jnp.where(iota(end.shape, 1) == rope, end, 0.0), axis=1, keepdims=True)
    scale = jnp.broadcast_to(scale, (rows, block))
    scale = jnp.where(iota(scale.shape, 1) == iota(scale.shape, 0) % block, scale, 0.0)
    out_scale[...] = jnp.sum(scale.reshape(new, block, block), axis=1).astype(BF16)


def absorb_kernel(nope, rotary, weight, after, out):
    heads, depth, width = weight.shape
    tokens = nope.shape[0]
    rope = rotary.shape[1] // heads
    tail = out.shape[1] - width
    filler = (iota((tokens, tail - rope), 1) == 0).astype(F32).astype(BF16)
    for h in range(heads):
        rows = slice(h * tokens, (h + 1) * tokens)
        out[rows, :width] = dot(nope[:, h * depth : (h + 1) * depth], weight[h]).astype(BF16)
        out[rows, width:] = jnp.concatenate([rotary[:, h * rope : (h + 1) * rope], filler], axis=1)


LANES = 128


def attend_kernel(shards, first, last, sub, tokens, scale, *refs):
    refs = list(refs)
    query = refs.pop(0)
    key_refs = [refs.pop(0) for _ in range(shards)]
    if not first:
        acc_in, top_in, total_in = refs.pop(0), refs.pop(0), refs.pop(0)
    if last:
        ids, all_refs, value = refs.pop(0), refs[:8], refs[8]
        del refs[:9]
        (out,) = refs
    else:
        acc_out, top_out, total_out = refs
    prefix = key_refs[0].shape[0] - tokens
    width = value.shape[1] if last else acc_out.shape[1]
    keys = [ref[:prefix, :] for ref in key_refs]
    if last:
        suffix = jnp.concatenate([ref[prefix:, :] for ref in all_refs], axis=0)
        shape = (1, suffix.shape[0])
        place = iota(shape, 1) % tokens
        for i in range(len(all_refs)):
            place = place + jnp.where(iota(shape, 1) // tokens == i, ids[2 + i] * tokens, 0)
        seen = place <= ids[1] * tokens + iota((sub, 1), 0) % tokens
    for part in range(query.shape[0] // sub):
        rows = slice(part * sub, (part + 1) * sub)
        q = query[rows, :]
        scores = [dot_nt(q, k) for k in keys]
        held = list(keys)
        if last:
            scores.append(jnp.where(seen, dot_nt(q, suffix), HIDDEN))
            held.append(suffix)
        top = functools.reduce(jnp.maximum, [jnp.max(s, axis=1, keepdims=True) for s in scores])
        weights = [jnp.exp((s - top) * scale) for s in scores]
        total = sum(jnp.sum(w, axis=1, keepdims=True) for w in weights)
        mixed = sum(dot(w.astype(BF16), k[:, :width]) for w, k in zip(weights, held))
        top = jnp.broadcast_to(top, (sub, LANES))
        total = jnp.broadcast_to(total, (sub, LANES))
        if first:
            acc_out[rows, :] = mixed
            top_out[rows, :] = top
            total_out[rows, :] = total
            continue
        joint = jnp.maximum(top, top_in[rows, :])
        gain = jnp.exp((top - joint) * scale)
        fade = jnp.exp((top_in[rows, :] - joint) * scale)
        total = total * gain + total_in[rows, :] * fade
        if last:
            inverse = 1.0 / total
            gain, fade = gain * inverse, fade * inverse
        chunks = []
        for c in range(width // LANES):
            at = slice(c * LANES, (c + 1) * LANES)
            chunk = mixed[:, at] * gain + acc_in[rows, at] * fade
            if last:
                chunks.append(chunk.astype(BF16))
            else:
                acc_out[rows, at] = chunk
        if last:
            mixed = jnp.concatenate(chunks, axis=1)
            lanes = value.shape[2]
            for h in range(sub // tokens):
                head = part * (sub // tokens) + h
                out[:, head * lanes : (head + 1) * lanes] = dot(
                    mixed[h * tokens : (h + 1) * tokens], value[head]
                ).astype(BF16)
        else:
            top_out[rows, :] = joint
            total_out[rows, :] = total


def attend(query, shards, tokens, width, scale, state=None, final=None, sub=1024):
    rows, wide = query.shape
    first, last = state is None, final is not None
    operands, specs = [query, *shards], [VMEM] * (1 + len(shards))
    if not first:
        operands += list(state)
        specs += [VMEM] * 3
    keys = sum(s.shape[0] - tokens for s in shards)
    if last:
        ids, every, value = final
        operands += [ids, *every, value]
        specs += [SMEM] + [VMEM] * (len(every) + 1)
        out_shape = jax.ShapeDtypeStruct((tokens, rows // tokens * value.shape[2]), BF16)
        out_specs = VMEM
        keys += tokens * len(every)
    else:
        out_shape = tuple(jax.ShapeDtypeStruct((rows, n), F32) for n in (width, LANES, LANES))
        out_specs = (VMEM, VMEM, VMEM)
    return pl.pallas_call(
        functools.partial(attend_kernel, len(shards), first, last, sub, tokens, scale),
        in_specs=specs,
        out_specs=out_specs,
        out_shape=out_shape,
        compiler_params=pltpu.CompilerParams(vmem_limit_bytes=24 * MIB),
        cost_estimate=pl.CostEstimate(
            flops=2 * rows * keys * (wide + width), bytes_accessed=MIB, transcendentals=rows * keys
        ),
    )(*operands)


def body(
    query_nope,
    query_rope,
    suffix_latent,
    suffix_rope,
    absorb_key,
    absorb_value,
    pool_latent,
    pool_rope,
    pool_scale,
    prefix_tokens,
    block_owner,
    block_slot,
    write_owner,
    write_slot,
):
    own = lax.axis_index("pool")
    column = lax.axis_index("ctx")
    count = lax.axis_size("pool")
    ctx = lax.axis_size("ctx")
    heads, nope, latent = absorb_key.shape
    tokens = query_nope.shape[1]
    rope = query_rope.shape[2] // heads
    block = pool_scale.shape[3]
    slots = pool_scale.shape[2]
    new_blocks = write_owner.shape[2]
    wide = latent + 128
    scale = (nope + rope) ** -0.5
    core = column % 2
    turn = jnp.where(core == 0, -2, 2)
    a, c = (column + turn) % ctx, (column + 2 * turn) % ctx
    a_swap = ((column ^ 1) - turn) % ctx
    c_swap = ((column ^ 1) - 2 * turn) % ctx
    order = [column, column ^ 1, a, a_swap, a ^ 1, a_swap ^ 1, c, c_swap]
    ids = jnp.stack([own, column] + order).astype(jnp.int32)

    rows = slots * block
    message = pl.pallas_call(
        pack_kernel,
        in_specs=[SMEM] + [VMEM] * 6,
        out_specs=VMEM,
        out_shape=jax.ShapeDtypeStruct((count, block, wide), BF16),
        compiler_params=pltpu.CompilerParams(vmem_limit_bytes=60 * MIB),
    )(ids, pool_latent[0, 0], pool_rope[0, 0], pool_scale[0, 0].T, prefix_tokens[None], block_owner, block_slot)
    arrived = lax.all_to_all(message, "pool", split_axis=0, concat_axis=0, tiled=True)

    targets, target_slots = jnp.transpose(write_owner, (1, 2, 0)), jnp.transpose(write_slot, (1, 2, 0))
    suffix, codes = pl.pallas_call(
        code_kernel,
        in_specs=[SMEM, ANY] + [VMEM] * 3,
        out_specs=(VMEM, VMEM),
        out_shape=(
            jax.ShapeDtypeStruct((tokens, wide), BF16),
            jax.ShapeDtypeStruct((count, block, wide), BF16),
        ),
        compiler_params=pltpu.CompilerParams(vmem_limit_bytes=4 * MIB),
        cost_estimate=pl.CostEstimate(flops=10**8, bytes_accessed=MIB, transcendentals=0),
    )(ids, message, suffix_latent[0], suffix_rope, targets)
    landed = lax.all_to_all(codes, "pool", split_axis=0, concat_axis=0, tiled=True)

    tile = 4
    query = pl.pallas_call(
        absorb_kernel,
        grid=(heads // tile,),
        in_specs=[
            pl.BlockSpec((tokens, tile * nope), lambda i: (0, i)),
            pl.BlockSpec((tokens, tile * rope), lambda i: (0, i)),
            pl.BlockSpec((tile, nope, latent), lambda i: (i, 0, 0)),
            ANY,
        ],
        out_specs=pl.BlockSpec((tile * tokens, wide), lambda i: (i, 0)),
        out_shape=jax.ShapeDtypeStruct((heads * tokens, wide), BF16),
        compiler_params=pltpu.CompilerParams(vmem_limit_bytes=8 * MIB),
        cost_estimate=pl.CostEstimate(
            flops=2 * heads * tokens * nope * latent, bytes_accessed=8 * MIB, transcendentals=0
        ),
    )(query_nope[0], query_rope[0], absorb_key, codes)

    shard = pl.pallas_call(
        shard_kernel,
        in_specs=[VMEM, VMEM, ANY],
        out_specs=VMEM,
        out_shape=jax.ShapeDtypeStruct((rows + tokens, wide), BF16),
        compiler_params=pltpu.CompilerParams(vmem_limit_bytes=4 * MIB),
    )(arrived.reshape(rows, wide), suffix, query)

    ring = [(s, (s + (2 if s % 2 == 0 else -2)) % ctx) for s in range(ctx)]
    swap = [(s, s ^ 1) for s in range(ctx)]
    first = lax.ppermute(shard, "ctx", ring)
    sibling = lax.ppermute(shard, "ctx", swap)
    second = lax.ppermute(sibling, "ctx", ring)
    third = lax.ppermute(first, "ctx", ring)
    first_swap = lax.ppermute(first, "ctx", swap)
    second_swap = lax.ppermute(second, "ctx", swap)
    third_swap = lax.ppermute(third, "ctx", swap)

    run = functools.partial(attend, query, tokens=tokens, width=latent, scale=scale)
    state = run([shard, sibling])
    state = run([first, first_swap], state=state)
    state = run([second, second_swap], state=state)
    every = [shard, sibling, first, first_swap, second, second_swap, third, third_swap]
    attended = run([third, third_swap], state=state, final=(ids, every, absorb_value))

    written_latent, written_rope, written_scale = pl.pallas_call(
        land_kernel,
        in_specs=[SMEM] + [VMEM] * 3,
        out_specs=(VMEM, VMEM, VMEM),
        out_shape=(
            jax.ShapeDtypeStruct((new_blocks, block, latent), BF16),
            jax.ShapeDtypeStruct((new_blocks, block * rope), BF16),
            jax.ShapeDtypeStruct((new_blocks, block), BF16),
        ),
        compiler_params=pltpu.CompilerParams(vmem_limit_bytes=8 * MIB),
    )(ids, landed, targets, target_slots)
    return (attended[None], written_latent[None, None], written_rope[None, None], written_scale[None, None])


def solution(mesh):
    placed = (
        P("pool", "ctx", None),
        P("pool", "ctx", None),
        P("pool", "ctx", None),
        P("pool", "ctx"),
        P(),
        P(),
        P("pool", "ctx", None, None, None),
        P("pool", "ctx", None, None),
        P("pool", "ctx", None, None),
        P(),
        P(),
        P(),
        P(),
        P(),
    )
    return jax.shard_map(
        body,
        mesh=mesh,
        in_specs=placed,
        out_specs=(
            P("pool", "ctx", None),
            P("pool", "ctx", None, None, None),
            P("pool", "ctx", None, None),
            P("pool", "ctx", None, None),
        ),
        check_vma=False,
    )
```

time: 103 us -> 78 us (0.76)
  blocking collectives: 28.2 us -> 0 us
  starting transfers between devices: 13.4 us -> 32 us
  Pallas kernels: 42.8 us -> 31.3 us
  local copies, waits for them, and re-layouts: 13.2 us -> 8.7 us
    all_to_all x1 -> x0, blocking collectives: 28.2 us -> none  [body(): lax.all_to_all(message, 'pool', split_axis=0, concat_axis=0, tiled=True)]
    all_to_all x0 -> x2, starting transfers between devices: none -> 19.6 us  [the longest x1 11.9 us: body(): lax.all_to_all(message, 'pool', split_axis=0, concat_axis=0, tiled=True)]
    pallas_call x4, Pallas kernels: 34.9 us -> 23.6 us  [attend(): pl.pallas_call(functools.partial(attend_kernel, len(shards), first, last,...]
    unnamed x33 -> x24, local copies, waits for them, and re-layouts: 13.1 us -> 8.1 us
    ppermute x1, starting transfers between devices: 5.01 us -> 2.8 us  [body(): sibling = lax.ppermute(shard, 'ctx', swap)]
    ppermute x1, starting transfers between devices: 0.51 us -> 2.63 us  [body(): second_swap = lax.ppermute(second, 'ctx', swap)]
    ppermute x1, starting transfers between devices: 1.71 us -> 0.46 us  [body(): second = lax.ppermute(sibling, 'ctx', ring)]
    pallas_call x2 -> x3, Pallas kernels: 3.42 us -> 4.2 us  [the longest x1 2.42 us: body(): pl.pallas_call(pack_kernel, in_specs=[SMEM] + [VMEM] * 6, out_specs=VMEM,...]
  transfers between devices with their start and end apart: 7 -> 9, of which waited for: 1 -> 1; matrix products, arithmetic and copies ran while one was open for 1% -> 0% of each run, Pallas kernels for 25% -> 24%
where the time goes in v2:
time: 78 us; the launch traced here: 77.3 us
  starting transfers between devices  32 us (41%)
  Pallas kernels  31.3 us (40%)
  local copies, waits for them, and re-layouts  8.7 us (11%)
  waiting for transfers between devices  4.45 us (6%)
  between operations  0.86 us (1%)
    pallas_call x4, Pallas kernels, attend(): pl.pallas_call(functools.partial(attend_kernel, len(shards), first, last,...  23.6 us
    all_to_all x1, starting transfers between devices, body(): lax.all_to_all(message, 'pool', split_axis=0, concat_axis=0, tiled=True)  11.9 us
    unnamed x24, local copies, waits for them, and re-layouts  8.1 us
    all_to_all x1, starting transfers between devices, body(): lax.all_to_all(codes, 'pool', split_axis=0, concat_axis=0, tiled=True)  7.76 us
    ppermute x1, waiting for transfers between devices, body(): first = lax.ppermute(shard, 'ctx', ring)  4.43 us
    ppermute x1, starting transfers between devices, body(): third = lax.ppermute(first, 'ctx', ring)  3.41 us
    ppermute x1, starting transfers between devices, body(): first = lax.ppermute(shard, 'ctx', ring)  2.81 us
    ppermute x1, starting transfers between devices, body(): sibling = lax.ppermute(shard, 'ctx', swap)  2.8 us
  transfers between devices with their start and end apart: 9, of which 1 were waited for; matrix products, arithmetic and copies ran while one was open for 0% of the time, Pallas kernels for 24%

profile of v2, /device:TPU:1, one launch (start us, length us, event | category | flops | bytes accessed | tf_op | source)
XLA Modules:
  0.0 77.3 jit_solution(127031563471136861)
XLA Ops:
  0.7 0.6 stack.40.ids.refs_6_
  1.3 2.4 %shard_map.165.after = bf16[32,8,640]{2,1,0:T(8,128)(2,1)} custom-call(s32[10]{0:T(128)} %stack.40.ids.refs_6_, bf16[32,8,512]{2,1,0:T(8,128)(2,1)} %bitcast.32, bf16[32,512]{1,0:T(8,128)(2,1)} %bitcast.33, bf16[8,32]{1,0:T(8,128)(2,1)} %bitcast.34, s32[1,32]{1,0:T(1,128)} %bitcast.35, s32[32,8,32]{2,1,0:T(8,128)} %owners.1, s32[32,8,32]{2,1,0:T(8,128)} %slots.1), custom_call_target="tpu_custom_call" | custom-call | tf_op jit(solution)/shard_map/pallas_call | solution.py:312
  3.7 11.9 %all-to-all-start = ((bf16[32,8,640]{2,1,0:T(8,128)(2,1)}), bf16[32,8,640]{2,1,0:T(8,128)(2,1)S(1)}, u32[]{:S(2)}, u32[]{:S(2)}) async-start(bf16[32,8,640]{2,1,0:T(8,128)(2,1)} %shard_map.165.after), calls=%async_computation | async-start | bytes 655360 | tf_op jit(solution)/shard_map/all_to_all | solution.py:319
  15.6 0.0 copy-start.1
  15.6 1.0 %copy-done.1 = bf16[32,8,640]{2,1,0:T(8,128)(2,1)S(1)} copy-done((bf16[32,8,640]{2,1,0:T(8,128)(2,1)S(1)}, bf16[32,8,640]{2,1,0:T(8,128)(2,1)}, u32[]{:S(2)}) %copy-start.1) | copy-done | bytes 327704
  16.6 0.0 copy-start.4
  16.6 0.8 copy-done.4
  17.4 0.0 copy-start.6
  17.4 0.8 %copy-done.6 = bf16[1,64,512]{2,1,0:T(8,128)(2,1)S(1)} copy-done((bf16[1,64,512]{2,1,0:T(8,128)(2,1)S(1)}, bf16[1,64,512]{2,1,0:T(8,128)(2,1)}, u32[]{:S(2)}) %copy-start.6) | copy-done | bytes 65560
  18.2 0.0 copy-start.8
  18.2 0.7 copy-done.8
  18.9 0.0 copy-start.9
  18.9 0.6 copy-done.9
  19.5 1.8 %shard_map.166 = (bf16[64,640]{1,0:T(8,128)(2,1)S(1)}, bf16[32,8,640]{2,1,0:T(8,128)(2,1)}) custom-call(s32[10]{0:T(128)S(1)} %copy-done.9, bf16[32,8,640]{2,1,0:T(8,128)(2,1)S(1)} %copy-done.1, bf16[64,512]{1,0:T(8,128)(2,1)S(1)} %bitcast.30, bf16[1,4096]{1,0:T(2,128)(2,1)S(1)} %copy-done.8, s32[8,8,32]{2,1,0:T(8,128)S(1)} %bitcast.28), custom_call_target="tpu_custom_call" | custom-call | flops 100000000 | bytes 1048576 | tf_op jit(solution)/shard_map/pallas_call | solution.py:322
  21.3 0.0 copy-start
  21.3 2.2 %copy-done = bf16[32,128,512]{2,1,0:T(8,128)(2,1)S(1)} copy-done((bf16[32,128,512]{2,1,0:T(8,128)(2,1)S(1)}, bf16[32,128,512]{2,1,0:T(8,128)(2,1)}, u32[]{:S(2)}) %copy-start) | copy-done | bytes 4194328
  23.5 0.0 copy-start.2
  23.5 1.0 %copy-done.2 = bf16[1,64,4096]{2,1,0:T(8,128)(2,1)S(1)} copy-done((bf16[1,64,4096]{2,1,0:T(8,128)(2,1)S(1)}, bf16[1,64,4096]{2,1,0:T(8,128)(2,1)}, u32[]{:S(2)}) %copy-start.2) | copy-done | bytes 524312
  24.5 0.0 copy-start.3
  24.5 0.9 %copy-done.3 = bf16[1,64,2048]{2,1,0:T(8,128)(2,1)S(1)} copy-done((bf16[1,64,2048]{2,1,0:T(8,128)(2,1)S(1)}, bf16[1,64,2048]{2,1,0:T(8,128)(2,1)}, u32[]{:S(2)}) %copy-start.3) | copy-done | bytes 262168
  25.5 1.9 %shard_map.167.after.refs_0_ = bf16[2048,640]{1,0:T(8,128)(2,1)S(1)} custom-call(bf16[64,4096]{1,0:T(8,128)(2,1)S(1)} %bitcast.26, bf16[64,2048]{1,0:T(8,128)(2,1)S(1)} %bitcast.27, bf16[32,128,512]{2,1,0:T(8,128)(2,1)S(1)} %copy-done, bf16[32,8,640]{2,1,0:T(8,128)(2,1)} %get-tuple-element.18.after), custom_call_target="tpu_custom_call" | custom-call | flops 268435456 | bytes 8388608 | tf_op jit(solution)/shard_map/pallas_call | solution.py:336
  27.4 0.0 all-to-all-done
  27.4 2.8 %collective-permute-start.3 = (bf16[320,640]{1,0:T(8,128)(2,1)S(1)}, bf16[320,640]{1,0:T(8,128)(2,1)}, u32[]{:S(2)}, u32[]{:S(2)}) collective-permute-start(bf16[320,640]{1,0:T(8,128)(2,1)S(1)} %shard_map.168.refs_1_.refs_7_), channel_id=1, source_target_pairs={{0,1},{1,0},{2,3},{3,2},{4,5},{5,4},{6,7},{7,6},{8,9},{9,8},{10,11... | collective-permute-start | bytes 1228808 | tf_op jit(solution)/shard_map/ppermute | solution.py:364
  30.2 7.8 %all-to-all-start.1 = ((bf16[32,8,640]{2,1,0:T(8,128)(2,1)}), bf16[32,8,640]{2,1,0:T(8,128)(2,1)S(1)}, u32[]{:S(2)}, u32[]{:S(2)}) async-start(bf16[32,8,640]{2,1,0:T(8,128)(2,1)} %get-tuple-element.18.after), calls=%async_computation.1 | async-start | bytes 655360 | tf_op jit(solution)/shard_map/all_to_all | solution.py:333
  38.0 2.8 %collective-permute-start = (bf16[320,640]{1,0:T(8,128)(2,1)S(1)}, bf16[320,640]{1,0:T(8,128)(2,1)}, u32[]{:S(2)}, u32[]{:S(2)}) collective-permute-start(bf16[320,640]{1,0:T(8,128)(2,1)S(1)} %shard_map.168.refs_1_.refs_7_), channel_id=1, source_target_pairs={{0,2},{1,7},{2,4},{3,1},{4,6},{5,3},{6,0},{7,5},{8,10},{9,15},{10,... | collective-permute-start | bytes 1228808 | tf_op jit(solution)/shard_map/ppermute | solution.py:363
  40.8 0.0 collective-permute-done.3.refs_2_.refs_8_
  40.8 0.5 collective-permute-start.4
  41.3 4.4 %collective-permute-done.refs_1_.refs_9_ = bf16[320,640]{1,0:T(8,128)(2,1)} collective-permute-done((bf16[320,640]{1,0:T(8,128)(2,1)S(1)}, bf16[320,640]{1,0:T(8,128)(2,1)}, u32[]{:S(2)}, u32[]{:S(2)}) %collective-permute-start) | collective-permute-done | bytes 409632 | tf_op jit(solution)/shard_map/ppermute | solution.py:363
  45.7 3.4 %collective-permute-start.1 = (bf16[320,640]{1,0:T(8,128)(2,1)}, bf16[320,640]{1,0:T(8,128)(2,1)}, u32[]{:S(2)}, u32[]{:S(2)}) collective-permute-start(bf16[320,640]{1,0:T(8,128)(2,1)} %collective-permute-done.refs_1_.refs_9_), channel_id=1, source_target_pairs={{0,2},{1,7},{2,4},{3,1},{4,6},{5,3},{6,0},{7,5},{8,10},{9,15},{10,... | collective-permute-start | bytes 1228808 | tf_op jit(solution)/shard_map/ppermute | solution.py:366
  49.1 0.0 collective-permute-start.6
  49.1 0.0 all-to-all-done.1.arrived
  49.1 0.0 copy-done.5
  49.1 0.0 copy-done.7
  49.1 0.0 copy-done.10
  49.2 1.6 %shard_map.173 = (bf16[8,8,512]{2,1,0:T(8,128)(2,1)}, bf16[8,512]{1,0:T(8,128)(2,1)}, bf16[8,8]{1,0:T(8,128)(2,1)}) custom-call(s32[10]{0:T(128)S(1)} %copy-done.10, bf16[32,8,640]{2,1,0:T(8,128)(2,1)S(1)} %all-to-all-done.1.arrived, s32[8,8,32]{2,1,0:T(8,128)S(1)} %bitcast.29, s32[8,8,32]{2,1,0:T(8,128)S(1)} %bitcast.31), custom_call_target="tpu_custom_call" | custom-call | tf_op jit(solution)/shard_map/pallas_call | solution.py:378
  50.7 0.0 collective-permute-done.4.refs_1_.refs_11_
  50.7 2.6 %collective-permute-start.5 = (bf16[320,640]{1,0:T(8,128)(2,1)}, bf16[320,640]{1,0:T(8,128)(2,1)S(1)}, u32[]{:S(2)}, u32[]{:S(2)}) collective-permute-start(bf16[320,640]{1,0:T(8,128)(2,1)} %collective-permute-done.4.refs_1_.refs_11_), channel_id=1, source_target_pairs={{0,1},{1,0},{2,3},{3,2},{4,5},{5,4},{6,7},{7,6},{8,9},{9,8},{10,11... | collective-permute-start | bytes 1228808 | tf_op jit(solution)/shard_map/ppermute | solution.py:368
  53.4 4.2 %shard_map.169 = (f32[2048,512]{1,0:T(8,128)S(1)}, f32[2048,128]{1,0:T(8,128)S(1)}, f32[2048,128]{1,0:T(8,128)S(1)}) custom-call(bf16[2048,640]{1,0:T(8,128)(2,1)S(1)} %shard_map.167.after.refs_0_, bf16[320,640]{1,0:T(8,128)(2,1)S(1)} %shard_map.168.refs_1_.refs_7_, bf16[320,640]{1,0:T(8,128)(2,1)} %collective-permute-done.3.refs_2_.refs_8_), custom_call_target="tpu_custom_call" | custom-call | flops 2415919104 | bytes 1048576 | tf_op jit(solution)/shard_map/pallas_call | solution.py:263
  57.6 0.0 collective-permute-done.1.refs_1_.refs_13_
  57.6 0.3 collective-permute-start.2
  57.8 0.0 collective-permute-done.6.refs_2_.refs_10_
  57.9 4.7 %shard_map.170 = (f32[2048,512]{1,0:T(8,128)S(1)}, f32[2048,128]{1,0:T(8,128)S(1)}, f32[2048,128]{1,0:T(8,128)S(1)}) custom-call(bf16[2048,640]{1,0:T(8,128)(2,1)S(1)} %shard_map.167.after.refs_0_, bf16[320,640]{1,0:T(8,128)(2,1)} %collective-permute-done.refs_1_.refs_9_, bf16[320,640]{1,0:T(8,128)(2,1)} %collective-permute-done.6.refs_2_.refs_10_, ...), custom_call_target="tpu_custom_call" | custom-call | flops 2415919104 | bytes 1048576 | tf_op jit(solution)/shard_map/pallas_call | solution.py:263
  62.6 0.0 collective-permute-done.5.refs_2_.refs_12_
  62.6 0.0 copy-start.11
  62.6 4.7 %shard_map.171 = (f32[2048,512]{1,0:T(8,128)S(1)}, f32[2048,128]{1,0:T(8,128)S(1)}, f32[2048,128]{1,0:T(8,128)S(1)}) custom-call(bf16[2048,640]{1,0:T(8,128)(2,1)S(1)} %shard_map.167.after.refs_0_, bf16[320,640]{1,0:T(8,128)(2,1)} %collective-permute-done.4.refs_1_.refs_11_, bf16[320,640]{1,0:T(8,128)(2,1)S(1)} %collective-permute-done.5.refs_2_.refs_12_, ...), custom_call_target="tpu_custom_call" | custom-call | flops 2415919104 | bytes 1048576 | tf_op jit(solution)/shard_map/pallas_call | solution.py:263
  67.4 0.0 collective-permute-done.2.refs_2_.refs_14_
  67.4 0.0 copy-done.11
  67.4 10.0 %shard_map.172 = bf16[64,4096]{1,0:T(8,128)(2,1)} custom-call(bf16[2048,640]{1,0:T(8,128)(2,1)S(1)} %shard_map.167.after.refs_0_, bf16[320,640]{1,0:T(8,128)(2,1)} %collective-permute-done.1.refs_1_.refs_13_, bf16[320,640]{1,0:T(8,128)(2,1)S(1)} %collective-permute-done.2.refs_2_.refs_14_, f32[2048,512]{1,0:T(8,128)S(1)} %get-tuple-element.26.refs_3_, ...), custom_call_target="tpu_custom_call" | custom-call | flops 4831838208 | bytes 1048576 | tf_op jit(solution)/shard_map/pallas_call | solution.py:263
  (4 shorter events, 0.0 us)
Async XLA Ops:
  3.7 23.7 %all-to-all-start = ((bf16[32,8,640]{2,1,0:T(8,128)(2,1)}), bf16[32,8,640]{2,1,0:T(8,128)(2,1)S(1)}, u32[]{:S(2)}, u32[]{:S(2)}) async-start(bf16[32,8,640]{2,1,0:T(8,128)(2,1)} %shard_map.165.after), calls=%async_computation | async-start | bytes 655360 | tf_op jit(solution)/shard_map/all_to_all | solution.py:319
  15.6 1.0 %copy-start.1 = (bf16[32,8,640]{2,1,0:T(8,128)(2,1)S(1)}, bf16[32,8,640]{2,1,0:T(8,128)(2,1)}, u32[]{:S(2)}) copy-start(bf16[32,8,640]{2,1,0:T(8,128)(2,1)} %shard_map.165.after) | copy-start | bytes 983044
  16.6 0.8 copy-start.4
  17.4 0.8 %copy-start.6 = (bf16[1,64,512]{2,1,0:T(8,128)(2,1)S(1)}, bf16[1,64,512]{2,1,0:T(8,128)(2,1)}, u32[]{:S(2)}) copy-start(bf16[1,64,512]{2,1,0:T(8,128)(2,1)} %param.16) | copy-start | bytes 196612
  18.2 0.7 copy-start.8
  18.9 0.6 copy-start.9
  21.3 2.2 %copy-start = (bf16[32,128,512]{2,1,0:T(8,128)(2,1)S(1)}, bf16[32,128,512]{2,1,0:T(8,128)(2,1)}, u32[]{:S(2)}) copy-start(bf16[32,128,512]{2,1,0:T(8,128)(2,1)} %weight.1) | copy-start | bytes 12582916
  23.5 1.0 %copy-start.2 = (bf16[1,64,4096]{2,1,0:T(8,128)(2,1)S(1)}, bf16[1,64,4096]{2,1,0:T(8,128)(2,1)}, u32[]{:S(2)}) copy-start(bf16[1,64,4096]{2,1,0:T(8,128)(2,1)} %param.14) | copy-start | bytes 1572868
  24.5 0.9 %copy-start.3 = (bf16[1,64,2048]{2,1,0:T(8,128)(2,1)S(1)}, bf16[1,64,2048]{2,1,0:T(8,128)(2,1)}, u32[]{:S(2)}) copy-start(bf16[1,64,2048]{2,1,0:T(8,128)(2,1)} %param.15) | copy-start | bytes 786436
  25.4 23.7 %copy-start.5 = (s32[32,8,8]{0,2,1:T(8,128)S(1)}, s32[32,8,8]{0,2,1:T(8,128)}, u32[]{:S(2)}) copy-start(s32[32,8,8]{0,2,1:T(8,128)} %param.26) | copy-start | bytes 24580
  25.5 23.7 %copy-start.7 = (s32[32,8,8]{0,2,1:T(8,128)S(1)}, s32[32,8,8]{0,2,1:T(8,128)}, u32[]{:S(2)}) copy-start(s32[32,8,8]{0,2,1:T(8,128)} %param.27) | copy-start | bytes 24580
  25.5 23.7 %copy-start.10 = (s32[10]{0:T(128)S(1)}, s32[10]{0:T(128)}, u32[]{:S(2)}) copy-start(s32[10]{0:T(128)} %stack.40.ids.refs_6_) | copy-start | bytes 124
  27.4 13.4 %collective-permute-start.3 = (bf16[320,640]{1,0:T(8,128)(2,1)S(1)}, bf16[320,640]{1,0:T(8,128)(2,1)}, u32[]{:S(2)}, u32[]{:S(2)}) collective-permute-start(bf16[320,640]{1,0:T(8,128)(2,1)S(1)} %shard_map.168.refs_1_.refs_7_), channel_id=1, source_target_pairs={{0,1},{1,0},{2,3},{3,2},{4,5},{5,4},{6,7},{7,6},{8,9},{9,8},{10,11... | collective-permute-start | bytes 1228808 | tf_op jit(solution)/shard_map/ppermute | solution.py:364
  30.2 18.9 %all-to-all-start.1 = ((bf16[32,8,640]{2,1,0:T(8,128)(2,1)}), bf16[32,8,640]{2,1,0:T(8,128)(2,1)S(1)}, u32[]{:S(2)}, u32[]{:S(2)}) async-start(bf16[32,8,640]{2,1,0:T(8,128)(2,1)} %get-tuple-element.18.after), calls=%async_computation.1 | async-start | bytes 655360 | tf_op jit(solution)/shard_map/all_to_all | solution.py:333
  38.0 7.7 %collective-permute-start = (bf16[320,640]{1,0:T(8,128)(2,1)S(1)}, bf16[320,640]{1,0:T(8,128)(2,1)}, u32[]{:S(2)}, u32[]{:S(2)}) collective-permute-start(bf16[320,640]{1,0:T(8,128)(2,1)S(1)} %shard_map.168.refs_1_.refs_7_), channel_id=1, source_target_pairs={{0,2},{1,7},{2,4},{3,1},{4,6},{5,3},{6,0},{7,5},{8,10},{9,15},{10,... | collective-permute-start | bytes 1228808 | tf_op jit(solution)/shard_map/ppermute | solution.py:363
  40.8 9.9 %collective-permute-start.4 = (bf16[320,640]{1,0:T(8,128)(2,1)}, bf16[320,640]{1,0:T(8,128)(2,1)}, u32[]{:S(2)}, u32[]{:S(2)}) collective-permute-start(bf16[320,640]{1,0:T(8,128)(2,1)} %collective-permute-done.3.refs_2_.refs_8_), channel_id=1, source_target_pairs={{0,2},{1,7},{2,4},{3,1},{4,6},{5,3},{6,0},{7,5},{8,10},{9,15},{10,... | collective-permute-start | bytes 1228808 | tf_op jit(solution)/shard_map/ppermute | solution.py:365
  45.7 11.8 %collective-permute-start.1 = (bf16[320,640]{1,0:T(8,128)(2,1)}, bf16[320,640]{1,0:T(8,128)(2,1)}, u32[]{:S(2)}, u32[]{:S(2)}) collective-permute-start(bf16[320,640]{1,0:T(8,128)(2,1)} %collective-permute-done.refs_1_.refs_9_), channel_id=1, source_target_pairs={{0,2},{1,7},{2,4},{3,1},{4,6},{5,3},{6,0},{7,5},{8,10},{9,15},{10,... | collective-permute-start | bytes 1228808 | tf_op jit(solution)/shard_map/ppermute | solution.py:366
  49.1 8.7 %collective-permute-start.6 = (bf16[320,640]{1,0:T(8,128)(2,1)}, bf16[320,640]{1,0:T(8,128)(2,1)}, u32[]{:S(2)}, u32[]{:S(2)}) collective-permute-start(bf16[320,640]{1,0:T(8,128)(2,1)} %collective-permute-done.refs_1_.refs_9_), channel_id=1, source_target_pairs={{0,1},{1,0},{2,3},{3,2},{4,5},{5,4},{6,7},{7,6},{8,9},{9,8},{10,11... | collective-permute-start | bytes 1228808 | tf_op jit(solution)/shard_map/ppermute | solution.py:367
  50.7 11.9 %collective-permute-start.5 = (bf16[320,640]{1,0:T(8,128)(2,1)}, bf16[320,640]{1,0:T(8,128)(2,1)S(1)}, u32[]{:S(2)}, u32[]{:S(2)}) collective-permute-start(bf16[320,640]{1,0:T(8,128)(2,1)} %collective-permute-done.4.refs_1_.refs_11_), channel_id=1, source_target_pairs={{0,1},{1,0},{2,3},{3,2},{4,5},{5,4},{6,7},{7,6},{8,9},{9,8},{10,11... | collective-permute-start | bytes 1228808 | tf_op jit(solution)/shard_map/ppermute | solution.py:368
  57.6 9.8 %collective-permute-start.2 = (bf16[320,640]{1,0:T(8,128)(2,1)}, bf16[320,640]{1,0:T(8,128)(2,1)S(1)}, u32[]{:S(2)}, u32[]{:S(2)}) collective-permute-start(bf16[320,640]{1,0:T(8,128)(2,1)} %collective-permute-done.1.refs_1_.refs_13_), channel_id=1, source_target_pairs={{0,1},{1,0},{2,3},{3,2},{4,5},{5,4},{6,7},{7,6},{8,9},{9,8},{10,11... | collective-permute-start | bytes 1228808 | tf_op jit(solution)/shard_map/ppermute | solution.py:369
  62.6 4.8 %copy-start.11 = (bf16[32,512,128]{2,1,0:T(8,128)(2,1)S(1)}, bf16[32,512,128]{2,1,0:T(8,128)(2,1)}, u32[]{:S(2)}) copy-start(bf16[32,512,128]{2,1,0:T(8,128)(2,1)} %refs_15_.1) | copy-start | bytes 12582916

commit v3 on v2

v3 whole, which is shorter than its diff:
```python
import functools

import jax
import jax.numpy as jnp
from jax import lax
from jax.experimental import pallas as pl
from jax.experimental.pallas import tpu as pltpu
from jax.sharding import PartitionSpec as P

HIDDEN = -1e30
QUANT_TOP = 4.0
QUANT_EPS = 1e-06
MIB = 1 << 20
LANES = 128

F32 = jnp.float32
BF16 = jnp.bfloat16
VMEM = pl.BlockSpec(memory_space=pltpu.VMEM)
SMEM = pl.BlockSpec(memory_space=pltpu.SMEM)
ANY = pl.BlockSpec(memory_space=pl.ANY)
HBM = pl.BlockSpec(memory_space=pltpu.HBM)


def iota(shape, axis):
    return lax.broadcasted_iota(jnp.int32, shape, axis)


def dot(a, b):
    return jnp.dot(a, b, preferred_element_type=F32)


def dot_nt(a, b):
    return lax.dot_general(a, b, (((1,), (1,)), ((), ())), preferred_element_type=F32)


def fold_matrix(block, rope, lanes):
    shape = (block * rope, lanes)
    return (iota(shape, 0) % rope == iota(shape, 1)).astype(F32).astype(BF16)


def pick_column(table, column):
    return jnp.sum(jnp.where(iota(table.shape, 1) == column, table, 0), axis=1)


def fetch(sources, held, semaphores):
    copies = [
        pltpu.make_async_copy(source, target, semaphores.at[i])
        for i, (source, target) in enumerate(zip(sources, held))
    ]
    for copy in copies:
        copy.start()
    return copies


def pack_kernel(own_ref, column_ref, *refs):
    message, suffix, semaphores = refs[9], refs[10], refs[20]
    for copy in fetch(refs[:9], refs[11:20], semaphores):
        copy.wait()
    latent, ropes, scales, sfx_latent, sfx_rope, prefix, owners, slots, targets = refs[11:20]
    own, column = own_ref[0], column_ref[0]
    count, block, width = latent.shape
    rope = ropes.shape[1] // block
    ctx = owners.shape[1]
    tokens = sfx_latent.shape[0]
    tail = message.shape[2] - width
    rows = 2 * block * count
    fold = fold_matrix(block, rope, tail)

    cube = (count, block, count)
    factor = jnp.broadcast_to(scales[...].astype(F32)[None], cube)
    factor = jnp.sum(jnp.where(iota(cube, 0) == iota(cube, 2), factor, 0.0), axis=2, keepdims=True)
    keys = (latent[...].astype(F32) * factor).reshape(count * block, width).astype(BF16)
    wide = (count, block, block * rope)
    spread = jnp.broadcast_to(ropes[...].astype(F32)[:, None, :], wide) * factor
    spread = jnp.where(iota(wide, 2) // rope == iota(wide, 1), spread, 0.0)
    key_tail = dot(spread.reshape(count * block, block * rope).astype(BF16), fold).astype(BF16)

    own_latent = sfx_latent[...].astype(F32)
    pieces = []
    for g in range(tokens // block):
        piece = sfx_rope[:, g * block * rope : (g + 1) * block * rope].astype(F32)
        piece = jnp.broadcast_to(piece, (block, block * rope))
        pieces.append(jnp.where(iota(piece.shape, 1) // rope == iota(piece.shape, 0), piece, 0.0))
    own_tail = dot(jnp.concatenate(pieces, axis=0).astype(BF16), fold)
    suffix[:, :width] = sfx_latent[...]
    suffix[:, width:] = own_tail.astype(BF16)
    magnitude = jnp.maximum(
        jnp.max(jnp.abs(own_latent), axis=1, keepdims=True),
        jnp.max(jnp.abs(own_tail), axis=1, keepdims=True),
    )
    token_scale = ((magnitude + QUANT_EPS) / QUANT_TOP).astype(BF16).astype(F32)
    code = (own_latent / token_scale).astype(BF16)
    code_tail = jnp.where(iota(own_tail.shape, 1) == rope, token_scale, own_tail / token_scale)
    code_tail = code_tail.astype(BF16)

    def by_row(table):
        table = pick_column(table, column)[:, None, :]
        return jnp.broadcast_to(table, (count, 2 * block, table.shape[2])).reshape(rows, table.shape[2])

    mine = by_row(owners[...]) == own
    slot = jnp.sum(jnp.where(mine, by_row(slots[...]), 0), axis=1, keepdims=True)
    place = jnp.sum(jnp.where(mine, iota(mine.shape, 1), 0), axis=1, keepdims=True)
    unit = iota((rows, 1), 0) % (2 * block)
    limit_shape = (rows, count)
    limit = jnp.where(
        iota(limit_shape, 1) == iota(limit_shape, 0) // (2 * block),
        jnp.broadcast_to(prefix[...], limit_shape),
        0,
    )
    limit = jnp.sum(limit, axis=1, keepdims=True)
    read = unit < block
    bias = jnp.where(read & ((place * ctx + column) * block >= limit), HIDDEN, 0.0)
    source = jnp.where(read, slot * block + unit, -1)
    take_read = (iota((rows, count * block), 1) == source).astype(F32).astype(BF16)
    table = targets[...]
    mark = jnp.sum(jnp.where(iota(table.shape, 0) == column, table, 0), axis=0)
    mark = jnp.sum(jnp.where(iota(mark.shape, 1) == own, mark, 0), axis=1, keepdims=True)
    new = mark.shape[0]
    mark = jnp.broadcast_to(mark, (new, tokens))
    mark = jnp.sum(jnp.where(iota(mark.shape, 0) == iota(mark.shape, 1) // block, mark, 0), axis=0, keepdims=True)
    mark = mark * (2 * block) + block + iota((1, tokens), 1) % block
    take_new = (iota((rows, tokens), 0) == mark).astype(F32).astype(BF16)

    body = dot(take_read, keys) + dot(take_new, code)
    end = dot(take_read, key_tail) + dot(take_new, code_tail)
    end = end + jnp.where(iota(end.shape, 1) == rope, bias, 0.0)
    message[:, :, :width] = body.astype(BF16).reshape(count, 2 * block, width)
    message[:, :, width:] = end.astype(BF16).reshape(count, 2 * block, tail)


def shard_kernel(arrived, after_group, after_query, shard):
    count, double, width = arrived.shape
    block = double // 2
    shard[...] = arrived[...].astype(F32)[:, :block, :].reshape(count * block, width).astype(BF16)


def join_kernel(*refs):
    *pieces, out, done = refs
    rows = pieces[0].shape[0]
    for i, piece in enumerate(pieces):
        out[i * rows : (i + 1) * rows, :] = piece[...]
    done[...] = jnp.zeros_like(done)


def join(*pieces):
    rows, wide = pieces[0].shape
    return pl.pallas_call(
        join_kernel,
        in_specs=[VMEM] * len(pieces),
        out_specs=(VMEM, VMEM),
        out_shape=(
            jax.ShapeDtypeStruct((rows * len(pieces), wide), BF16),
            jax.ShapeDtypeStruct((8, LANES), F32),
        ),
        compiler_params=pltpu.CompilerParams(vmem_limit_bytes=2 * MIB),
    )(*pieces)


def land_kernel(own_ref, column_ref, arrived, targets, slots, out_latent, out_rope, out_scale, done):
    done[...] = jnp.zeros_like(done)
    own, column = own_ref[0], column_ref[0]
    new, block, width = out_latent.shape
    count, double, _ = arrived.shape
    rope = out_rope.shape[1] // block
    tail = arrived.shape[2] - width

    def pick(table):
        return jnp.sum(jnp.where(iota(table.shape, 0) == column, table, 0), axis=0)

    target, slot = pick(targets[...]), pick(slots[...])
    cube = (new,) + target.shape
    hit = (jnp.broadcast_to(target[None], cube) == own) & (jnp.broadcast_to(slot[None], cube) == iota(cube, 0))
    source = jnp.sum(jnp.where(hit, iota(cube, 2), 0), axis=2, keepdims=True)
    source = jnp.sum(source, axis=1, keepdims=True)
    rows = new * block
    source = jnp.broadcast_to(source, (new, block, 1)).reshape(rows, 1)
    source = source * double + block + iota((rows, 1), 0) % block
    take = (iota((rows, count * double), 1) == source).astype(F32).astype(BF16)
    flat = arrived[...].reshape(count * double, width + tail)
    out_latent[...] = dot(take, flat[:, :width]).astype(BF16).reshape(new, block, width)
    end = dot(take, flat[:, width:])
    fold = fold_matrix(block, rope, tail)
    wide = dot_nt(end.astype(BF16), fold)
    wide = jnp.where(iota(wide.shape, 1) // rope == iota(wide.shape, 0) % block, wide, 0.0)
    out_rope[...] = jnp.sum(wide.reshape(new, block, block * rope), axis=1).astype(BF16)
    scale = jnp.sum(jnp.where(iota(end.shape, 1) == rope, end, 0.0), axis=1, keepdims=True)
    scale = jnp.broadcast_to(scale, (rows, block))
    scale = jnp.where(iota(scale.shape, 1) == iota(scale.shape, 0) % block, scale, 0.0)
    out_scale[...] = jnp.sum(scale.reshape(new, block, block), axis=1).astype(BF16)


def absorb_kernel(nope_hbm, rotary_hbm, weight_hbm, after, out, done, nope, rotary, weight, semaphores):
    done[...] = jnp.zeros_like(done)
    heads, depth, width = weight.shape
    tokens = nope.shape[0]
    rope = rotary.shape[1] // heads
    tail = out.shape[1] - width
    chunk = 8
    parts = [pl.ds(i * chunk, chunk) for i in range(heads // chunk)]
    copies = fetch(
        [nope_hbm, rotary_hbm] + [weight_hbm.at[p] for p in parts],
        [nope, rotary] + [weight.at[p] for p in parts],
        semaphores,
    )
    copies[0].wait()
    copies[1].wait()
    filler = (iota((tokens, tail - rope), 1) == 0).astype(F32).astype(BF16)
    for h in range(heads):
        if h % chunk == 0:
            copies[2 + h // chunk].wait()
        rows = slice(h * tokens, (h + 1) * tokens)
        out[rows, :width] = dot(nope[:, h * depth : (h + 1) * depth], weight[h]).astype(BF16)
        out[rows, width:] = jnp.concatenate([rotary[:, h * rope : (h + 1) * rope], filler], axis=1)


def attend_kernel(groups, blocks, first, last, sub, tokens, scale, *refs):
    refs = list(refs)
    query = refs.pop(0)
    if groups:
        group_ref = refs.pop(0)
    block_refs = [refs.pop(0) for _ in range(blocks)]
    if groups:
        column = refs.pop(0)[0]
    if not first:
        acc_in, top_in, total_in = refs.pop(0), refs.pop(0), refs.pop(0)
    if last:
        value, out = refs
    else:
        acc_out, top_out, total_out = refs
    width = value.shape[1] if last else acc_out.shape[1]
    keys = [ref[...] for ref in block_refs]
    if groups:
        keys.insert(0, group_ref[...])
        ctx = group_ref.shape[0] // tokens
        core = lax.rem(column, 2)
        turn = 4 * core - 2
        order = [column, column + turn, column + 1 - 2 * core - turn, column + 2 * turn]
        order = [lax.rem(index + ctx, ctx) for index in order]
        order = [c for index in order for c in (index, index + 1 - 2 * core)]
        shape = (1, keys[0].shape[0])
        place = iota(shape, 1) % tokens
        for i, index in enumerate(order):
            place = place + jnp.where(iota(shape, 1) // tokens == i, index * tokens, 0)
        seen = place <= column * tokens + iota((sub, 1), 0) % tokens
    for part in range(query.shape[0] // sub):
        rows = slice(part * sub, (part + 1) * sub)
        q = query[rows, :]
        scores = [dot_nt(q, k) for k in keys]
        if groups:
            scores[0] = jnp.where(seen, scores[0], HIDDEN)
        top = functools.reduce(jnp.maximum, [jnp.max(s, axis=1, keepdims=True) for s in scores])
        weights = [jnp.exp((s - top) * scale) for s in scores]
        total = sum(jnp.sum(w, axis=1, keepdims=True) for w in weights)
        mixed = sum(dot(w.astype(BF16), k[:, :width]) for w, k in zip(weights, keys))
        top = jnp.broadcast_to(top, (sub, LANES))
        total = jnp.broadcast_to(total, (sub, LANES))
        if first:
            acc_out[rows, :] = mixed
            top_out[rows, :] = top
            total_out[rows, :] = total
            continue
        joint = jnp.maximum(top, top_in[rows, :])
        gain = jnp.exp((top - joint) * scale)
        fade = jnp.exp((top_in[rows, :] - joint) * scale)
        total = total * gain + total_in[rows, :] * fade
        if last:
            inverse = 1.0 / total
            gain, fade = gain * inverse, fade * inverse
        chunks = []
        for c in range(width // LANES):
            at = slice(c * LANES, (c + 1) * LANES)
            chunk = mixed[:, at] * gain + acc_in[rows, at] * fade
            if last:
                chunks.append(chunk.astype(BF16))
            else:
                acc_out[rows, at] = chunk
        if last:
            mixed = jnp.concatenate(chunks, axis=1)
            lanes = value.shape[2]
            for h in range(sub // tokens):
                head = part * (sub // tokens) + h
                out[:, head * lanes : (head + 1) * lanes] = dot(
                    mixed[h * tokens : (h + 1) * tokens], value[head]
                ).astype(BF16)
        else:
            top_out[rows, :] = joint
            total_out[rows, :] = total


def attend(query, blocks, tokens, width, scale, group=None, column=None, state=None, value=None, sub=1024):
    rows, wide = query.shape
    first, last = state is None, value is not None
    groups = group is not None
    operands = [query] + [group] * groups + list(blocks)
    specs = [VMEM] * len(operands)
    keys = sum(k.shape[0] for k in operands[1:])
    if groups:
        operands.append(column)
        specs.append(SMEM)
    if not first:
        operands += list(state)
        specs += [VMEM] * 3
    if last:
        operands.append(value)
        specs.append(VMEM)
        out_shape = jax.ShapeDtypeStruct((tokens, rows // tokens * value.shape[2]), BF16)
        out_specs = VMEM
    else:
        out_shape = tuple(jax.ShapeDtypeStruct((rows, n), F32) for n in (width, LANES, LANES))
        out_specs = (VMEM, VMEM, VMEM)
    return pl.pallas_call(
        functools.partial(attend_kernel, groups, len(blocks), first, last, sub, tokens, scale),
        in_specs=specs,
        out_specs=out_specs,
        out_shape=out_shape,
        compiler_params=pltpu.CompilerParams(vmem_limit_bytes=24 * MIB),
        cost_estimate=pl.CostEstimate(
            flops=2 * rows * keys * (wide + width), bytes_accessed=MIB, transcendentals=rows * keys
        ),
    )(*operands)


def body(
    query_nope,
    query_rope,
    suffix_latent,
    suffix_rope,
    absorb_key,
    absorb_value,
    pool_latent,
    pool_rope,
    pool_scale,
    prefix_tokens,
    block_owner,
    block_slot,
    write_owner,
    write_slot,
):
    own = lax.axis_index("pool")
    column = lax.axis_index("ctx")
    count = lax.axis_size("pool")
    ctx = lax.axis_size("ctx")
    heads, nope, latent = absorb_key.shape
    tokens = query_nope.shape[1]
    rope = query_rope.shape[2] // heads
    block = pool_scale.shape[3]
    slots = pool_scale.shape[2]
    new_blocks = write_owner.shape[2]
    wide = latent + 128
    scale = (nope + rope) ** -0.5
    own_at, column_at = own.reshape(1), column.reshape(1)
    ring = [(s, (s + (2 if s % 2 == 0 else -2)) % ctx) for s in range(ctx)]
    swap = [(s, s ^ 1) for s in range(ctx)]

    rows = slots * block
    targets, target_slots = jnp.transpose(write_owner, (1, 2, 0)), jnp.transpose(write_slot, (1, 2, 0))
    operands = (
        pool_latent[0, 0],
        pool_rope[0, 0],
        pool_scale[0, 0].T,
        suffix_latent[0],
        suffix_rope,
        prefix_tokens[None],
        block_owner,
        block_slot,
        targets,
    )
    message, suffix = pl.pallas_call(
        pack_kernel,
        in_specs=[SMEM, SMEM] + [HBM] * len(operands),
        out_specs=(VMEM, VMEM),
        out_shape=(
            jax.ShapeDtypeStruct((count, 2 * block, wide), BF16),
            jax.ShapeDtypeStruct((tokens, wide), BF16),
        ),
        scratch_shapes=[pltpu.VMEM(x.shape, x.dtype) for x in operands]
        + [pltpu.SemaphoreType.DMA((len(operands),))],
        compiler_params=pltpu.CompilerParams(vmem_limit_bytes=60 * MIB),
    )(own_at, column_at, *operands)
    arrived = lax.all_to_all(message, "pool", split_axis=0, concat_axis=0, tiled=True)

    pair, _ = join(suffix, lax.ppermute(suffix, "ctx", swap))
    pair_first = lax.ppermute(pair, "ctx", ring)
    operands = (query_nope[0], query_rope[0], absorb_key)
    query, query_done = pl.pallas_call(
        absorb_kernel,
        in_specs=[HBM] * 3 + [ANY],
        out_specs=(VMEM, VMEM),
        out_shape=(jax.ShapeDtypeStruct((heads * tokens, wide), BF16), jax.ShapeDtypeStruct((8, LANES), F32)),
        scratch_shapes=[pltpu.VMEM(x.shape, x.dtype) for x in operands]
        + [pltpu.SemaphoreType.DMA((2 + heads // 8,))],
        compiler_params=pltpu.CompilerParams(vmem_limit_bytes=16 * MIB),
        cost_estimate=pl.CostEstimate(
            flops=2 * heads * tokens * nope * latent, bytes_accessed=8 * MIB, transcendentals=0
        ),
    )(*operands, pair)

    pair_swap = lax.ppermute(pair_first, "ctx", swap)
    pair_far = lax.ppermute(pair_first, "ctx", ring)
    group, group_done = join(pair, pair_first, pair_swap, pair_far)

    shard = pl.pallas_call(
        shard_kernel,
        in_specs=[VMEM, ANY, ANY],
        out_specs=VMEM,
        out_shape=jax.ShapeDtypeStruct((rows, wide), BF16),
        compiler_params=pltpu.CompilerParams(vmem_limit_bytes=4 * MIB),
    )(arrived, group_done, query_done)

    run = functools.partial(attend, query, tokens=tokens, width=latent, scale=scale)
    first = lax.ppermute(shard, "ctx", ring)
    sibling = lax.ppermute(shard, "ctx", swap)
    state = run([], group=group, column=column_at)
    sibling, first, total = lax.optimization_barrier((sibling, first, state[2]))
    second = lax.ppermute(sibling, "ctx", ring)
    first_swap = lax.ppermute(first, "ctx", swap)
    third = lax.ppermute(first, "ctx", ring)
    state = run([shard, sibling], state=(state[0], state[1], total))
    written_latent, written_rope, written_scale, landed = pl.pallas_call(
        land_kernel,
        in_specs=[SMEM, SMEM] + [VMEM] * 3,
        out_specs=(VMEM,) * 4,
        out_shape=(
            jax.ShapeDtypeStruct((new_blocks, block, latent), BF16),
            jax.ShapeDtypeStruct((new_blocks, block * rope), BF16),
            jax.ShapeDtypeStruct((new_blocks, block), BF16),
            jax.ShapeDtypeStruct((8, LANES), F32),
        ),
        compiler_params=pltpu.CompilerParams(vmem_limit_bytes=8 * MIB),
    )(own_at, column_at, arrived, targets, target_slots)
    first_swap, landed = lax.optimization_barrier((first_swap, landed))
    state = run([first, first_swap], state=state)
    second, third, total = lax.optimization_barrier((second, third, state[2]))
    second_swap = lax.ppermute(second, "ctx", swap)
    third_swap = lax.ppermute(third, "ctx", swap)
    state = run([second, third], state=(state[0], state[1], total))
    attended = run([second_swap, third_swap], state=state, value=absorb_value)
    return (attended[None], written_latent[None, None], written_rope[None, None], written_scale[None, None])


def solution(mesh):
    placed = (
        P("pool", "ctx", None),
        P("pool", "ctx", None),
        P("pool", "ctx", None),
        P("pool", "ctx"),
        P(),
        P(),
        P("pool", "ctx", None, None, None),
        P("pool", "ctx", None, None),
        P("pool", "ctx", None, None),
        P(),
        P(),
        P(),
        P(),
        P(),
    )
    return jax.shard_map(
        body,
        mesh=mesh,
        in_specs=placed,
        out_specs=(
            P("pool", "ctx", None),
            P("pool", "ctx", None, None, None),
            P("pool", "ctx", None, None),
            P("pool", "ctx", None, None),
        ),
        check_vma=False,
    )
```

time: 78 us -> 67.3 us (0.86)
  Pallas kernels: 31.3 us -> 25.5 us
  starting transfers between devices: 32 us -> 29.6 us
  local copies, waits for them, and re-layouts: 8.7 us -> 7.05 us
    all_to_all x1 -> x0, starting transfers between devices: 7.76 us -> none  [body(): lax.all_to_all(codes, 'pool', split_axis=0, concat_axis=0, tiled=True)]
    ppermute x0 -> x4, starting transfers between devices: none -> 7.19 us  [the longest x1 3.41 us: body(): pair_far = lax.ppermute(pair_first, 'ctx', ring)]
    pallas_call x9 -> x11, Pallas kernels: 31.3 us -> 25.5 us  [the longest x5 19.1 us: attend(): pl.pallas_call(functools.partial(attend_kernel, groups, len(blocks), firs...]
    ppermute x1, waiting for transfers between devices: 4.43 us -> 0.01 us  [body(): first = lax.ppermute(shard, 'ctx', ring)]
    ppermute x0 -> x4, waiting for transfers between devices: none -> 3.4 us  [the longest x1 2.26 us: body(): pair_first = lax.ppermute(pair, 'ctx', ring)]
    ppermute x1, starting transfers between devices: 0.01 us -> 2.31 us  [body(): first_swap = lax.ppermute(first, 'ctx', swap)]
    ppermute x1, starting transfers between devices: 3.41 us -> 1.51 us  [body(): third = lax.ppermute(first, 'ctx', ring)]
    ppermute x1, starting transfers between devices: 2.81 us -> 1.51 us  [body(): first = lax.ppermute(shard, 'ctx', ring)]
  transfers between devices with their start and end apart: 9 -> 12, of which waited for: 1 -> 3; matrix products, arithmetic and copies ran while one was open for 0% -> 0% of each run, Pallas kernels for 24% -> 26%
where the time goes in v3:
time: 67.3 us; the launch traced here: 66.9 us
  starting transfers between devices  29.6 us (44%)
  Pallas kernels  25.5 us (38%)
  local copies, waits for them, and re-layouts  7.05 us (10%)
  waiting for transfers between devices  3.96 us (6%)
  between operations  0.8 us (1%)
    pallas_call x5, Pallas kernels, attend(): pl.pallas_call(functools.partial(attend_kernel, groups, len(blocks), firs...  19.1 us
    all_to_all x1, starting transfers between devices, body(): lax.all_to_all(message, 'pool', split_axis=0, concat_axis=0, tiled=True)  11.9 us
    unnamed x18, local copies, waits for them, and re-layouts  7.05 us
    ppermute x1, starting transfers between devices, body(): pair_far = lax.ppermute(pair_first, 'ctx', ring)  3.41 us
    pallas_call x1, Pallas kernels, body(): pl.pallas_call(pack_kernel, in_specs=[SMEM, SMEM] + [HBM] * len(operands)...  3.07 us
    ppermute x1, starting transfers between devices, body(): pair_first = lax.ppermute(pair, 'ctx', ring)  2.73 us
    ppermute x1, starting transfers between devices, body(): sibling = lax.ppermute(shard, 'ctx', swap)  2.7 us
    ppermute x1, starting transfers between devices, body(): first_swap = lax.ppermute(first, 'ctx', swap)  2.31 us
  transfers between devices with their start and end apart: 12, of which 3 were waited for; matrix products, arithmetic and copies ran while one was open for 0% of the time, Pallas kernels for 26%

profile of v3, /device:TPU:1, one launch (start us, length us, event | category | flops | bytes accessed | tf_op | source)
XLA Modules:
  0.0 66.9 jit_solution(10942603321600385502)
XLA Ops:
  0.6 3.1 %shard_map.165 = (bf16[32,16,640]{2,1,0:T(8,128)(2,1)}, bf16[64,640]{1,0:T(8,128)(2,1)}) custom-call(s32[1]{0:T(128)} %bitcast.2.own_ref, s32[1]{0:T(128)} %bitcast.3.column_ref.refs_2_, bf16[32,8,512]{2,1,0:T(8,128)(2,1)} %bitcast.23, bf16[32,512]{1,0:T(8,128)(2,1)} %bitcast.25, bf16[8,32]{1,0:T(8,128)(2,1)} %bitcast.26, bf16[64,512]{1,0:T(8,128)(2,1)} %bitcast.24, ...), custom_call_target="tpu_custom_call" | custom-call | tf_op jit(solution)/shard_map/pallas_call | solution.py:368
  3.7 11.9 %all-to-all-start = ((bf16[32,16,640]{2,1,0:T(8,128)(2,1)}), bf16[32,16,640]{2,1,0:T(8,128)(2,1)S(1)}, u32[]{:S(2)}, u32[]{:S(2)}) async-start(bf16[32,16,640]{2,1,0:T(8,128)(2,1)} %get-tuple-element.35), calls=%async_computation | async-start | bytes 1310720 | tf_op jit(solution)/shard_map/all_to_all | solution.py:380
  15.6 1.0 %collective-permute-start = (bf16[64,640]{1,0:T(8,128)(2,1)}, bf16[64,640]{1,0:T(8,128)(2,1)S(1)}, u32[]{:S(2)}, u32[]{:S(2)}) collective-permute-start(bf16[64,640]{1,0:T(8,128)(2,1)} %get-tuple-element.32.refs_0_), channel_id=1, source_target_pairs={{0,1},{1,0},{2,3},{3,2},{4,5},{5,4},{6,7},{7,6},{8,9},{9,8},{10,11... | collective-permute-start | bytes 245768 | tf_op jit(solution)/shard_map/ppermute | solution.py:382
  16.6 1.1 %collective-permute-done.refs_1_ = bf16[64,640]{1,0:T(8,128)(2,1)S(1)} collective-permute-done((bf16[64,640]{1,0:T(8,128)(2,1)}, bf16[64,640]{1,0:T(8,128)(2,1)S(1)}, u32[]{:S(2)}, u32[]{:S(2)}) %collective-permute-start) | collective-permute-done | bytes 81952 | tf_op jit(solution)/shard_map/ppermute | solution.py:382
  17.8 0.0 copy-start.5
  17.8 0.9 %copy-done.5 = bf16[64,640]{1,0:T(8,128)(2,1)S(1)} copy-done((bf16[64,640]{1,0:T(8,128)(2,1)S(1)}, bf16[64,640]{1,0:T(8,128)(2,1)}, u32[]{:S(2)}) %copy-start.5) | copy-done | bytes 81944
  18.7 0.6 shard_map.166
  19.3 2.7 %collective-permute-start.1 = (bf16[128,640]{1,0:T(8,128)(2,1)S(1)}, bf16[128,640]{1,0:T(8,128)(2,1)S(1)}, u32[]{:S(2)}, u32[]{:S(2)}) collective-permute-start(bf16[128,640]{1,0:T(8,128)(2,1)S(1)} %get-tuple-element.33.after.refs_0_), channel_id=1, source_target_pairs={{0,2},{1,7},{2,4},{3,1},{4,6},{5,3},{6,0},{7,5},{8,10},{9,15},{10,... | collective-permute-start | bytes 491528 | tf_op jit(solution)/shard_map/ppermute | solution.py:383
  22.0 2.3 %collective-permute-done.1.refs_1_ = bf16[128,640]{1,0:T(8,128)(2,1)S(1)} collective-permute-done((bf16[128,640]{1,0:T(8,128)(2,1)S(1)}, bf16[128,640]{1,0:T(8,128)(2,1)S(1)}, u32[]{:S(2)}, u32[]{:S(2)}) %collective-permute-start.1) | collective-permute-done | bytes 163872 | tf_op jit(solution)/shard_map/ppermute | solution.py:383
  24.3 3.4 %collective-permute-start.3 = (bf16[128,640]{1,0:T(8,128)(2,1)S(1)}, bf16[128,640]{1,0:T(8,128)(2,1)S(1)}, u32[]{:S(2)}, u32[]{:S(2)}) collective-permute-start(bf16[128,640]{1,0:T(8,128)(2,1)S(1)} %collective-permute-done.1.refs_1_), channel_id=1, source_target_pairs={{0,2},{1,7},{2,4},{3,1},{4,6},{5,3},{6,0},{7,5},{8,10},{9,15},{10,... | collective-permute-start | bytes 491528 | tf_op jit(solution)/shard_map/ppermute | solution.py:399
  27.7 0.0 collective-permute-start.2
  27.7 0.0 copy-start.1
  27.7 2.2 %copy-done.1 = bf16[32,128,512]{2,1,0:T(8,128)(2,1)S(1)} copy-done((bf16[32,128,512]{2,1,0:T(8,128)(2,1)S(1)}, bf16[32,128,512]{2,1,0:T(8,128)(2,1)}, u32[]{:S(2)}) %copy-start.1) | copy-done | bytes 4194328
  29.9 1.0 %copy-done.2 = bf16[1,64,4096]{2,1,0:T(8,128)(2,1)S(1)} copy-done((bf16[1,64,4096]{2,1,0:T(8,128)(2,1)S(1)}, bf16[1,64,4096]{2,1,0:T(8,128)(2,1)}, u32[]{:S(2)}) %copy-start.2) | copy-done | bytes 524312
  30.9 0.9 %copy-done.3 = bf16[1,64,2048]{2,1,0:T(8,128)(2,1)S(1)} copy-done((bf16[1,64,2048]{2,1,0:T(8,128)(2,1)S(1)}, bf16[1,64,2048]{2,1,0:T(8,128)(2,1)}, u32[]{:S(2)}) %copy-start.3) | copy-done | bytes 262168
  31.9 1.6 %shard_map.167 = (bf16[2048,640]{1,0:T(8,128)(2,1)S(1)}, f32[8,128]{1,0:T(8,128)S(1)}) custom-call(bf16[64,4096]{1,0:T(8,128)(2,1)S(1)} %bitcast.17, bf16[64,2048]{1,0:T(8,128)(2,1)S(1)} %bitcast.18, bf16[32,128,512]{2,1,0:T(8,128)(2,1)S(1)} %copy-done.1, bf16[128,640]{1,0:T(8,128)(2,1)S(1)} %get-tuple-element.33.after.refs_0_), custom_call_target="tpu_custom_call" | custom-call | flops 268435456 | bytes 8388608 | tf_op jit(solution)/shard_map/pallas_call | solution.py:385
  33.5 0.0 collective-permute-done.3.refs_3_
  33.5 0.0 collective-permute-done.2.refs_2_
  33.5 0.1 shard_map.168
  33.5 0.0 copy-start.7
  33.6 0.9 %copy-done.7 = bf16[512,640]{1,0:T(8,128)(2,1)} copy-done((bf16[512,640]{1,0:T(8,128)(2,1)}, bf16[512,640]{1,0:T(8,128)(2,1)S(1)}, u32[]{:S(2)}) %copy-start.7) | copy-done | bytes 655384
  34.4 0.0 all-to-all-done.arrived
  34.5 1.5 %collective-permute-start.5 = (bf16[256,640]{1,0:T(8,128)(2,1)S(1)}, bf16[256,640]{1,0:T(8,128)(2,1)S(1)}, u32[]{:S(2)}, u32[]{:S(2)}) collective-permute-start(bf16[256,640]{1,0:T(8,128)(2,1)S(1)} %shard_map.169.refs_1_), channel_id=1, source_target_pairs={{0,2},{1,7},{2,4},{3,1},{4,6},{5,3},{6,0},{7,5},{8,10},{9,15},{10,... | collective-permute-start | bytes 983048 | tf_op jit(solution)/shard_map/ppermute | solution.py:411
  36.0 2.7 %collective-permute-start.4 = (bf16[256,640]{1,0:T(8,128)(2,1)S(1)}, bf16[256,640]{1,0:T(8,128)(2,1)S(1)}, u32[]{:S(2)}, u32[]{:S(2)}) collective-permute-start(bf16[256,640]{1,0:T(8,128)(2,1)S(1)} %shard_map.169.refs_1_), channel_id=1, source_target_pairs={{0,1},{1,0},{2,3},{3,2},{4,5},{5,4},{6,7},{7,6},{8,9},{9,8},{10,11... | collective-permute-start | bytes 983048 | tf_op jit(solution)/shard_map/ppermute | solution.py:412
  38.7 1.1 %copy-done.8 = bf16[512,640]{1,0:T(8,128)(2,1)S(1)} copy-done((bf16[512,640]{1,0:T(8,128)(2,1)S(1)}, bf16[512,640]{1,0:T(8,128)(2,1)}, u32[]{:S(2)}) %copy-start.8) | copy-done | bytes 655384
  39.8 3.3 %shard_map.170 = (f32[2048,512]{1,0:T(8,128)S(1)}, f32[2048,128]{1,0:T(8,128)S(1)}, f32[2048,128]{1,0:T(8,128)S(1)}) custom-call(bf16[2048,640]{1,0:T(8,128)(2,1)S(1)} %get-tuple-element.34.refs_0_, bf16[512,640]{1,0:T(8,128)(2,1)S(1)} %copy-done.8, s32[1]{0:T(128)} %bitcast.3.column_ref.refs_2_), custom_call_target="tpu_custom_call" | custom-call | flops 2415919104 | bytes 1048576 | tf_op jit(solution)/shard_map/pallas_call | solution.py:311
  43.1 0.0 collective-permute-done.5.refs_1_
  43.1 0.0 collective-permute-done.4.refs_2_
  43.1 2.3 %collective-permute-start.8 = (bf16[256,640]{1,0:T(8,128)(2,1)S(1)}, bf16[256,640]{1,0:T(8,128)(2,1)S(1)}, u32[]{:S(2)}, u32[]{:S(2)}) collective-permute-start(bf16[256,640]{1,0:T(8,128)(2,1)S(1)} %collective-permute-done.5.refs_1_), channel_id=1, source_target_pairs={{0,1},{1,0},{2,3},{3,2},{4,5},{5,4},{6,7},{7,6},{8,9},{9,8},{10,11... | collective-permute-start | bytes 983048 | tf_op jit(solution)/shard_map/ppermute | solution.py:416
  45.4 1.5 %collective-permute-start.7 = (bf16[256,640]{1,0:T(8,128)(2,1)S(1)}, bf16[256,640]{1,0:T(8,128)(2,1)S(1)}, u32[]{:S(2)}, u32[]{:S(2)}) collective-permute-start(bf16[256,640]{1,0:T(8,128)(2,1)S(1)} %collective-permute-done.5.refs_1_), channel_id=1, source_target_pairs={{0,2},{1,7},{2,4},{3,1},{4,6},{5,3},{6,0},{7,5},{8,10},{9,15},{10,... | collective-permute-start | bytes 983048 | tf_op jit(solution)/shard_map/ppermute | solution.py:417
  46.9 0.5 collective-permute-start.6
  47.4 3.6 %shard_map.171 = (f32[2048,512]{1,0:T(8,128)S(1)}, f32[2048,128]{1,0:T(8,128)S(1)}, f32[2048,128]{1,0:T(8,128)S(1)}) custom-call(bf16[2048,640]{1,0:T(8,128)(2,1)S(1)} %get-tuple-element.34.refs_0_, bf16[256,640]{1,0:T(8,128)(2,1)S(1)} %shard_map.169.refs_1_, bf16[256,640]{1,0:T(8,128)(2,1)S(1)} %collective-permute-done.4.refs_2_, ...), custom_call_target="tpu_custom_call" | custom-call | flops 2415919104 | bytes 1048576 | tf_op jit(solution)/shard_map/pallas_call | solution.py:311
  51.0 0.0 collective-permute-done.8.refs_2_
  51.0 0.0 copy-start.4
  51.0 0.0 copy-start.6
  51.0 3.6 %shard_map.172 = (f32[2048,512]{1,0:T(8,128)S(1)}, f32[2048,128]{1,0:T(8,128)S(1)}, f32[2048,128]{1,0:T(8,128)S(1)}) custom-call(bf16[2048,640]{1,0:T(8,128)(2,1)S(1)} %get-tuple-element.34.refs_0_, bf16[256,640]{1,0:T(8,128)(2,1)S(1)} %collective-permute-done.5.refs_1_, bf16[256,640]{1,0:T(8,128)(2,1)S(1)} %collective-permute-done.8.refs_2_, ...), custom_call_target="tpu_custom_call" | custom-call | flops 2415919104 | bytes 1048576 | tf_op jit(solution)/shard_map/pallas_call | solution.py:311
  54.6 0.5 collective-permute-done.6.refs_1_
  55.1 0.0 collective-permute-done.7.refs_2_
  55.1 2.1 %collective-permute-start.9 = (bf16[256,640]{1,0:T(8,128)(2,1)S(1)}, bf16[256,640]{1,0:T(8,128)(2,1)S(1)}, u32[]{:S(2)}, u32[]{:S(2)}) collective-permute-start(bf16[256,640]{1,0:T(8,128)(2,1)S(1)} %collective-permute-done.6.refs_1_), channel_id=1, source_target_pairs={{0,1},{1,0},{2,3},{3,2},{4,5},{5,4},{6,7},{7,6},{8,9},{9,8},{10,11... | collective-permute-start | bytes 983048 | tf_op jit(solution)/shard_map/ppermute | solution.py:434
  57.2 0.0 collective-permute-start.10
  57.2 0.0 copy-done.4
  57.2 0.0 copy-done.6
  57.2 1.1 %shard_map.175 = (bf16[8,8,512]{2,1,0:T(8,128)(2,1)}, bf16[8,512]{1,0:T(8,128)(2,1)}, bf16[8,8]{1,0:T(8,128)(2,1)}, f32[8,128]{1,0:T(8,128)}) custom-call(s32[1]{0:T(128)} %bitcast.2.own_ref, s32[1]{0:T(128)} %bitcast.3.column_ref.refs_2_, bf16[32,16,640]{2,1,0:T(8,128)(2,1)S(1)} %all-to-all-done.arrived, s32[8,8,32]{2,1,0:T(8,128)S(1)} %bitcast.20, ...), custom_call_target="tpu_custom_call" | custom-call | tf_op jit(solution)/shard_map/pallas_call | solution.py:419
  58.3 3.6 %shard_map.173 = (f32[2048,512]{1,0:T(8,128)S(1)}, f32[2048,128]{1,0:T(8,128)S(1)}, f32[2048,128]{1,0:T(8,128)S(1)}) custom-call(bf16[2048,640]{1,0:T(8,128)(2,1)S(1)} %get-tuple-element.34.refs_0_, bf16[256,640]{1,0:T(8,128)(2,1)S(1)} %collective-permute-done.6.refs_1_, bf16[256,640]{1,0:T(8,128)(2,1)S(1)} %collective-permute-done.7.refs_2_, ...), custom_call_target="tpu_custom_call" | custom-call | flops 2415919104 | bytes 1048576 | tf_op jit(solution)/shard_map/pallas_call | solution.py:311
  61.9 0.0 collective-permute-done.9.refs_1_
  61.9 0.0 collective-permute-done.10.refs_2_
  61.9 0.0 copy-done
  61.9 5.0 %shard_map.174 = bf16[64,4096]{1,0:T(8,128)(2,1)} custom-call(bf16[2048,640]{1,0:T(8,128)(2,1)S(1)} %get-tuple-element.34.refs_0_, bf16[256,640]{1,0:T(8,128)(2,1)S(1)} %collective-permute-done.9.refs_1_, bf16[256,640]{1,0:T(8,128)(2,1)S(1)} %collective-permute-done.10.refs_2_, f32[2048,512]{1,0:T(8,128)S(1)} %get-tuple-element.54.refs_3_, ...), custom_call_target="tpu_custom_call" | custom-call | flops 2415919104 | bytes 1048576 | tf_op jit(solution)/shard_map/pallas_call | solution.py:311
  (5 shorter events, 0.0 us)
Async XLA Ops:
  3.7 30.7 %all-to-all-start = ((bf16[32,16,640]{2,1,0:T(8,128)(2,1)}), bf16[32,16,640]{2,1,0:T(8,128)(2,1)S(1)}, u32[]{:S(2)}, u32[]{:S(2)}) async-start(bf16[32,16,640]{2,1,0:T(8,128)(2,1)} %get-tuple-element.35), calls=%async_computation | async-start | bytes 1310720 | tf_op jit(solution)/shard_map/all_to_all | solution.py:380
  15.6 2.2 %collective-permute-start = (bf16[64,640]{1,0:T(8,128)(2,1)}, bf16[64,640]{1,0:T(8,128)(2,1)S(1)}, u32[]{:S(2)}, u32[]{:S(2)}) collective-permute-start(bf16[64,640]{1,0:T(8,128)(2,1)} %get-tuple-element.32.refs_0_), channel_id=1, source_target_pairs={{0,1},{1,0},{2,3},{3,2},{4,5},{5,4},{6,7},{7,6},{8,9},{9,8},{10,11... | collective-permute-start | bytes 245768 | tf_op jit(solution)/shard_map/ppermute | solution.py:382
  17.8 0.9 %copy-start.5 = (bf16[64,640]{1,0:T(8,128)(2,1)S(1)}, bf16[64,640]{1,0:T(8,128)(2,1)}, u32[]{:S(2)}) copy-start(bf16[64,640]{1,0:T(8,128)(2,1)} %get-tuple-element.32.refs_0_) | copy-start | bytes 245764
  19.3 5.0 %collective-permute-start.1 = (bf16[128,640]{1,0:T(8,128)(2,1)S(1)}, bf16[128,640]{1,0:T(8,128)(2,1)S(1)}, u32[]{:S(2)}, u32[]{:S(2)}) collective-permute-start(bf16[128,640]{1,0:T(8,128)(2,1)S(1)} %get-tuple-element.33.after.refs_0_), channel_id=1, source_target_pairs={{0,2},{1,7},{2,4},{3,1},{4,6},{5,3},{6,0},{7,5},{8,10},{9,15},{10,... | collective-permute-start | bytes 491528 | tf_op jit(solution)/shard_map/ppermute | solution.py:383
  24.3 9.2 %collective-permute-start.3 = (bf16[128,640]{1,0:T(8,128)(2,1)S(1)}, bf16[128,640]{1,0:T(8,128)(2,1)S(1)}, u32[]{:S(2)}, u32[]{:S(2)}) collective-permute-start(bf16[128,640]{1,0:T(8,128)(2,1)S(1)} %collective-permute-done.1.refs_1_), channel_id=1, source_target_pairs={{0,2},{1,7},{2,4},{3,1},{4,6},{5,3},{6,0},{7,5},{8,10},{9,15},{10,... | collective-permute-start | bytes 491528 | tf_op jit(solution)/shard_map/ppermute | solution.py:399
  27.7 5.8 %collective-permute-start.2 = (bf16[128,640]{1,0:T(8,128)(2,1)S(1)}, bf16[128,640]{1,0:T(8,128)(2,1)S(1)}, u32[]{:S(2)}, u32[]{:S(2)}) collective-permute-start(bf16[128,640]{1,0:T(8,128)(2,1)S(1)} %collective-permute-done.1.refs_1_), channel_id=1, source_target_pairs={{0,1},{1,0},{2,3},{3,2},{4,5},{5,4},{6,7},{7,6},{8,9},{9,8},{10,11... | collective-permute-start | bytes 491528 | tf_op jit(solution)/shard_map/ppermute | solution.py:398
  27.7 2.2 %copy-start.1 = (bf16[32,128,512]{2,1,0:T(8,128)(2,1)S(1)}, bf16[32,128,512]{2,1,0:T(8,128)(2,1)}, u32[]{:S(2)}) copy-start(bf16[32,128,512]{2,1,0:T(8,128)(2,1)} %weight_hbm.1) | copy-start | bytes 12582916
  29.9 1.0 %copy-start.2 = (bf16[1,64,4096]{2,1,0:T(8,128)(2,1)S(1)}, bf16[1,64,4096]{2,1,0:T(8,128)(2,1)}, u32[]{:S(2)}) copy-start(bf16[1,64,4096]{2,1,0:T(8,128)(2,1)} %param.14) | copy-start | bytes 1572868
  30.9 0.9 %copy-start.3 = (bf16[1,64,2048]{2,1,0:T(8,128)(2,1)S(1)}, bf16[1,64,2048]{2,1,0:T(8,128)(2,1)}, u32[]{:S(2)}) copy-start(bf16[1,64,2048]{2,1,0:T(8,128)(2,1)} %param.15) | copy-start | bytes 786436
  33.5 0.9 %copy-start.7 = (bf16[512,640]{1,0:T(8,128)(2,1)}, bf16[512,640]{1,0:T(8,128)(2,1)S(1)}, u32[]{:S(2)}) copy-start(bf16[512,640]{1,0:T(8,128)(2,1)S(1)} %get-tuple-element.38.refs_1_) | copy-start | bytes 1966084
  34.5 8.6 %collective-permute-start.5 = (bf16[256,640]{1,0:T(8,128)(2,1)S(1)}, bf16[256,640]{1,0:T(8,128)(2,1)S(1)}, u32[]{:S(2)}, u32[]{:S(2)}) collective-permute-start(bf16[256,640]{1,0:T(8,128)(2,1)S(1)} %shard_map.169.refs_1_), channel_id=1, source_target_pairs={{0,2},{1,7},{2,4},{3,1},{4,6},{5,3},{6,0},{7,5},{8,10},{9,15},{10,... | collective-permute-start | bytes 983048 | tf_op jit(solution)/shard_map/ppermute | solution.py:411
  36.0 7.1 %collective-permute-start.4 = (bf16[256,640]{1,0:T(8,128)(2,1)S(1)}, bf16[256,640]{1,0:T(8,128)(2,1)S(1)}, u32[]{:S(2)}, u32[]{:S(2)}) collective-permute-start(bf16[256,640]{1,0:T(8,128)(2,1)S(1)} %shard_map.169.refs_1_), channel_id=1, source_target_pairs={{0,1},{1,0},{2,3},{3,2},{4,5},{5,4},{6,7},{7,6},{8,9},{9,8},{10,11... | collective-permute-start | bytes 983048 | tf_op jit(solution)/shard_map/ppermute | solution.py:412
  38.7 1.1 %copy-start.8 = (bf16[512,640]{1,0:T(8,128)(2,1)S(1)}, bf16[512,640]{1,0:T(8,128)(2,1)}, u32[]{:S(2)}) copy-start(bf16[512,640]{1,0:T(8,128)(2,1)} %copy-done.7) | copy-start | bytes 1966084
  43.1 7.9 %collective-permute-start.8 = (bf16[256,640]{1,0:T(8,128)(2,1)S(1)}, bf16[256,640]{1,0:T(8,128)(2,1)S(1)}, u32[]{:S(2)}, u32[]{:S(2)}) collective-permute-start(bf16[256,640]{1,0:T(8,128)(2,1)S(1)} %collective-permute-done.5.refs_1_), channel_id=1, source_target_pairs={{0,1},{1,0},{2,3},{3,2},{4,5},{5,4},{6,7},{7,6},{8,9},{9,8},{10,11... | collective-permute-start | bytes 983048 | tf_op jit(solution)/shard_map/ppermute | solution.py:416
  45.4 9.7 %collective-permute-start.7 = (bf16[256,640]{1,0:T(8,128)(2,1)S(1)}, bf16[256,640]{1,0:T(8,128)(2,1)S(1)}, u32[]{:S(2)}, u32[]{:S(2)}) collective-permute-start(bf16[256,640]{1,0:T(8,128)(2,1)S(1)} %collective-permute-done.5.refs_1_), channel_id=1, source_target_pairs={{0,2},{1,7},{2,4},{3,1},{4,6},{5,3},{6,0},{7,5},{8,10},{9,15},{10,... | collective-permute-start | bytes 983048 | tf_op jit(solution)/shard_map/ppermute | solution.py:417
  46.9 8.2 %collective-permute-start.6 = (bf16[256,640]{1,0:T(8,128)(2,1)S(1)}, bf16[256,640]{1,0:T(8,128)(2,1)S(1)}, u32[]{:S(2)}, u32[]{:S(2)}) collective-permute-start(bf16[256,640]{1,0:T(8,128)(2,1)S(1)} %collective-permute-done.4.refs_2_), channel_id=1, source_target_pairs={{0,2},{1,7},{2,4},{3,1},{4,6},{5,3},{6,0},{7,5},{8,10},{9,15},{10,... | collective-permute-start | bytes 983048 | tf_op jit(solution)/shard_map/ppermute | solution.py:415
  51.0 6.2 %copy-start.4 = (s32[32,8,8]{0,2,1:T(8,128)S(1)}, s32[32,8,8]{0,2,1:T(8,128)}, u32[]{:S(2)}) copy-start(s32[32,8,8]{0,2,1:T(8,128)} %param.26) | copy-start | bytes 24580
  51.0 6.2 %copy-start.6 = (s32[32,8,8]{0,2,1:T(8,128)S(1)}, s32[32,8,8]{0,2,1:T(8,128)}, u32[]{:S(2)}) copy-start(s32[32,8,8]{0,2,1:T(8,128)} %param.27) | copy-start | bytes 24580
  55.1 6.8 %collective-permute-start.9 = (bf16[256,640]{1,0:T(8,128)(2,1)S(1)}, bf16[256,640]{1,0:T(8,128)(2,1)S(1)}, u32[]{:S(2)}, u32[]{:S(2)}) collective-permute-start(bf16[256,640]{1,0:T(8,128)(2,1)S(1)} %collective-permute-done.6.refs_1_), channel_id=1, source_target_pairs={{0,1},{1,0},{2,3},{3,2},{4,5},{5,4},{6,7},{7,6},{8,9},{9,8},{10,11... | collective-permute-start | bytes 983048 | tf_op jit(solution)/shard_map/ppermute | solution.py:434
  57.2 4.7 %collective-permute-start.10 = (bf16[256,640]{1,0:T(8,128)(2,1)S(1)}, bf16[256,640]{1,0:T(8,128)(2,1)S(1)}, u32[]{:S(2)}, u32[]{:S(2)}) collective-permute-start(bf16[256,640]{1,0:T(8,128)(2,1)S(1)} %collective-permute-done.7.refs_2_), channel_id=1, source_target_pairs={{0,1},{1,0},{2,3},{3,2},{4,5},{5,4},{6,7},{7,6},{8,9},{9,8},{10,11... | collective-permute-start | bytes 983048 | tf_op jit(solution)/shard_map/ppermute | solution.py:435
  58.3 3.6 %copy-start = (bf16[32,512,128]{2,1,0:T(8,128)(2,1)S(1)}, bf16[32,512,128]{2,1,0:T(8,128)(2,1)}, u32[]{:S(2)}) copy-start(bf16[32,512,128]{2,1,0:T(8,128)(2,1)} %refs_6_.3) | copy-start | bytes 12582916

commit v4 on v3

--- a/solution.py
+++ b/solution.py
@@ -156,7 +156,22 @@
     )(*pieces)
 
 
-def land_kernel(own_ref, column_ref, arrived, targets, slots, out_latent, out_rope, out_scale, done):
+def gate_kernel(held, done, out):
+    pass
+
+
+def gate(held, done):
+    return pl.pallas_call(
+        gate_kernel,
+        in_specs=[ANY, ANY],
+        out_specs=ANY,
+        out_shape=jax.ShapeDtypeStruct(held.shape, held.dtype),
+        input_output_aliases={0: 0},
+        compiler_params=pltpu.CompilerParams(vmem_limit_bytes=MIB),
+    )(held, done)
+
+
+def land_kernel(own_ref, column_ref, after, arrived, targets, slots, out_latent, out_rope, out_scale, done):
     done[...] = jnp.zeros_like(done)
     own, column = own_ref[0], column_ref[0]
     new, block, width = out_latent.shape
@@ -226,7 +241,8 @@
     if last:
         value, out = refs
     else:
-        acc_out, top_out, total_out = refs
+        acc_out, top_out, total_out, done = refs
+        done[...] = jnp.zeros_like(done)
     width = value.shape[1] if last else acc_out.shape[1]
     keys = [ref[...] for ref in block_refs]
     if groups:
@@ -306,8 +322,9 @@
         out_shape = jax.ShapeDtypeStruct((tokens, rows // tokens * value.shape[2]), BF16)
         out_specs = VMEM
     else:
-        out_shape = tuple(jax.ShapeDtypeStruct((rows, n), F32) for n in (width, LANES, LANES))
-        out_specs = (VMEM, VMEM, VMEM)
+        shapes = ((rows, width), (rows, LANES), (rows, LANES), (8, LANES))
+        out_shape = tuple(jax.ShapeDtypeStruct(shape, F32) for shape in shapes)
+        out_specs = (VMEM,) * 4
     return pl.pallas_call(
         functools.partial(attend_kernel, groups, len(blocks), first, last, sub, tokens, scale),
         in_specs=specs,
@@ -408,17 +425,17 @@
     )(arrived, group_done, query_done)
 
     run = functools.partial(attend, query, tokens=tokens, width=latent, scale=scale)
+    sibling = lax.ppermute(shard, "ctx", swap)
     first = lax.ppermute(shard, "ctx", ring)
-    sibling = lax.ppermute(shard, "ctx", swap)
-    state = run([], group=group, column=column_at)
-    sibling, first, total = lax.optimization_barrier((sibling, first, state[2]))
     second = lax.ppermute(sibling, "ctx", ring)
+    *state, done = run([], group=group, column=column_at)
+    first = gate(first, done)
     first_swap = lax.ppermute(first, "ctx", swap)
     third = lax.ppermute(first, "ctx", ring)
-    state = run([shard, sibling], state=(state[0], state[1], total))
+    *state, done = run([shard, sibling], state=state)
     written_latent, written_rope, written_scale, landed = pl.pallas_call(
         land_kernel,
-        in_specs=[SMEM, SMEM] + [VMEM] * 3,
+        in_specs=[SMEM, SMEM, ANY] + [VMEM] * 3,
         out_specs=(VMEM,) * 4,
         out_shape=(
             jax.ShapeDtypeStruct((new_blocks, block, latent), BF16),
@@ -427,14 +444,14 @@
             jax.ShapeDtypeStruct((8, LANES), F32),
         ),
         compiler_params=pltpu.CompilerParams(vmem_limit_bytes=8 * MIB),
-    )(own_at, column_at, arrived, targets, target_slots)
-    first_swap, landed = lax.optimization_barrier((first_swap, landed))
-    state = run([first, first_swap], state=state)
-    second, third, total = lax.optimization_barrier((second, third, state[2]))
+    )(own_at, column_at, done, arrived, targets, target_slots)
+    second = gate(second, landed)
     second_swap = lax.ppermute(second, "ctx", swap)
+    *state, done = run([first, first_swap], state=state)
+    third = gate(third, done)
     third_swap = lax.ppermute(third, "ctx", swap)
-    state = run([second, third], state=(state[0], state[1], total))
-    attended = run([second_swap, third_swap], state=state, value=absorb_value)
+    *state, done = run([second, second_swap], state=state)
+    attended = run([third, third_swap], state=state, value=absorb_value)
     return (attended[None], written_latent[None, None], written_rope[None, None], written_scale[None, None])
 
 

time: 67.3 us -> 65.7 us (0.976)
  starting transfers between devices: 29.6 us -> 28 us
    ppermute x1, starting transfers between devices: 2.07 us -> 0.01 us  [body(): second_swap = lax.ppermute(second, 'ctx', swap)]
    ppermute x1, starting transfers between devices: 0.01 us -> 1.89 us  [body(): pair_swap = lax.ppermute(pair_first, 'ctx', swap)]
    ppermute x1, starting transfers between devices: 3.41 us -> 1.52 us  [body(): pair_far = lax.ppermute(pair_first, 'ctx', ring)]
    ppermute x1, starting transfers between devices: 2.31 us -> 0.72 us  [body(): first_swap = lax.ppermute(first, 'ctx', swap)]
    ppermute x1, starting transfers between devices: 1.51 us -> 2.72 us  [body(): first = lax.ppermute(shard, 'ctx', ring)]
    ppermute x1, starting transfers between devices: 0.01 us -> 0.81 us  [body(): third_swap = lax.ppermute(third, 'ctx', swap)]
  transfers between devices with their start and end apart: 12 -> 12, of which waited for: 3 -> 2; matrix products, arithmetic and copies ran while one was open for 0% -> 0% of each run, Pallas kernels for 26% -> 28%
where the time goes in v4:
time: 65.7 us; the launch traced here: 65.3 us
  starting transfers between devices  28 us (43%)
  Pallas kernels  26.1 us (40%)
  local copies, waits for them, and re-layouts  7.05 us (11%)
  waiting for transfers between devices  3.42 us (5%)
  between operations  0.78 us (1%)
    pallas_call x5, Pallas kernels, attend(): pl.pallas_call(functools.partial(attend_kernel, groups, len(blocks), firs...  19.6 us
    all_to_all x1, starting transfers between devices, body(): lax.all_to_all(message, 'pool', split_axis=0, concat_axis=0, tiled=True)  11.9 us
    unnamed x18, local copies, waits for them, and re-layouts  7.05 us
    pallas_call x1, Pallas kernels, body(): pl.pallas_call(pack_kernel, in_specs=[SMEM, SMEM] + [HBM] * len(operands)...  3.07 us
    ppermute x1, starting transfers between devices, body(): pair_first = lax.ppermute(pair, 'ctx', ring)  2.73 us
    ppermute x1, starting transfers between devices, body(): first = lax.ppermute(shard, 'ctx', ring)  2.72 us
    ppermute x1, starting transfers between devices, body(): sibling = lax.ppermute(shard, 'ctx', swap)  2.64 us
    ppermute x1, waiting for transfers between devices, body(): pair_first = lax.ppermute(pair, 'ctx', ring)  2.26 us
  transfers between devices with their start and end apart: 12, of which 2 were waited for; matrix products, arithmetic and copies ran while one was open for 0% of the time, Pallas kernels for 28%

profile of v4, /device:TPU:1, one launch (start us, length us, event | category | flops | bytes accessed | tf_op | source)
XLA Modules:
  0.0 65.3 jit_solution(1450353456795065878)
XLA Ops:
  0.6 3.1 %shard_map.165 = (bf16[32,16,640]{2,1,0:T(8,128)(2,1)}, bf16[64,640]{1,0:T(8,128)(2,1)}) custom-call(s32[1]{0:T(128)} %bitcast.2.own_ref, s32[1]{0:T(128)} %bitcast.3.column_ref.refs_2_, bf16[32,8,512]{2,1,0:T(8,128)(2,1)} %bitcast.23, bf16[32,512]{1,0:T(8,128)(2,1)} %bitcast.25, bf16[8,32]{1,0:T(8,128)(2,1)} %bitcast.26, bf16[64,512]{1,0:T(8,128)(2,1)} %bitcast.24, ...), custom_call_target="tpu_custom_call" | custom-call | tf_op jit(solution)/shard_map/pallas_call | solution.py:385
  3.7 11.9 %all-to-all-start = ((bf16[32,16,640]{2,1,0:T(8,128)(2,1)}), bf16[32,16,640]{2,1,0:T(8,128)(2,1)S(1)}, u32[]{:S(2)}, u32[]{:S(2)}) async-start(bf16[32,16,640]{2,1,0:T(8,128)(2,1)} %get-tuple-element.33), calls=%async_computation | async-start | bytes 1310720 | tf_op jit(solution)/shard_map/all_to_all | solution.py:397
  15.6 1.0 %collective-permute-start = (bf16[64,640]{1,0:T(8,128)(2,1)}, bf16[64,640]{1,0:T(8,128)(2,1)S(1)}, u32[]{:S(2)}, u32[]{:S(2)}) collective-permute-start(bf16[64,640]{1,0:T(8,128)(2,1)} %get-tuple-element.30.refs_0_), channel_id=1, source_target_pairs={{0,1},{1,0},{2,3},{3,2},{4,5},{5,4},{6,7},{7,6},{8,9},{9,8},{10,11... | collective-permute-start | bytes 245768 | tf_op jit(solution)/shard_map/ppermute | solution.py:399
  16.6 1.1 %collective-permute-done.refs_1_ = bf16[64,640]{1,0:T(8,128)(2,1)S(1)} collective-permute-done((bf16[64,640]{1,0:T(8,128)(2,1)}, bf16[64,640]{1,0:T(8,128)(2,1)S(1)}, u32[]{:S(2)}, u32[]{:S(2)}) %collective-permute-start) | collective-permute-done | bytes 81952 | tf_op jit(solution)/shard_map/ppermute | solution.py:399
  17.8 0.0 copy-start.5
  17.8 0.9 %copy-done.5 = bf16[64,640]{1,0:T(8,128)(2,1)S(1)} copy-done((bf16[64,640]{1,0:T(8,128)(2,1)S(1)}, bf16[64,640]{1,0:T(8,128)(2,1)}, u32[]{:S(2)}) %copy-start.5) | copy-done | bytes 81944
  18.7 0.6 shard_map.166
  19.3 2.7 %collective-permute-start.1 = (bf16[128,640]{1,0:T(8,128)(2,1)S(1)}, bf16[128,640]{1,0:T(8,128)(2,1)S(1)}, u32[]{:S(2)}, u32[]{:S(2)}) collective-permute-start(bf16[128,640]{1,0:T(8,128)(2,1)S(1)} %get-tuple-element.31.after.refs_0_), channel_id=1, source_target_pairs={{0,2},{1,7},{2,4},{3,1},{4,6},{5,3},{6,0},{7,5},{8,10},{9,15},{10,... | collective-permute-start | bytes 491528 | tf_op jit(solution)/shard_map/ppermute | solution.py:400
  22.0 2.3 %collective-permute-done.1.refs_1_ = bf16[128,640]{1,0:T(8,128)(2,1)S(1)} collective-permute-done((bf16[128,640]{1,0:T(8,128)(2,1)S(1)}, bf16[128,640]{1,0:T(8,128)(2,1)S(1)}, u32[]{:S(2)}, u32[]{:S(2)}) %collective-permute-start.1) | collective-permute-done | bytes 163872 | tf_op jit(solution)/shard_map/ppermute | solution.py:400
  24.3 1.9 %collective-permute-start.2 = (bf16[128,640]{1,0:T(8,128)(2,1)S(1)}, bf16[128,640]{1,0:T(8,128)(2,1)S(1)}, u32[]{:S(2)}, u32[]{:S(2)}) collective-permute-start(bf16[128,640]{1,0:T(8,128)(2,1)S(1)} %collective-permute-done.1.refs_1_), channel_id=1, source_target_pairs={{0,1},{1,0},{2,3},{3,2},{4,5},{5,4},{6,7},{7,6},{8,9},{9,8},{10,11... | collective-permute-start | bytes 491528 | tf_op jit(solution)/shard_map/ppermute | solution.py:415
  26.2 1.5 %collective-permute-start.3 = (bf16[128,640]{1,0:T(8,128)(2,1)S(1)}, bf16[128,640]{1,0:T(8,128)(2,1)S(1)}, u32[]{:S(2)}, u32[]{:S(2)}) collective-permute-start(bf16[128,640]{1,0:T(8,128)(2,1)S(1)} %collective-permute-done.1.refs_1_), channel_id=1, source_target_pairs={{0,2},{1,7},{2,4},{3,1},{4,6},{5,3},{6,0},{7,5},{8,10},{9,15},{10,... | collective-permute-start | bytes 491528 | tf_op jit(solution)/shard_map/ppermute | solution.py:416
  27.7 0.0 copy-start.1
  27.7 2.2 %copy-done.1 = bf16[32,128,512]{2,1,0:T(8,128)(2,1)S(1)} copy-done((bf16[32,128,512]{2,1,0:T(8,128)(2,1)S(1)}, bf16[32,128,512]{2,1,0:T(8,128)(2,1)}, u32[]{:S(2)}) %copy-start.1) | copy-done | bytes 4194328
  29.9 0.0 copy-start.2
  29.9 1.0 %copy-done.2 = bf16[1,64,4096]{2,1,0:T(8,128)(2,1)S(1)} copy-done((bf16[1,64,4096]{2,1,0:T(8,128)(2,1)S(1)}, bf16[1,64,4096]{2,1,0:T(8,128)(2,1)}, u32[]{:S(2)}) %copy-start.2) | copy-done | bytes 524312
  30.9 0.0 copy-start.3
  30.9 0.9 %copy-done.3 = bf16[1,64,2048]{2,1,0:T(8,128)(2,1)S(1)} copy-done((bf16[1,64,2048]{2,1,0:T(8,128)(2,1)S(1)}, bf16[1,64,2048]{2,1,0:T(8,128)(2,1)}, u32[]{:S(2)}) %copy-start.3) | copy-done | bytes 262168
  31.9 1.6 %shard_map.167 = (bf16[2048,640]{1,0:T(8,128)(2,1)S(1)}, f32[8,128]{1,0:T(8,128)S(1)}) custom-call(bf16[64,4096]{1,0:T(8,128)(2,1)S(1)} %bitcast.17, bf16[64,2048]{1,0:T(8,128)(2,1)S(1)} %bitcast.18, bf16[32,128,512]{2,1,0:T(8,128)(2,1)S(1)} %copy-done.1, bf16[128,640]{1,0:T(8,128)(2,1)S(1)} %get-tuple-element.31.after.refs_0_), custom_call_target="tpu_custom_call" | custom-call | flops 268435456 | bytes 8388608 | tf_op jit(solution)/shard_map/pallas_call | solution.py:402
  33.5 0.0 collective-permute-done.2.refs_2_
  33.5 0.0 collective-permute-done.3.refs_3_
  33.5 0.1 shard_map.168
  33.5 0.0 copy-start.7
  33.6 0.9 %copy-done.7 = bf16[512,640]{1,0:T(8,128)(2,1)} copy-done((bf16[512,640]{1,0:T(8,128)(2,1)}, bf16[512,640]{1,0:T(8,128)(2,1)S(1)}, u32[]{:S(2)}) %copy-start.7) | copy-done | bytes 655384
  34.4 0.0 all-to-all-done.arrived
  34.5 2.6 %collective-permute-start.7 = (bf16[256,640]{1,0:T(8,128)(2,1)S(1)}, bf16[256,640]{1,0:T(8,128)(2,1)S(1)}, u32[]{:S(2)}, u32[]{:S(2)}) collective-permute-start(bf16[256,640]{1,0:T(8,128)(2,1)S(1)} %shard_map.169.refs_1_), channel_id=1, source_target_pairs={{0,1},{1,0},{2,3},{3,2},{4,5},{5,4},{6,7},{7,6},{8,9},{9,8},{10,11... | collective-permute-start | bytes 983048 | tf_op jit(solution)/shard_map/ppermute | solution.py:428
  37.1 2.7 %collective-permute-start.4 = (bf16[256,640]{1,0:T(8,128)(2,1)S(1)}, bf16[256,640]{1,0:T(8,128)(2,1)S(1)}, u32[]{:S(2)}, u32[]{:S(2)}) collective-permute-start(bf16[256,640]{1,0:T(8,128)(2,1)S(1)} %shard_map.169.refs_1_), channel_id=1, source_target_pairs={{0,2},{1,7},{2,4},{3,1},{4,6},{5,3},{6,0},{7,5},{8,10},{9,15},{10,... | collective-permute-start | bytes 983048 | tf_op jit(solution)/shard_map/ppermute | solution.py:429
  39.8 1.1 %copy-done.8 = bf16[512,640]{1,0:T(8,128)(2,1)S(1)} copy-done((bf16[512,640]{1,0:T(8,128)(2,1)S(1)}, bf16[512,640]{1,0:T(8,128)(2,1)}, u32[]{:S(2)}) %copy-start.8) | copy-done | bytes 655384
  40.9 3.3 %shard_map.170 = (f32[2048,512]{1,0:T(8,128)S(1)}, f32[2048,128]{1,0:T(8,128)S(1)}, f32[2048,128]{1,0:T(8,128)S(1)}, f32[8,128]{1,0:T(8,128)S(1)}) custom-call(bf16[2048,640]{1,0:T(8,128)(2,1)S(1)} %get-tuple-element.32.refs_0_, bf16[512,640]{1,0:T(8,128)(2,1)S(1)} %copy-done.8, s32[1]{0:T(128)} %bitcast.3.column_ref.refs_2_), custom_call_target="tpu_custom_call" | custom-call | flops 2415919104 | bytes 1048576 | tf_op jit(solution)/shard_map/pallas_call | solution.py:328
  44.2 0.0 collective-permute-done.7.refs_2_
  44.2 0.5 collective-permute-start.9
  44.8 0.0 collective-permute-done.4.held
  44.8 0.7 %collective-permute-start.6 = (bf16[256,640]{1,0:T(8,128)(2,1)S(1)}, bf16[256,640]{1,0:T(8,128)(2,1)S(1)}, u32[]{:S(2)}, u32[]{:S(2)}) collective-permute-start(bf16[256,640]{1,0:T(8,128)(2,1)S(1)} %shard_map.171.refs_1_), channel_id=1, source_target_pairs={{0,1},{1,0},{2,3},{3,2},{4,5},{5,4},{6,7},{7,6},{8,9},{9,8},{10,11... | collective-permute-start | bytes 983048 | tf_op jit(solution)/shard_map/ppermute | solution.py:433
  45.5 1.5 %collective-permute-start.5 = (bf16[256,640]{1,0:T(8,128)(2,1)S(1)}, bf16[256,640]{1,0:T(8,128)(2,1)S(1)}, u32[]{:S(2)}, u32[]{:S(2)}) collective-permute-start(bf16[256,640]{1,0:T(8,128)(2,1)S(1)} %shard_map.171.refs_1_), channel_id=1, source_target_pairs={{0,2},{1,7},{2,4},{3,1},{4,6},{5,3},{6,0},{7,5},{8,10},{9,15},{10,... | collective-permute-start | bytes 983048 | tf_op jit(solution)/shard_map/ppermute | solution.py:434
  47.0 3.6 %shard_map.172 = (f32[2048,512]{1,0:T(8,128)S(1)}, f32[2048,128]{1,0:T(8,128)S(1)}, f32[2048,128]{1,0:T(8,128)S(1)}, f32[8,128]{1,0:T(8,128)S(1)}) custom-call(bf16[2048,640]{1,0:T(8,128)(2,1)S(1)} %get-tuple-element.32.refs_0_, bf16[256,640]{1,0:T(8,128)(2,1)S(1)} %shard_map.169.refs_1_, bf16[256,640]{1,0:T(8,128)(2,1)S(1)} %collective-permute-done.7.refs_2_, ...), custom_call_target="tpu_custom_call" | custom-call | flops 2415919104 | bytes 1048576 | tf_op jit(solution)/shard_map/pallas_call | solution.py:328
  50.6 0.0 copy-done.4
  50.6 0.0 copy-done.6
  50.6 1.1 %shard_map.175 = (bf16[8,8,512]{2,1,0:T(8,128)(2,1)}, bf16[8,512]{1,0:T(8,128)(2,1)}, bf16[8,8]{1,0:T(8,128)(2,1)}, f32[8,128]{1,0:T(8,128)S(1)}) custom-call(s32[1]{0:T(128)} %bitcast.2.own_ref, s32[1]{0:T(128)} %bitcast.3.column_ref.refs_2_, f32[8,128]{1,0:T(8,128)S(1)} %get-tuple-element.45.after, bf16[32,16,640]{2,1,0:T(8,128)(2,1)S(1)} %all-to-all-done.arrived, ...), custom_call_target="tpu_custom_call" | custom-call | tf_op jit(solution)/shard_map/pallas_call | solution.py:436
  51.7 0.0 collective-permute-done.9.held
  51.7 0.0 collective-permute-start.10
  51.7 0.0 collective-permute-done.6.refs_2_
  51.7 3.6 %shard_map.173 = (f32[2048,512]{1,0:T(8,128)S(1)}, f32[2048,128]{1,0:T(8,128)S(1)}, f32[2048,128]{1,0:T(8,128)S(1)}, f32[8,128]{1,0:T(8,128)S(1)}) custom-call(bf16[2048,640]{1,0:T(8,128)(2,1)S(1)} %get-tuple-element.32.refs_0_, bf16[256,640]{1,0:T(8,128)(2,1)S(1)} %shard_map.171.refs_1_, bf16[256,640]{1,0:T(8,128)(2,1)S(1)} %collective-permute-done.6.refs_2_, ...), custom_call_target="tpu_custom_call" | custom-call | flops 2415919104 | bytes 1048576 | tf_op jit(solution)/shard_map/pallas_call | solution.py:328
  55.3 0.0 collective-permute-done.5.held
  55.3 0.8 %collective-permute-start.8 = (bf16[256,640]{1,0:T(8,128)(2,1)S(1)}, bf16[256,640]{1,0:T(8,128)(2,1)S(1)}, u32[]{:S(2)}, u32[]{:S(2)}) collective-permute-start(bf16[256,640]{1,0:T(8,128)(2,1)S(1)} %shard_map.174.refs_1_), channel_id=1, source_target_pairs={{0,1},{1,0},{2,3},{3,2},{4,5},{5,4},{6,7},{7,6},{8,9},{9,8},{10,11... | collective-permute-start | bytes 983048 | tf_op jit(solution)/shard_map/ppermute | solution.py:452
  56.1 0.0 collective-permute-done.10.refs_2_
  56.1 4.2 %shard_map.177 = (f32[2048,512]{1,0:T(8,128)S(1)}, f32[2048,128]{1,0:T(8,128)S(1)}, f32[2048,128]{1,0:T(8,128)S(1)}, f32[8,128]{1,0:T(8,128)}) custom-call(bf16[2048,640]{1,0:T(8,128)(2,1)S(1)} %get-tuple-element.32.refs_0_, bf16[256,640]{1,0:T(8,128)(2,1)S(1)} %shard_map.176.refs_1_, bf16[256,640]{1,0:T(8,128)(2,1)S(1)} %collective-permute-done.10.refs_2_, ...), custom_call_target="tpu_custom_call" | custom-call | flops 2415919104 | bytes 1048576 | tf_op jit(solution)/shard_map/pallas_call | solution.py:328
  60.3 0.0 collective-permute-done.8.refs_2_
  60.3 0.0 copy-done
  60.3 5.0 %shard_map.178 = bf16[64,4096]{1,0:T(8,128)(2,1)} custom-call(bf16[2048,640]{1,0:T(8,128)(2,1)S(1)} %get-tuple-element.32.refs_0_, bf16[256,640]{1,0:T(8,128)(2,1)S(1)} %shard_map.174.refs_1_, bf16[256,640]{1,0:T(8,128)(2,1)S(1)} %collective-permute-done.8.refs_2_, f32[2048,512]{1,0:T(8,128)S(1)} %get-tuple-element.50.refs_3_, ...), custom_call_target="tpu_custom_call" | custom-call | flops 2415919104 | bytes 1048576 | tf_op jit(solution)/shard_map/pallas_call | solution.py:328
  (8 shorter events, 0.0 us)
Async XLA Ops:
  3.7 30.7 %all-to-all-start = ((bf16[32,16,640]{2,1,0:T(8,128)(2,1)}), bf16[32,16,640]{2,1,0:T(8,128)(2,1)S(1)}, u32[]{:S(2)}, u32[]{:S(2)}) async-start(bf16[32,16,640]{2,1,0:T(8,128)(2,1)} %get-tuple-element.33), calls=%async_computation | async-start | bytes 1310720 | tf_op jit(solution)/shard_map/all_to_all | solution.py:397
  15.6 2.2 %collective-permute-start = (bf16[64,640]{1,0:T(8,128)(2,1)}, bf16[64,640]{1,0:T(8,128)(2,1)S(1)}, u32[]{:S(2)}, u32[]{:S(2)}) collective-permute-start(bf16[64,640]{1,0:T(8,128)(2,1)} %get-tuple-element.30.refs_0_), channel_id=1, source_target_pairs={{0,1},{1,0},{2,3},{3,2},{4,5},{5,4},{6,7},{7,6},{8,9},{9,8},{10,11... | collective-permute-start | bytes 245768 | tf_op jit(solution)/shard_map/ppermute | solution.py:399
  17.8 0.9 %copy-start.5 = (bf16[64,640]{1,0:T(8,128)(2,1)S(1)}, bf16[64,640]{1,0:T(8,128)(2,1)}, u32[]{:S(2)}) copy-start(bf16[64,640]{1,0:T(8,128)(2,1)} %get-tuple-element.30.refs_0_) | copy-start | bytes 245764
  19.3 5.0 %collective-permute-start.1 = (bf16[128,640]{1,0:T(8,128)(2,1)S(1)}, bf16[128,640]{1,0:T(8,128)(2,1)S(1)}, u32[]{:S(2)}, u32[]{:S(2)}) collective-permute-start(bf16[128,640]{1,0:T(8,128)(2,1)S(1)} %get-tuple-element.31.after.refs_0_), channel_id=1, source_target_pairs={{0,2},{1,7},{2,4},{3,1},{4,6},{5,3},{6,0},{7,5},{8,10},{9,15},{10,... | collective-permute-start | bytes 491528 | tf_op jit(solution)/shard_map/ppermute | solution.py:400
  24.3 9.2 %collective-permute-start.2 = (bf16[128,640]{1,0:T(8,128)(2,1)S(1)}, bf16[128,640]{1,0:T(8,128)(2,1)S(1)}, u32[]{:S(2)}, u32[]{:S(2)}) collective-permute-start(bf16[128,640]{1,0:T(8,128)(2,1)S(1)} %collective-permute-done.1.refs_1_), channel_id=1, source_target_pairs={{0,1},{1,0},{2,3},{3,2},{4,5},{5,4},{6,7},{7,6},{8,9},{9,8},{10,11... | collective-permute-start | bytes 491528 | tf_op jit(solution)/shard_map/ppermute | solution.py:415
  26.2 7.3 %collective-permute-start.3 = (bf16[128,640]{1,0:T(8,128)(2,1)S(1)}, bf16[128,640]{1,0:T(8,128)(2,1)S(1)}, u32[]{:S(2)}, u32[]{:S(2)}) collective-permute-start(bf16[128,640]{1,0:T(8,128)(2,1)S(1)} %collective-permute-done.1.refs_1_), channel_id=1, source_target_pairs={{0,2},{1,7},{2,4},{3,1},{4,6},{5,3},{6,0},{7,5},{8,10},{9,15},{10,... | collective-permute-start | bytes 491528 | tf_op jit(solution)/shard_map/ppermute | solution.py:416
  27.7 2.2 %copy-start.1 = (bf16[32,128,512]{2,1,0:T(8,128)(2,1)S(1)}, bf16[32,128,512]{2,1,0:T(8,128)(2,1)}, u32[]{:S(2)}) copy-start(bf16[32,128,512]{2,1,0:T(8,128)(2,1)} %weight_hbm.1) | copy-start | bytes 12582916
  29.9 1.0 %copy-start.2 = (bf16[1,64,4096]{2,1,0:T(8,128)(2,1)S(1)}, bf16[1,64,4096]{2,1,0:T(8,128)(2,1)}, u32[]{:S(2)}) copy-start(bf16[1,64,4096]{2,1,0:T(8,128)(2,1)} %param.14) | copy-start | bytes 1572868
  30.9 0.9 %copy-start.3 = (bf16[1,64,2048]{2,1,0:T(8,128)(2,1)S(1)}, bf16[1,64,2048]{2,1,0:T(8,128)(2,1)}, u32[]{:S(2)}) copy-start(bf16[1,64,2048]{2,1,0:T(8,128)(2,1)} %param.15) | copy-start | bytes 786436
  33.5 0.9 %copy-start.7 = (bf16[512,640]{1,0:T(8,128)(2,1)}, bf16[512,640]{1,0:T(8,128)(2,1)S(1)}, u32[]{:S(2)}) copy-start(bf16[512,640]{1,0:T(8,128)(2,1)S(1)} %get-tuple-element.36.refs_1_) | copy-start | bytes 1966084
  34.5 9.7 %collective-permute-start.7 = (bf16[256,640]{1,0:T(8,128)(2,1)S(1)}, bf16[256,640]{1,0:T(8,128)(2,1)S(1)}, u32[]{:S(2)}, u32[]{:S(2)}) collective-permute-start(bf16[256,640]{1,0:T(8,128)(2,1)S(1)} %shard_map.169.refs_1_), channel_id=1, source_target_pairs={{0,1},{1,0},{2,3},{3,2},{4,5},{5,4},{6,7},{7,6},{8,9},{9,8},{10,11... | collective-permute-start | bytes 983048 | tf_op jit(solution)/shard_map/ppermute | solution.py:428
  37.1 7.7 %collective-permute-start.4 = (bf16[256,640]{1,0:T(8,128)(2,1)S(1)}, bf16[256,640]{1,0:T(8,128)(2,1)S(1)}, u32[]{:S(2)}, u32[]{:S(2)}) collective-permute-start(bf16[256,640]{1,0:T(8,128)(2,1)S(1)} %shard_map.169.refs_1_), channel_id=1, source_target_pairs={{0,2},{1,7},{2,4},{3,1},{4,6},{5,3},{6,0},{7,5},{8,10},{9,15},{10,... | collective-permute-start | bytes 983048 | tf_op jit(solution)/shard_map/ppermute | solution.py:429
  39.8 1.1 %copy-start.8 = (bf16[512,640]{1,0:T(8,128)(2,1)S(1)}, bf16[512,640]{1,0:T(8,128)(2,1)}, u32[]{:S(2)}) copy-start(bf16[512,640]{1,0:T(8,128)(2,1)} %copy-done.7) | copy-start | bytes 1966084
  44.2 7.5 %collective-permute-start.9 = (bf16[256,640]{1,0:T(8,128)(2,1)S(1)}, bf16[256,640]{1,0:T(8,128)(2,1)S(1)}, u32[]{:S(2)}, u32[]{:S(2)}) collective-permute-start(bf16[256,640]{1,0:T(8,128)(2,1)S(1)} %collective-permute-done.7.refs_2_), channel_id=1, source_target_pairs={{0,2},{1,7},{2,4},{3,1},{4,6},{5,3},{6,0},{7,5},{8,10},{9,15},{10,... | collective-permute-start | bytes 983048 | tf_op jit(solution)/shard_map/ppermute | solution.py:430
  44.8 6.9 %collective-permute-start.6 = (bf16[256,640]{1,0:T(8,128)(2,1)S(1)}, bf16[256,640]{1,0:T(8,128)(2,1)S(1)}, u32[]{:S(2)}, u32[]{:S(2)}) collective-permute-start(bf16[256,640]{1,0:T(8,128)(2,1)S(1)} %shard_map.171.refs_1_), channel_id=1, source_target_pairs={{0,1},{1,0},{2,3},{3,2},{4,5},{5,4},{6,7},{7,6},{8,9},{9,8},{10,11... | collective-permute-start | bytes 983048 | tf_op jit(solution)/shard_map/ppermute | solution.py:433
  45.5 9.8 %collective-permute-start.5 = (bf16[256,640]{1,0:T(8,128)(2,1)S(1)}, bf16[256,640]{1,0:T(8,128)(2,1)S(1)}, u32[]{:S(2)}, u32[]{:S(2)}) collective-permute-start(bf16[256,640]{1,0:T(8,128)(2,1)S(1)} %shard_map.171.refs_1_), channel_id=1, source_target_pairs={{0,2},{1,7},{2,4},{3,1},{4,6},{5,3},{6,0},{7,5},{8,10},{9,15},{10,... | collective-permute-start | bytes 983048 | tf_op jit(solution)/shard_map/ppermute | solution.py:434
  47.0 3.6 %copy-start.4 = (s32[32,8,8]{0,2,1:T(8,128)S(1)}, s32[32,8,8]{0,2,1:T(8,128)}, u32[]{:S(2)}) copy-start(s32[32,8,8]{0,2,1:T(8,128)} %param.26) | copy-start | bytes 24580
  47.0 3.6 %copy-start.6 = (s32[32,8,8]{0,2,1:T(8,128)S(1)}, s32[32,8,8]{0,2,1:T(8,128)}, u32[]{:S(2)}) copy-start(s32[32,8,8]{0,2,1:T(8,128)} %param.27) | copy-start | bytes 24580
  51.7 4.4 %collective-permute-start.10 = (bf16[256,640]{1,0:T(8,128)(2,1)S(1)}, bf16[256,640]{1,0:T(8,128)(2,1)S(1)}, u32[]{:S(2)}, u32[]{:S(2)}) collective-permute-start(bf16[256,640]{1,0:T(8,128)(2,1)S(1)} %shard_map.176.refs_1_), channel_id=1, source_target_pairs={{0,1},{1,0},{2,3},{3,2},{4,5},{5,4},{6,7},{7,6},{8,9},{9,8},{10,11... | collective-permute-start | bytes 983048 | tf_op jit(solution)/shard_map/ppermute | solution.py:449
  55.3 5.0 %collective-permute-start.8 = (bf16[256,640]{1,0:T(8,128)(2,1)S(1)}, bf16[256,640]{1,0:T(8,128)(2,1)S(1)}, u32[]{:S(2)}, u32[]{:S(2)}) collective-permute-start(bf16[256,640]{1,0:T(8,128)(2,1)S(1)} %shard_map.174.refs_1_), channel_id=1, source_target_pairs={{0,1},{1,0},{2,3},{3,2},{4,5},{5,4},{6,7},{7,6},{8,9},{9,8},{10,11... | collective-permute-start | bytes 983048 | tf_op jit(solution)/shard_map/ppermute | solution.py:452
  56.1 4.2 %copy-start = (bf16[32,512,128]{2,1,0:T(8,128)(2,1)S(1)}, bf16[32,512,128]{2,1,0:T(8,128)(2,1)}, u32[]{:S(2)}) copy-start(bf16[32,512,128]{2,1,0:T(8,128)(2,1)} %refs_6_.3) | copy-start | bytes 12582916

commit v5 on v4

--- a/solution.py
+++ b/solution.py
@@ -1,4 +1,5 @@
 import functools
+import math
 
 import jax
 import jax.numpy as jnp
@@ -265,7 +266,7 @@
         if groups:
             scores[0] = jnp.where(seen, scores[0], HIDDEN)
         top = functools.reduce(jnp.maximum, [jnp.max(s, axis=1, keepdims=True) for s in scores])
-        weights = [jnp.exp((s - top) * scale) for s in scores]
+        weights = [jnp.exp2((s - top) * scale) for s in scores]
         total = sum(jnp.sum(w, axis=1, keepdims=True) for w in weights)
         mixed = sum(dot(w.astype(BF16), k[:, :width]) for w, k in zip(weights, keys))
         top = jnp.broadcast_to(top, (sub, LANES))
@@ -276,8 +277,8 @@
             total_out[rows, :] = total
             continue
         joint = jnp.maximum(top, top_in[rows, :])
-        gain = jnp.exp((top - joint) * scale)
-        fade = jnp.exp((top_in[rows, :] - joint) * scale)
+        gain = jnp.exp2((top - joint) * scale)
+        fade = jnp.exp2((top_in[rows, :] - joint) * scale)
         total = total * gain + total_in[rows, :] * fade
         if last:
             inverse = 1.0 / total
@@ -364,7 +365,7 @@
     slots = pool_scale.shape[2]
     new_blocks = write_owner.shape[2]
     wide = latent + 128
-    scale = (nope + rope) ** -0.5
+    scale = (nope + rope) ** -0.5 * math.log2(math.e)
     own_at, column_at = own.reshape(1), column.reshape(1)
     ring = [(s, (s + (2 if s % 2 == 0 else -2)) % ctx) for s in range(ctx)]
     swap = [(s, s ^ 1) for s in range(ctx)]

time: 65.7 us -> 65 us (0.989)
  Pallas kernels: 26.1 us -> 25.2 us
    pallas_call x5, Pallas kernels: 19.6 us -> 18.8 us  [attend(): pl.pallas_call(functools.partial(attend_kernel, groups, len(blocks), firs...]
  transfers between devices with their start and end apart: 12 -> 12, of which waited for: 2 -> 2; matrix products, arithmetic and copies ran while one was open for 0% -> 0% of each run, Pallas kernels for 28% -> 27%
where the time goes in v5:
time: 65 us; the launch traced here: 64.6 us
  starting transfers between devices  28.1 us (43%)
  Pallas kernels  25.2 us (39%)
  local copies, waits for them, and re-layouts  7.05 us (11%)
  waiting for transfers between devices  3.42 us (5%)
  between operations  0.78 us (1%)
    pallas_call x5, Pallas kernels, attend(): pl.pallas_call(functools.partial(attend_kernel, groups, len(blocks), firs...  18.8 us
    all_to_all x1, starting transfers between devices, body(): lax.all_to_all(message, 'pool', split_axis=0, concat_axis=0, tiled=True)  11.9 us
    unnamed x18, local copies, waits for them, and re-layouts  7.05 us
    pallas_call x1, Pallas kernels, body(): pl.pallas_call(pack_kernel, in_specs=[SMEM, SMEM] + [HBM] * len(operands)...  3.07 us
    ppermute x1, starting transfers between devices, body(): pair_first = lax.ppermute(pair, 'ctx', ring)  2.73 us
    ppermute x1, starting transfers between devices, body(): first = lax.ppermute(shard, 'ctx', ring)  2.72 us
    ppermute x1, starting transfers between devices, body(): sibling = lax.ppermute(shard, 'ctx', swap)  2.64 us
    ppermute x1, waiting for transfers between devices, body(): pair_first = lax.ppermute(pair, 'ctx', ring)  2.26 us
  transfers between devices with their start and end apart: 12, of which 2 were waited for; matrix products, arithmetic and copies ran while one was open for 0% of the time, Pallas kernels for 27%

profile of v5, /device:TPU:1, one launch (start us, length us, event | category | flops | bytes accessed | tf_op | source)
XLA Modules:
  0.0 64.6 jit_solution(3847880201840674820)
XLA Ops:
  0.6 3.1 %shard_map.165 = (bf16[32,16,640]{2,1,0:T(8,128)(2,1)}, bf16[64,640]{1,0:T(8,128)(2,1)}) custom-call(s32[1]{0:T(128)} %bitcast.2.own_ref, s32[1]{0:T(128)} %bitcast.3.column_ref.refs_2_, bf16[32,8,512]{2,1,0:T(8,128)(2,1)} %bitcast.23, bf16[32,512]{1,0:T(8,128)(2,1)} %bitcast.25, bf16[8,32]{1,0:T(8,128)(2,1)} %bitcast.26, bf16[64,512]{1,0:T(8,128)(2,1)} %bitcast.24, ...), custom_call_target="tpu_custom_call" | custom-call | tf_op jit(solution)/shard_map/pallas_call | solution.py:386
  3.7 11.9 %all-to-all-start = ((bf16[32,16,640]{2,1,0:T(8,128)(2,1)}), bf16[32,16,640]{2,1,0:T(8,128)(2,1)S(1)}, u32[]{:S(2)}, u32[]{:S(2)}) async-start(bf16[32,16,640]{2,1,0:T(8,128)(2,1)} %get-tuple-element.33), calls=%async_computation | async-start | bytes 1310720 | tf_op jit(solution)/shard_map/all_to_all | solution.py:398
  15.6 1.0 %collective-permute-start = (bf16[64,640]{1,0:T(8,128)(2,1)}, bf16[64,640]{1,0:T(8,128)(2,1)S(1)}, u32[]{:S(2)}, u32[]{:S(2)}) collective-permute-start(bf16[64,640]{1,0:T(8,128)(2,1)} %get-tuple-element.30.refs_0_), channel_id=1, source_target_pairs={{0,1},{1,0},{2,3},{3,2},{4,5},{5,4},{6,7},{7,6},{8,9},{9,8},{10,11... | collective-permute-start | bytes 245768 | tf_op jit(solution)/shard_map/ppermute | solution.py:400
  16.6 1.1 %collective-permute-done.refs_1_ = bf16[64,640]{1,0:T(8,128)(2,1)S(1)} collective-permute-done((bf16[64,640]{1,0:T(8,128)(2,1)}, bf16[64,640]{1,0:T(8,128)(2,1)S(1)}, u32[]{:S(2)}, u32[]{:S(2)}) %collective-permute-start) | collective-permute-done | bytes 81952 | tf_op jit(solution)/shard_map/ppermute | solution.py:400
  17.8 0.0 copy-start.5
  17.8 0.9 %copy-done.5 = bf16[64,640]{1,0:T(8,128)(2,1)S(1)} copy-done((bf16[64,640]{1,0:T(8,128)(2,1)S(1)}, bf16[64,640]{1,0:T(8,128)(2,1)}, u32[]{:S(2)}) %copy-start.5) | copy-done | bytes 81944
  18.7 0.6 shard_map.166
  19.3 2.7 %collective-permute-start.1 = (bf16[128,640]{1,0:T(8,128)(2,1)S(1)}, bf16[128,640]{1,0:T(8,128)(2,1)S(1)}, u32[]{:S(2)}, u32[]{:S(2)}) collective-permute-start(bf16[128,640]{1,0:T(8,128)(2,1)S(1)} %get-tuple-element.31.after.refs_0_), channel_id=1, source_target_pairs={{0,2},{1,7},{2,4},{3,1},{4,6},{5,3},{6,0},{7,5},{8,10},{9,15},{10,... | collective-permute-start | bytes 491528 | tf_op jit(solution)/shard_map/ppermute | solution.py:401
  22.0 2.3 %collective-permute-done.1.refs_1_ = bf16[128,640]{1,0:T(8,128)(2,1)S(1)} collective-permute-done((bf16[128,640]{1,0:T(8,128)(2,1)S(1)}, bf16[128,640]{1,0:T(8,128)(2,1)S(1)}, u32[]{:S(2)}, u32[]{:S(2)}) %collective-permute-start.1) | collective-permute-done | bytes 163872 | tf_op jit(solution)/shard_map/ppermute | solution.py:401
  24.3 1.9 %collective-permute-start.2 = (bf16[128,640]{1,0:T(8,128)(2,1)S(1)}, bf16[128,640]{1,0:T(8,128)(2,1)S(1)}, u32[]{:S(2)}, u32[]{:S(2)}) collective-permute-start(bf16[128,640]{1,0:T(8,128)(2,1)S(1)} %collective-permute-done.1.refs_1_), channel_id=1, source_target_pairs={{0,1},{1,0},{2,3},{3,2},{4,5},{5,4},{6,7},{7,6},{8,9},{9,8},{10,11... | collective-permute-start | bytes 491528 | tf_op jit(solution)/shard_map/ppermute | solution.py:416
  26.2 1.5 %collective-permute-start.3 = (bf16[128,640]{1,0:T(8,128)(2,1)S(1)}, bf16[128,640]{1,0:T(8,128)(2,1)S(1)}, u32[]{:S(2)}, u32[]{:S(2)}) collective-permute-start(bf16[128,640]{1,0:T(8,128)(2,1)S(1)} %collective-permute-done.1.refs_1_), channel_id=1, source_target_pairs={{0,2},{1,7},{2,4},{3,1},{4,6},{5,3},{6,0},{7,5},{8,10},{9,15},{10,... | collective-permute-start | bytes 491528 | tf_op jit(solution)/shard_map/ppermute | solution.py:417
  27.7 0.0 copy-start.1
  27.7 2.2 %copy-done.1 = bf16[32,128,512]{2,1,0:T(8,128)(2,1)S(1)} copy-done((bf16[32,128,512]{2,1,0:T(8,128)(2,1)S(1)}, bf16[32,128,512]{2,1,0:T(8,128)(2,1)}, u32[]{:S(2)}) %copy-start.1) | copy-done | bytes 4194328
  29.9 1.0 %copy-done.2 = bf16[1,64,4096]{2,1,0:T(8,128)(2,1)S(1)} copy-done((bf16[1,64,4096]{2,1,0:T(8,128)(2,1)S(1)}, bf16[1,64,4096]{2,1,0:T(8,128)(2,1)}, u32[]{:S(2)}) %copy-start.2) | copy-done | bytes 524312
  30.9 0.0 copy-start.3
  30.9 0.9 %copy-done.3 = bf16[1,64,2048]{2,1,0:T(8,128)(2,1)S(1)} copy-done((bf16[1,64,2048]{2,1,0:T(8,128)(2,1)S(1)}, bf16[1,64,2048]{2,1,0:T(8,128)(2,1)}, u32[]{:S(2)}) %copy-start.3) | copy-done | bytes 262168
  31.9 1.6 %shard_map.167 = (bf16[2048,640]{1,0:T(8,128)(2,1)S(1)}, f32[8,128]{1,0:T(8,128)S(1)}) custom-call(bf16[64,4096]{1,0:T(8,128)(2,1)S(1)} %bitcast.17, bf16[64,2048]{1,0:T(8,128)(2,1)S(1)} %bitcast.18, bf16[32,128,512]{2,1,0:T(8,128)(2,1)S(1)} %copy-done.1, bf16[128,640]{1,0:T(8,128)(2,1)S(1)} %get-tuple-element.31.after.refs_0_), custom_call_target="tpu_custom_call" | custom-call | flops 268435456 | bytes 8388608 | tf_op jit(solution)/shard_map/pallas_call | solution.py:403
  33.5 0.0 collective-permute-done.2.refs_2_
  33.5 0.0 collective-permute-done.3.refs_3_
  33.5 0.1 shard_map.168
  33.5 0.0 copy-start.7
  33.6 0.9 %copy-done.7 = bf16[512,640]{1,0:T(8,128)(2,1)} copy-done((bf16[512,640]{1,0:T(8,128)(2,1)}, bf16[512,640]{1,0:T(8,128)(2,1)S(1)}, u32[]{:S(2)}) %copy-start.7) | copy-done | bytes 655384
  34.4 0.0 all-to-all-done.arrived
  34.5 2.6 %collective-permute-start.7 = (bf16[256,640]{1,0:T(8,128)(2,1)S(1)}, bf16[256,640]{1,0:T(8,128)(2,1)S(1)}, u32[]{:S(2)}, u32[]{:S(2)}) collective-permute-start(bf16[256,640]{1,0:T(8,128)(2,1)S(1)} %shard_map.169.refs_1_), channel_id=1, source_target_pairs={{0,1},{1,0},{2,3},{3,2},{4,5},{5,4},{6,7},{7,6},{8,9},{9,8},{10,11... | collective-permute-start | bytes 983048 | tf_op jit(solution)/shard_map/ppermute | solution.py:429
  37.1 2.7 %collective-permute-start.4 = (bf16[256,640]{1,0:T(8,128)(2,1)S(1)}, bf16[256,640]{1,0:T(8,128)(2,1)S(1)}, u32[]{:S(2)}, u32[]{:S(2)}) collective-permute-start(bf16[256,640]{1,0:T(8,128)(2,1)S(1)} %shard_map.169.refs_1_), channel_id=1, source_target_pairs={{0,2},{1,7},{2,4},{3,1},{4,6},{5,3},{6,0},{7,5},{8,10},{9,15},{10,... | collective-permute-start | bytes 983048 | tf_op jit(solution)/shard_map/ppermute | solution.py:430
  39.8 0.0 copy-start.8
  39.8 1.1 %copy-done.8 = bf16[512,640]{1,0:T(8,128)(2,1)S(1)} copy-done((bf16[512,640]{1,0:T(8,128)(2,1)S(1)}, bf16[512,640]{1,0:T(8,128)(2,1)}, u32[]{:S(2)}) %copy-start.8) | copy-done | bytes 655384
  40.9 3.2 %shard_map.170 = (f32[2048,512]{1,0:T(8,128)S(1)}, f32[2048,128]{1,0:T(8,128)S(1)}, f32[2048,128]{1,0:T(8,128)S(1)}, f32[8,128]{1,0:T(8,128)S(1)}) custom-call(bf16[2048,640]{1,0:T(8,128)(2,1)S(1)} %get-tuple-element.32.refs_0_, bf16[512,640]{1,0:T(8,128)(2,1)S(1)} %copy-done.8, s32[1]{0:T(128)} %bitcast.3.column_ref.refs_2_), custom_call_target="tpu_custom_call" | custom-call | flops 2415919104 | bytes 1048576 | tf_op jit(solution)/shard_map/pallas_call | solution.py:329
  44.1 0.0 collective-permute-done.7.refs_2_
  44.1 0.5 collective-permute-start.9
  44.7 0.0 collective-permute-done.4.held
  44.7 0.8 %collective-permute-start.6 = (bf16[256,640]{1,0:T(8,128)(2,1)S(1)}, bf16[256,640]{1,0:T(8,128)(2,1)S(1)}, u32[]{:S(2)}, u32[]{:S(2)}) collective-permute-start(bf16[256,640]{1,0:T(8,128)(2,1)S(1)} %shard_map.171.refs_1_), channel_id=1, source_target_pairs={{0,1},{1,0},{2,3},{3,2},{4,5},{5,4},{6,7},{7,6},{8,9},{9,8},{10,11... | collective-permute-start | bytes 983048 | tf_op jit(solution)/shard_map/ppermute | solution.py:434
  45.5 1.5 %collective-permute-start.5 = (bf16[256,640]{1,0:T(8,128)(2,1)S(1)}, bf16[256,640]{1,0:T(8,128)(2,1)S(1)}, u32[]{:S(2)}, u32[]{:S(2)}) collective-permute-start(bf16[256,640]{1,0:T(8,128)(2,1)S(1)} %shard_map.171.refs_1_), channel_id=1, source_target_pairs={{0,2},{1,7},{2,4},{3,1},{4,6},{5,3},{6,0},{7,5},{8,10},{9,15},{10,... | collective-permute-start | bytes 983048 | tf_op jit(solution)/shard_map/ppermute | solution.py:435
  47.0 3.4 %shard_map.172 = (f32[2048,512]{1,0:T(8,128)S(1)}, f32[2048,128]{1,0:T(8,128)S(1)}, f32[2048,128]{1,0:T(8,128)S(1)}, f32[8,128]{1,0:T(8,128)S(1)}) custom-call(bf16[2048,640]{1,0:T(8,128)(2,1)S(1)} %get-tuple-element.32.refs_0_, bf16[256,640]{1,0:T(8,128)(2,1)S(1)} %shard_map.169.refs_1_, bf16[256,640]{1,0:T(8,128)(2,1)S(1)} %collective-permute-done.7.refs_2_, ...), custom_call_target="tpu_custom_call" | custom-call | flops 2415919104 | bytes 1048576 | tf_op jit(solution)/shard_map/pallas_call | solution.py:329
  50.4 0.0 copy-done.4
  50.4 0.0 copy-done.6
  50.4 1.1 %shard_map.175 = (bf16[8,8,512]{2,1,0:T(8,128)(2,1)}, bf16[8,512]{1,0:T(8,128)(2,1)}, bf16[8,8]{1,0:T(8,128)(2,1)}, f32[8,128]{1,0:T(8,128)S(1)}) custom-call(s32[1]{0:T(128)} %bitcast.2.own_ref, s32[1]{0:T(128)} %bitcast.3.column_ref.refs_2_, f32[8,128]{1,0:T(8,128)S(1)} %get-tuple-element.45.after, bf16[32,16,640]{2,1,0:T(8,128)(2,1)S(1)} %all-to-all-done.arrived, ...), custom_call_target="tpu_custom_call" | custom-call | tf_op jit(solution)/shard_map/pallas_call | solution.py:437
  51.5 0.0 collective-permute-done.9.held
  51.5 0.0 collective-permute-start.10
  51.5 0.0 collective-permute-done.6.refs_2_
  51.5 3.4 %shard_map.173 = (f32[2048,512]{1,0:T(8,128)S(1)}, f32[2048,128]{1,0:T(8,128)S(1)}, f32[2048,128]{1,0:T(8,128)S(1)}, f32[8,128]{1,0:T(8,128)S(1)}) custom-call(bf16[2048,640]{1,0:T(8,128)(2,1)S(1)} %get-tuple-element.32.refs_0_, bf16[256,640]{1,0:T(8,128)(2,1)S(1)} %shard_map.171.refs_1_, bf16[256,640]{1,0:T(8,128)(2,1)S(1)} %collective-permute-done.6.refs_2_, ...), custom_call_target="tpu_custom_call" | custom-call | flops 2415919104 | bytes 1048576 | tf_op jit(solution)/shard_map/pallas_call | solution.py:329
  54.9 0.0 collective-permute-done.5.held
  55.0 0.8 %collective-permute-start.8 = (bf16[256,640]{1,0:T(8,128)(2,1)S(1)}, bf16[256,640]{1,0:T(8,128)(2,1)S(1)}, u32[]{:S(2)}, u32[]{:S(2)}) collective-permute-start(bf16[256,640]{1,0:T(8,128)(2,1)S(1)} %shard_map.174.refs_1_), channel_id=1, source_target_pairs={{0,1},{1,0},{2,3},{3,2},{4,5},{5,4},{6,7},{7,6},{8,9},{9,8},{10,11... | collective-permute-start | bytes 983048 | tf_op jit(solution)/shard_map/ppermute | solution.py:453
  55.8 0.0 collective-permute-done.10.refs_2_
  55.8 4.0 %shard_map.177 = (f32[2048,512]{1,0:T(8,128)S(1)}, f32[2048,128]{1,0:T(8,128)S(1)}, f32[2048,128]{1,0:T(8,128)S(1)}, f32[8,128]{1,0:T(8,128)}) custom-call(bf16[2048,640]{1,0:T(8,128)(2,1)S(1)} %get-tuple-element.32.refs_0_, bf16[256,640]{1,0:T(8,128)(2,1)S(1)} %shard_map.176.refs_1_, bf16[256,640]{1,0:T(8,128)(2,1)S(1)} %collective-permute-done.10.refs_2_, ...), custom_call_target="tpu_custom_call" | custom-call | flops 2415919104 | bytes 1048576 | tf_op jit(solution)/shard_map/pallas_call | solution.py:329
  59.7 0.0 collective-permute-done.8.refs_2_
  59.7 0.0 copy-done
  59.8 4.8 %shard_map.178 = bf16[64,4096]{1,0:T(8,128)(2,1)} custom-call(bf16[2048,640]{1,0:T(8,128)(2,1)S(1)} %get-tuple-element.32.refs_0_, bf16[256,640]{1,0:T(8,128)(2,1)S(1)} %shard_map.174.refs_1_, bf16[256,640]{1,0:T(8,128)(2,1)S(1)} %collective-permute-done.8.refs_2_, f32[2048,512]{1,0:T(8,128)S(1)} %get-tuple-element.50.refs_3_, ...), custom_call_target="tpu_custom_call" | custom-call | flops 2415919104 | bytes 1048576 | tf_op jit(solution)/shard_map/pallas_call | solution.py:329
  (8 shorter events, 0.0 us)
Async XLA Ops:
  3.7 30.7 %all-to-all-start = ((bf16[32,16,640]{2,1,0:T(8,128)(2,1)}), bf16[32,16,640]{2,1,0:T(8,128)(2,1)S(1)}, u32[]{:S(2)}, u32[]{:S(2)}) async-start(bf16[32,16,640]{2,1,0:T(8,128)(2,1)} %get-tuple-element.33), calls=%async_computation | async-start | bytes 1310720 | tf_op jit(solution)/shard_map/all_to_all | solution.py:398
  15.6 2.2 %collective-permute-start = (bf16[64,640]{1,0:T(8,128)(2,1)}, bf16[64,640]{1,0:T(8,128)(2,1)S(1)}, u32[]{:S(2)}, u32[]{:S(2)}) collective-permute-start(bf16[64,640]{1,0:T(8,128)(2,1)} %get-tuple-element.30.refs_0_), channel_id=1, source_target_pairs={{0,1},{1,0},{2,3},{3,2},{4,5},{5,4},{6,7},{7,6},{8,9},{9,8},{10,11... | collective-permute-start | bytes 245768 | tf_op jit(solution)/shard_map/ppermute | solution.py:400
  17.8 0.9 %copy-start.5 = (bf16[64,640]{1,0:T(8,128)(2,1)S(1)}, bf16[64,640]{1,0:T(8,128)(2,1)}, u32[]{:S(2)}) copy-start(bf16[64,640]{1,0:T(8,128)(2,1)} %get-tuple-element.30.refs_0_) | copy-start | bytes 245764
  19.3 5.0 %collective-permute-start.1 = (bf16[128,640]{1,0:T(8,128)(2,1)S(1)}, bf16[128,640]{1,0:T(8,128)(2,1)S(1)}, u32[]{:S(2)}, u32[]{:S(2)}) collective-permute-start(bf16[128,640]{1,0:T(8,128)(2,1)S(1)} %get-tuple-element.31.after.refs_0_), channel_id=1, source_target_pairs={{0,2},{1,7},{2,4},{3,1},{4,6},{5,3},{6,0},{7,5},{8,10},{9,15},{10,... | collective-permute-start | bytes 491528 | tf_op jit(solution)/shard_map/ppermute | solution.py:401
  24.3 9.2 %collective-permute-start.2 = (bf16[128,640]{1,0:T(8,128)(2,1)S(1)}, bf16[128,640]{1,0:T(8,128)(2,1)S(1)}, u32[]{:S(2)}, u32[]{:S(2)}) collective-permute-start(bf16[128,640]{1,0:T(8,128)(2,1)S(1)} %collective-permute-done.1.refs_1_), channel_id=1, source_target_pairs={{0,1},{1,0},{2,3},{3,2},{4,5},{5,4},{6,7},{7,6},{8,9},{9,8},{10,11... | collective-permute-start | bytes 491528 | tf_op jit(solution)/shard_map/ppermute | solution.py:416
  26.2 7.3 %collective-permute-start.3 = (bf16[128,640]{1,0:T(8,128)(2,1)S(1)}, bf16[128,640]{1,0:T(8,128)(2,1)S(1)}, u32[]{:S(2)}, u32[]{:S(2)}) collective-permute-start(bf16[128,640]{1,0:T(8,128)(2,1)S(1)} %collective-permute-done.1.refs_1_), channel_id=1, source_target_pairs={{0,2},{1,7},{2,4},{3,1},{4,6},{5,3},{6,0},{7,5},{8,10},{9,15},{10,... | collective-permute-start | bytes 491528 | tf_op jit(solution)/shard_map/ppermute | solution.py:417
  27.7 2.2 %copy-start.1 = (bf16[32,128,512]{2,1,0:T(8,128)(2,1)S(1)}, bf16[32,128,512]{2,1,0:T(8,128)(2,1)}, u32[]{:S(2)}) copy-start(bf16[32,128,512]{2,1,0:T(8,128)(2,1)} %weight_hbm.1) | copy-start | bytes 12582916
  29.9 1.0 %copy-start.2 = (bf16[1,64,4096]{2,1,0:T(8,128)(2,1)S(1)}, bf16[1,64,4096]{2,1,0:T(8,128)(2,1)}, u32[]{:S(2)}) copy-start(bf16[1,64,4096]{2,1,0:T(8,128)(2,1)} %param.14) | copy-start | bytes 1572868
  30.9 0.9 %copy-start.3 = (bf16[1,64,2048]{2,1,0:T(8,128)(2,1)S(1)}, bf16[1,64,2048]{2,1,0:T(8,128)(2,1)}, u32[]{:S(2)}) copy-start(bf16[1,64,2048]{2,1,0:T(8,128)(2,1)} %param.15) | copy-start | bytes 786436
  33.5 0.9 %copy-start.7 = (bf16[512,640]{1,0:T(8,128)(2,1)}, bf16[512,640]{1,0:T(8,128)(2,1)S(1)}, u32[]{:S(2)}) copy-start(bf16[512,640]{1,0:T(8,128)(2,1)S(1)} %get-tuple-element.36.refs_1_) | copy-start | bytes 1966084
  34.5 9.6 %collective-permute-start.7 = (bf16[256,640]{1,0:T(8,128)(2,1)S(1)}, bf16[256,640]{1,0:T(8,128)(2,1)S(1)}, u32[]{:S(2)}, u32[]{:S(2)}) collective-permute-start(bf16[256,640]{1,0:T(8,128)(2,1)S(1)} %shard_map.169.refs_1_), channel_id=1, source_target_pairs={{0,1},{1,0},{2,3},{3,2},{4,5},{5,4},{6,7},{7,6},{8,9},{9,8},{10,11... | collective-permute-start | bytes 983048 | tf_op jit(solution)/shard_map/ppermute | solution.py:429
  37.1 7.5 %collective-permute-start.4 = (bf16[256,640]{1,0:T(8,128)(2,1)S(1)}, bf16[256,640]{1,0:T(8,128)(2,1)S(1)}, u32[]{:S(2)}, u32[]{:S(2)}) collective-permute-start(bf16[256,640]{1,0:T(8,128)(2,1)S(1)} %shard_map.169.refs_1_), channel_id=1, source_target_pairs={{0,2},{1,7},{2,4},{3,1},{4,6},{5,3},{6,0},{7,5},{8,10},{9,15},{10,... | collective-permute-start | bytes 983048 | tf_op jit(solution)/shard_map/ppermute | solution.py:430
  39.8 1.1 %copy-start.8 = (bf16[512,640]{1,0:T(8,128)(2,1)S(1)}, bf16[512,640]{1,0:T(8,128)(2,1)}, u32[]{:S(2)}) copy-start(bf16[512,640]{1,0:T(8,128)(2,1)} %copy-done.7) | copy-start | bytes 1966084
  44.1 7.4 %collective-permute-start.9 = (bf16[256,640]{1,0:T(8,128)(2,1)S(1)}, bf16[256,640]{1,0:T(8,128)(2,1)S(1)}, u32[]{:S(2)}, u32[]{:S(2)}) collective-permute-start(bf16[256,640]{1,0:T(8,128)(2,1)S(1)} %collective-permute-done.7.refs_2_), channel_id=1, source_target_pairs={{0,2},{1,7},{2,4},{3,1},{4,6},{5,3},{6,0},{7,5},{8,10},{9,15},{10,... | collective-permute-start | bytes 983048 | tf_op jit(solution)/shard_map/ppermute | solution.py:431
  44.7 6.9 %collective-permute-start.6 = (bf16[256,640]{1,0:T(8,128)(2,1)S(1)}, bf16[256,640]{1,0:T(8,128)(2,1)S(1)}, u32[]{:S(2)}, u32[]{:S(2)}) collective-permute-start(bf16[256,640]{1,0:T(8,128)(2,1)S(1)} %shard_map.171.refs_1_), channel_id=1, source_target_pairs={{0,1},{1,0},{2,3},{3,2},{4,5},{5,4},{6,7},{7,6},{8,9},{9,8},{10,11... | collective-permute-start | bytes 983048 | tf_op jit(solution)/shard_map/ppermute | solution.py:434
  45.5 9.5 %collective-permute-start.5 = (bf16[256,640]{1,0:T(8,128)(2,1)S(1)}, bf16[256,640]{1,0:T(8,128)(2,1)S(1)}, u32[]{:S(2)}, u32[]{:S(2)}) collective-permute-start(bf16[256,640]{1,0:T(8,128)(2,1)S(1)} %shard_map.171.refs_1_), channel_id=1, source_target_pairs={{0,2},{1,7},{2,4},{3,1},{4,6},{5,3},{6,0},{7,5},{8,10},{9,15},{10,... | collective-permute-start | bytes 983048 | tf_op jit(solution)/shard_map/ppermute | solution.py:435
  47.0 3.4 %copy-start.4 = (s32[32,8,8]{0,2,1:T(8,128)S(1)}, s32[32,8,8]{0,2,1:T(8,128)}, u32[]{:S(2)}) copy-start(s32[32,8,8]{0,2,1:T(8,128)} %param.26) | copy-start | bytes 24580
  47.0 3.4 %copy-start.6 = (s32[32,8,8]{0,2,1:T(8,128)S(1)}, s32[32,8,8]{0,2,1:T(8,128)}, u32[]{:S(2)}) copy-start(s32[32,8,8]{0,2,1:T(8,128)} %param.27) | copy-start | bytes 24580
  51.5 4.3 %collective-permute-start.10 = (bf16[256,640]{1,0:T(8,128)(2,1)S(1)}, bf16[256,640]{1,0:T(8,128)(2,1)S(1)}, u32[]{:S(2)}, u32[]{:S(2)}) collective-permute-start(bf16[256,640]{1,0:T(8,128)(2,1)S(1)} %shard_map.176.refs_1_), channel_id=1, source_target_pairs={{0,1},{1,0},{2,3},{3,2},{4,5},{5,4},{6,7},{7,6},{8,9},{9,8},{10,11... | collective-permute-start | bytes 983048 | tf_op jit(solution)/shard_map/ppermute | solution.py:450
  55.0 4.8 %collective-permute-start.8 = (bf16[256,640]{1,0:T(8,128)(2,1)S(1)}, bf16[256,640]{1,0:T(8,128)(2,1)S(1)}, u32[]{:S(2)}, u32[]{:S(2)}) collective-permute-start(bf16[256,640]{1,0:T(8,128)(2,1)S(1)} %shard_map.174.refs_1_), channel_id=1, source_target_pairs={{0,1},{1,0},{2,3},{3,2},{4,5},{5,4},{6,7},{7,6},{8,9},{9,8},{10,11... | collective-permute-start | bytes 983048 | tf_op jit(solution)/shard_map/ppermute | solution.py:453
  55.8 4.0 %copy-start = (bf16[32,512,128]{2,1,0:T(8,128)(2,1)S(1)}, bf16[32,512,128]{2,1,0:T(8,128)(2,1)}, u32[]{:S(2)}) copy-start(bf16[32,512,128]{2,1,0:T(8,128)(2,1)} %refs_6_.3) | copy-start | bytes 12582916

commit v6 on v5

--- a/solution.py
+++ b/solution.py
@@ -397,8 +397,14 @@
     )(own_at, column_at, *operands)
     arrived = lax.all_to_all(message, "pool", split_axis=0, concat_axis=0, tiled=True)
 
-    pair, _ = join(suffix, lax.ppermute(suffix, "ctx", swap))
-    pair_first = lax.ppermute(pair, "ctx", ring)
+    near = lax.ppermute(suffix, "ctx", swap)
+    chip = lax.ppermute(suffix, "ctx", ring)
+    chip_near = lax.ppermute(near, "ctx", ring)
+    far = lax.ppermute(chip, "ctx", ring)
+    far_near = lax.ppermute(chip_near, "ctx", ring)
+    pieces = [suffix, near, chip, chip_near]
+    pieces += [lax.ppermute(piece, "ctx", swap) for piece in (chip, chip_near)]
+    group, group_done = join(*pieces, far, far_near)
     operands = (query_nope[0], query_rope[0], absorb_key)
     query, query_done = pl.pallas_call(
         absorb_kernel,
@@ -411,11 +417,7 @@
         cost_estimate=pl.CostEstimate(
             flops=2 * heads * tokens * nope * latent, bytes_accessed=8 * MIB, transcendentals=0
         ),
-    )(*operands, pair)
-
-    pair_swap = lax.ppermute(pair_first, "ctx", swap)
-    pair_far = lax.ppermute(pair_first, "ctx", ring)
-    group, group_done = join(pair, pair_first, pair_swap, pair_far)
+    )(*operands, near)
 
     shard = pl.pallas_call(
         shard_kernel,

time: 65 us -> 65.1 us (level)
  starting transfers between devices: 28.1 us -> 32.4 us
  waiting for transfers between devices: 3.42 us -> 0.7 us
  local copies, waits for them, and re-layouts: 7.05 us -> 6.16 us
    ppermute x4 -> x7, waiting for transfers between devices: 3.4 us -> 0.68 us  [the longest x1 0.67 us: body(): chip = lax.ppermute(suffix, 'ctx', ring)]
    ppermute x4 -> x7, starting transfers between devices: 7.19 us -> 9.29 us  [the longest x1 2.73 us: body(): chip = lax.ppermute(suffix, 'ctx', ring)]
    ppermute x1, starting transfers between devices: 2.64 us -> 4.73 us  [body(): sibling = lax.ppermute(shard, 'ctx', swap)]
    unnamed x18, local copies, waits for them, and re-layouts: 7.05 us -> 6.16 us
  transfers between devices with their start and end apart: 12 -> 15, of which waited for: 2 -> 1; matrix products, arithmetic and copies ran while one was open for 0% -> 0% of each run, Pallas kernels for 27% -> 26%
where the time goes in v6:
time: 65.1 us; the launch traced here: 64.7 us
  starting transfers between devices  32.4 us (50%)
  Pallas kernels  24.6 us (38%)
  local copies, waits for them, and re-layouts  6.16 us (9%)
  between operations  0.81 us (1%)
  waiting for transfers between devices  0.7 us (1%)
    pallas_call x5, Pallas kernels, attend(): pl.pallas_call(functools.partial(attend_kernel, groups, len(blocks), firs...  18.8 us
    all_to_all x1, starting transfers between devices, body(): lax.all_to_all(message, 'pool', split_axis=0, concat_axis=0, tiled=True)  12 us
    unnamed x18, local copies, waits for them, and re-layouts  6.16 us
    ppermute x1, starting transfers between devices, body(): sibling = lax.ppermute(shard, 'ctx', swap)  4.73 us
    pallas_call x1, Pallas kernels, body(): pl.pallas_call(pack_kernel, in_specs=[SMEM, SMEM] + [HBM] * len(operands)...  3.07 us
    ppermute x1, starting transfers between devices, body(): chip = lax.ppermute(suffix, 'ctx', ring)  2.73 us
    ppermute x1, starting transfers between devices, body(): first = lax.ppermute(shard, 'ctx', ring)  2.72 us
    ppermute x1, starting transfers between devices, body(): far = lax.ppermute(chip, 'ctx', ring)  1.79 us
  transfers between devices with their start and end apart: 15, of which 1 were waited for; matrix products, arithmetic and copies ran while one was open for 0% of the time, Pallas kernels for 26%

profile of v6, /device:TPU:1, one launch (start us, length us, event | category | flops | bytes accessed | tf_op | source)
XLA Modules:
  0.0 64.7 jit_solution(2688409076927935913)
XLA Ops:
  0.6 3.1 %shard_map.165 = (bf16[32,16,640]{2,1,0:T(8,128)(2,1)}, bf16[64,640]{1,0:T(8,128)(2,1)}) custom-call(s32[1]{0:T(128)} %bitcast.2.own_ref, s32[1]{0:T(128)} %bitcast.3.column_ref.refs_2_, bf16[32,8,512]{2,1,0:T(8,128)(2,1)} %bitcast.23, bf16[32,512]{1,0:T(8,128)(2,1)} %bitcast.25, bf16[8,32]{1,0:T(8,128)(2,1)} %bitcast.26, bf16[64,512]{1,0:T(8,128)(2,1)} %bitcast.24, ...), custom_call_target="tpu_custom_call" | custom-call | tf_op jit(solution)/shard_map/pallas_call | solution.py:386
  3.7 0.0 copy-start.5
  3.7 12.0 %all-to-all-start = ((bf16[32,16,640]{2,1,0:T(8,128)(2,1)}), bf16[32,16,640]{2,1,0:T(8,128)(2,1)S(1)}, u32[]{:S(2)}, u32[]{:S(2)}) async-start(bf16[32,16,640]{2,1,0:T(8,128)(2,1)} %get-tuple-element.31), calls=%async_computation | async-start | bytes 1310720 | tf_op jit(solution)/shard_map/all_to_all | solution.py:398
  15.7 1.0 %collective-permute-start = (bf16[64,640]{1,0:T(8,128)(2,1)}, bf16[64,640]{1,0:T(8,128)(2,1)S(1)}, u32[]{:S(2)}, u32[]{:S(2)}) collective-permute-start(bf16[64,640]{1,0:T(8,128)(2,1)} %get-tuple-element.29.refs_0_), channel_id=1, source_target_pairs={{0,1},{1,0},{2,3},{3,2},{4,5},{5,4},{6,7},{7,6},{8,9},{9,8},{10,11... | collective-permute-start | bytes 245768 | tf_op jit(solution)/shard_map/ppermute | solution.py:400
  16.8 2.7 %collective-permute-start.1 = (bf16[64,640]{1,0:T(8,128)(2,1)}, bf16[64,640]{1,0:T(8,128)(2,1)S(1)}, u32[]{:S(2)}, u32[]{:S(2)}) collective-permute-start(bf16[64,640]{1,0:T(8,128)(2,1)} %get-tuple-element.29.refs_0_), channel_id=1, source_target_pairs={{0,2},{1,7},{2,4},{3,1},{4,6},{5,3},{6,0},{7,5},{8,10},{9,15},{10,... | collective-permute-start | bytes 245768 | tf_op jit(solution)/shard_map/ppermute | solution.py:401
  19.5 0.0 collective-permute-done.after.refs_1_
  19.5 1.1 %collective-permute-start.2 = (bf16[64,640]{1,0:T(8,128)(2,1)S(1)}, bf16[64,640]{1,0:T(8,128)(2,1)S(1)}, u32[]{:S(2)}, u32[]{:S(2)}) collective-permute-start(bf16[64,640]{1,0:T(8,128)(2,1)S(1)} %collective-permute-done.after.refs_1_), channel_id=1, source_target_pairs={{0,2},{1,7},{2,4},{3,1},{4,6},{5,3},{6,0},{7,5},{8,10},{9,15},{10,... | collective-permute-start | bytes 245768 | tf_op jit(solution)/shard_map/ppermute | solution.py:402
  20.7 0.7 %collective-permute-done.1.refs_2_ = bf16[64,640]{1,0:T(8,128)(2,1)S(1)} collective-permute-done((bf16[64,640]{1,0:T(8,128)(2,1)}, bf16[64,640]{1,0:T(8,128)(2,1)S(1)}, u32[]{:S(2)}, u32[]{:S(2)}) %collective-permute-start.1) | collective-permute-done | bytes 81952 | tf_op jit(solution)/shard_map/ppermute | solution.py:401
  21.3 1.4 %collective-permute-start.3 = (bf16[64,640]{1,0:T(8,128)(2,1)S(1)}, bf16[64,640]{1,0:T(8,128)(2,1)S(1)}, u32[]{:S(2)}, u32[]{:S(2)}) collective-permute-start(bf16[64,640]{1,0:T(8,128)(2,1)S(1)} %collective-permute-done.1.refs_2_), channel_id=1, source_target_pairs={{0,1},{1,0},{2,3},{3,2},{4,5},{5,4},{6,7},{7,6},{8,9},{9,8},{10,11... | collective-permute-start | bytes 245768 | tf_op jit(solution)/shard_map/ppermute | solution.py:406
  22.7 1.8 %collective-permute-start.5 = (bf16[64,640]{1,0:T(8,128)(2,1)S(1)}, bf16[64,640]{1,0:T(8,128)(2,1)S(1)}, u32[]{:S(2)}, u32[]{:S(2)}) collective-permute-start(bf16[64,640]{1,0:T(8,128)(2,1)S(1)} %collective-permute-done.1.refs_2_), channel_id=1, source_target_pairs={{0,2},{1,7},{2,4},{3,1},{4,6},{5,3},{6,0},{7,5},{8,10},{9,15},{10,... | collective-permute-start | bytes 245768 | tf_op jit(solution)/shard_map/ppermute | solution.py:403
  24.5 0.0 collective-permute-done.2.refs_3_
  24.5 0.0 collective-permute-start.4
  24.5 1.2 %collective-permute-start.6 = (bf16[64,640]{1,0:T(8,128)(2,1)S(1)}, bf16[64,640]{1,0:T(8,128)(2,1)S(1)}, u32[]{:S(2)}, u32[]{:S(2)}) collective-permute-start(bf16[64,640]{1,0:T(8,128)(2,1)S(1)} %collective-permute-done.2.refs_3_), channel_id=1, source_target_pairs={{0,2},{1,7},{2,4},{3,1},{4,6},{5,3},{6,0},{7,5},{8,10},{9,15},{10,... | collective-permute-start | bytes 245768 | tf_op jit(solution)/shard_map/ppermute | solution.py:404
  25.7 2.2 %copy-done.1 = bf16[32,128,512]{2,1,0:T(8,128)(2,1)S(1)} copy-done((bf16[32,128,512]{2,1,0:T(8,128)(2,1)S(1)}, bf16[32,128,512]{2,1,0:T(8,128)(2,1)}, u32[]{:S(2)}) %copy-start.1) | copy-done | bytes 4194328
  27.9 1.0 %copy-done.2 = bf16[1,64,4096]{2,1,0:T(8,128)(2,1)S(1)} copy-done((bf16[1,64,4096]{2,1,0:T(8,128)(2,1)S(1)}, bf16[1,64,4096]{2,1,0:T(8,128)(2,1)}, u32[]{:S(2)}) %copy-start.2) | copy-done | bytes 524312
  28.9 0.9 %copy-done.3 = bf16[1,64,2048]{2,1,0:T(8,128)(2,1)S(1)} copy-done((bf16[1,64,2048]{2,1,0:T(8,128)(2,1)S(1)}, bf16[1,64,2048]{2,1,0:T(8,128)(2,1)}, u32[]{:S(2)}) %copy-start.3) | copy-done | bytes 262168
  29.9 1.6 %shard_map.166 = (bf16[2048,640]{1,0:T(8,128)(2,1)S(1)}, f32[8,128]{1,0:T(8,128)S(1)}) custom-call(bf16[64,4096]{1,0:T(8,128)(2,1)S(1)} %bitcast.17, bf16[64,2048]{1,0:T(8,128)(2,1)S(1)} %bitcast.18, bf16[32,128,512]{2,1,0:T(8,128)(2,1)S(1)} %copy-done.1, bf16[64,640]{1,0:T(8,128)(2,1)S(1)} %collective-permute-done.after.refs_1_), custom_call_target="tpu_custom_call" | custom-call | flops 268435456 | bytes 8388608 | tf_op jit(solution)/shard_map/pallas_call | solution.py:409
  31.5 0.0 collective-permute-done.3.refs_4_
  31.5 0.0 collective-permute-done.5.refs_6_
  31.5 0.0 collective-permute-done.4.refs_5_
  31.5 0.0 collective-permute-done.6.refs_7_
  31.5 0.0 copy-done.5
  31.5 0.1 shard_map.167
  31.6 0.0 copy-start.7
  31.6 0.9 %copy-done.7 = bf16[512,640]{1,0:T(8,128)(2,1)} copy-done((bf16[512,640]{1,0:T(8,128)(2,1)}, bf16[512,640]{1,0:T(8,128)(2,1)S(1)}, u32[]{:S(2)}) %copy-start.7) | copy-done | bytes 655384
  32.5 0.0 all-to-all-done.arrived
  32.5 4.7 %collective-permute-start.10 = (bf16[256,640]{1,0:T(8,128)(2,1)S(1)}, bf16[256,640]{1,0:T(8,128)(2,1)S(1)}, u32[]{:S(2)}, u32[]{:S(2)}) collective-permute-start(bf16[256,640]{1,0:T(8,128)(2,1)S(1)} %shard_map.168.refs_1_), channel_id=1, source_target_pairs={{0,1},{1,0},{2,3},{3,2},{4,5},{5,4},{6,7},{7,6},{8,9},{9,8},{10,11... | collective-permute-start | bytes 983048 | tf_op jit(solution)/shard_map/ppermute | solution.py:431
  37.3 2.7 %collective-permute-start.7 = (bf16[256,640]{1,0:T(8,128)(2,1)S(1)}, bf16[256,640]{1,0:T(8,128)(2,1)S(1)}, u32[]{:S(2)}, u32[]{:S(2)}) collective-permute-start(bf16[256,640]{1,0:T(8,128)(2,1)S(1)} %shard_map.168.refs_1_), channel_id=1, source_target_pairs={{0,2},{1,7},{2,4},{3,1},{4,6},{5,3},{6,0},{7,5},{8,10},{9,15},{10,... | collective-permute-start | bytes 983048 | tf_op jit(solution)/shard_map/ppermute | solution.py:432
  40.0 1.1 %copy-done.8 = bf16[512,640]{1,0:T(8,128)(2,1)S(1)} copy-done((bf16[512,640]{1,0:T(8,128)(2,1)S(1)}, bf16[512,640]{1,0:T(8,128)(2,1)}, u32[]{:S(2)}) %copy-start.8) | copy-done | bytes 655384
  41.1 3.2 %shard_map.169 = (f32[2048,512]{1,0:T(8,128)S(1)}, f32[2048,128]{1,0:T(8,128)S(1)}, f32[2048,128]{1,0:T(8,128)S(1)}, f32[8,128]{1,0:T(8,128)S(1)}) custom-call(bf16[2048,640]{1,0:T(8,128)(2,1)S(1)} %get-tuple-element.30.refs_0_, bf16[512,640]{1,0:T(8,128)(2,1)S(1)} %copy-done.8, s32[1]{0:T(128)} %bitcast.3.column_ref.refs_2_), custom_call_target="tpu_custom_call" | custom-call | flops 2415919104 | bytes 1048576 | tf_op jit(solution)/shard_map/pallas_call | solution.py:329
  44.2 0.0 collective-permute-done.10.refs_2_
  44.2 0.5 collective-permute-start.12
  44.8 0.0 collective-permute-done.7.held
  44.8 0.8 %collective-permute-start.9 = (bf16[256,640]{1,0:T(8,128)(2,1)S(1)}, bf16[256,640]{1,0:T(8,128)(2,1)S(1)}, u32[]{:S(2)}, u32[]{:S(2)}) collective-permute-start(bf16[256,640]{1,0:T(8,128)(2,1)S(1)} %shard_map.170.refs_1_), channel_id=1, source_target_pairs={{0,1},{1,0},{2,3},{3,2},{4,5},{5,4},{6,7},{7,6},{8,9},{9,8},{10,11... | collective-permute-start | bytes 983048 | tf_op jit(solution)/shard_map/ppermute | solution.py:436
  45.6 1.5 %collective-permute-start.8 = (bf16[256,640]{1,0:T(8,128)(2,1)S(1)}, bf16[256,640]{1,0:T(8,128)(2,1)S(1)}, u32[]{:S(2)}, u32[]{:S(2)}) collective-permute-start(bf16[256,640]{1,0:T(8,128)(2,1)S(1)} %shard_map.170.refs_1_), channel_id=1, source_target_pairs={{0,2},{1,7},{2,4},{3,1},{4,6},{5,3},{6,0},{7,5},{8,10},{9,15},{10,... | collective-permute-start | bytes 983048 | tf_op jit(solution)/shard_map/ppermute | solution.py:437
  47.1 3.4 %shard_map.171 = (f32[2048,512]{1,0:T(8,128)S(1)}, f32[2048,128]{1,0:T(8,128)S(1)}, f32[2048,128]{1,0:T(8,128)S(1)}, f32[8,128]{1,0:T(8,128)S(1)}) custom-call(bf16[2048,640]{1,0:T(8,128)(2,1)S(1)} %get-tuple-element.30.refs_0_, bf16[256,640]{1,0:T(8,128)(2,1)S(1)} %shard_map.168.refs_1_, bf16[256,640]{1,0:T(8,128)(2,1)S(1)} %collective-permute-done.10.refs_2_, ...), custom_call_target="tpu_custom_call" | custom-call | flops 2415919104 | bytes 1048576 | tf_op jit(solution)/shard_map/pallas_call | solution.py:329
  50.6 1.1 %shard_map.174 = (bf16[8,8,512]{2,1,0:T(8,128)(2,1)}, bf16[8,512]{1,0:T(8,128)(2,1)}, bf16[8,8]{1,0:T(8,128)(2,1)}, f32[8,128]{1,0:T(8,128)S(1)}) custom-call(s32[1]{0:T(128)} %bitcast.2.own_ref, s32[1]{0:T(128)} %bitcast.3.column_ref.refs_2_, f32[8,128]{1,0:T(8,128)S(1)} %get-tuple-element.43.after, bf16[32,16,640]{2,1,0:T(8,128)(2,1)S(1)} %all-to-all-done.arrived, ...), custom_call_target="tpu_custom_call" | custom-call | tf_op jit(solution)/shard_map/pallas_call | solution.py:439
  51.7 0.0 collective-permute-done.12.held
  51.7 0.0 collective-permute-start.13
  51.7 0.0 collective-permute-done.9.refs_2_
  51.7 3.4 %shard_map.172 = (f32[2048,512]{1,0:T(8,128)S(1)}, f32[2048,128]{1,0:T(8,128)S(1)}, f32[2048,128]{1,0:T(8,128)S(1)}, f32[8,128]{1,0:T(8,128)S(1)}) custom-call(bf16[2048,640]{1,0:T(8,128)(2,1)S(1)} %get-tuple-element.30.refs_0_, bf16[256,640]{1,0:T(8,128)(2,1)S(1)} %shard_map.170.refs_1_, bf16[256,640]{1,0:T(8,128)(2,1)S(1)} %collective-permute-done.9.refs_2_, ...), custom_call_target="tpu_custom_call" | custom-call | flops 2415919104 | bytes 1048576 | tf_op jit(solution)/shard_map/pallas_call | solution.py:329
  55.1 0.0 collective-permute-done.8.held
  55.1 0.8 %collective-permute-start.11 = (bf16[256,640]{1,0:T(8,128)(2,1)S(1)}, bf16[256,640]{1,0:T(8,128)(2,1)S(1)}, u32[]{:S(2)}, u32[]{:S(2)}) collective-permute-start(bf16[256,640]{1,0:T(8,128)(2,1)S(1)} %shard_map.173.refs_1_), channel_id=1, source_target_pairs={{0,1},{1,0},{2,3},{3,2},{4,5},{5,4},{6,7},{7,6},{8,9},{9,8},{10,11... | collective-permute-start | bytes 983048 | tf_op jit(solution)/shard_map/ppermute | solution.py:455
  55.9 0.0 collective-permute-done.13.refs_2_
  55.9 4.0 %shard_map.176 = (f32[2048,512]{1,0:T(8,128)S(1)}, f32[2048,128]{1,0:T(8,128)S(1)}, f32[2048,128]{1,0:T(8,128)S(1)}, f32[8,128]{1,0:T(8,128)}) custom-call(bf16[2048,640]{1,0:T(8,128)(2,1)S(1)} %get-tuple-element.30.refs_0_, bf16[256,640]{1,0:T(8,128)(2,1)S(1)} %shard_map.175.refs_1_, bf16[256,640]{1,0:T(8,128)(2,1)S(1)} %collective-permute-done.13.refs_2_, ...), custom_call_target="tpu_custom_call" | custom-call | flops 2415919104 | bytes 1048576 | tf_op jit(solution)/shard_map/pallas_call | solution.py:329
  59.9 0.0 collective-permute-done.11.refs_2_
  59.9 0.0 copy-done
  59.9 4.8 %shard_map.177 = bf16[64,4096]{1,0:T(8,128)(2,1)} custom-call(bf16[2048,640]{1,0:T(8,128)(2,1)S(1)} %get-tuple-element.30.refs_0_, bf16[256,640]{1,0:T(8,128)(2,1)S(1)} %shard_map.173.refs_1_, bf16[256,640]{1,0:T(8,128)(2,1)S(1)} %collective-permute-done.11.refs_2_, f32[2048,512]{1,0:T(8,128)S(1)} %get-tuple-element.48.refs_3_, ...), custom_call_target="tpu_custom_call" | custom-call | flops 2415919104 | bytes 1048576 | tf_op jit(solution)/shard_map/pallas_call | solution.py:329
  (13 shorter events, 0.0 us)
Async XLA Ops:
  3.7 27.8 %copy-start.5 = (bf16[64,640]{1,0:T(8,128)(2,1)S(1)}, bf16[64,640]{1,0:T(8,128)(2,1)}, u32[]{:S(2)}) copy-start(bf16[64,640]{1,0:T(8,128)(2,1)} %get-tuple-element.29.refs_0_) | copy-start | bytes 245764
  3.7 28.8 %all-to-all-start = ((bf16[32,16,640]{2,1,0:T(8,128)(2,1)}), bf16[32,16,640]{2,1,0:T(8,128)(2,1)S(1)}, u32[]{:S(2)}, u32[]{:S(2)}) async-start(bf16[32,16,640]{2,1,0:T(8,128)(2,1)} %get-tuple-element.31), calls=%async_computation | async-start | bytes 1310720 | tf_op jit(solution)/shard_map/all_to_all | solution.py:398
  15.7 3.8 %collective-permute-start = (bf16[64,640]{1,0:T(8,128)(2,1)}, bf16[64,640]{1,0:T(8,128)(2,1)S(1)}, u32[]{:S(2)}, u32[]{:S(2)}) collective-permute-start(bf16[64,640]{1,0:T(8,128)(2,1)} %get-tuple-element.29.refs_0_), channel_id=1, source_target_pairs={{0,1},{1,0},{2,3},{3,2},{4,5},{5,4},{6,7},{7,6},{8,9},{9,8},{10,11... | collective-permute-start | bytes 245768 | tf_op jit(solution)/shard_map/ppermute | solution.py:400
  16.8 4.5 %collective-permute-start.1 = (bf16[64,640]{1,0:T(8,128)(2,1)}, bf16[64,640]{1,0:T(8,128)(2,1)S(1)}, u32[]{:S(2)}, u32[]{:S(2)}) collective-permute-start(bf16[64,640]{1,0:T(8,128)(2,1)} %get-tuple-element.29.refs_0_), channel_id=1, source_target_pairs={{0,2},{1,7},{2,4},{3,1},{4,6},{5,3},{6,0},{7,5},{8,10},{9,15},{10,... | collective-permute-start | bytes 245768 | tf_op jit(solution)/shard_map/ppermute | solution.py:401
  19.5 5.0 %collective-permute-start.2 = (bf16[64,640]{1,0:T(8,128)(2,1)S(1)}, bf16[64,640]{1,0:T(8,128)(2,1)S(1)}, u32[]{:S(2)}, u32[]{:S(2)}) collective-permute-start(bf16[64,640]{1,0:T(8,128)(2,1)S(1)} %collective-permute-done.after.refs_1_), channel_id=1, source_target_pairs={{0,2},{1,7},{2,4},{3,1},{4,6},{5,3},{6,0},{7,5},{8,10},{9,15},{10,... | collective-permute-start | bytes 245768 | tf_op jit(solution)/shard_map/ppermute | solution.py:402
  21.3 10.2 %collective-permute-start.3 = (bf16[64,640]{1,0:T(8,128)(2,1)S(1)}, bf16[64,640]{1,0:T(8,128)(2,1)S(1)}, u32[]{:S(2)}, u32[]{:S(2)}) collective-permute-start(bf16[64,640]{1,0:T(8,128)(2,1)S(1)} %collective-permute-done.1.refs_2_), channel_id=1, source_target_pairs={{0,1},{1,0},{2,3},{3,2},{4,5},{5,4},{6,7},{7,6},{8,9},{9,8},{10,11... | collective-permute-start | bytes 245768 | tf_op jit(solution)/shard_map/ppermute | solution.py:406
  22.7 8.8 %collective-permute-start.5 = (bf16[64,640]{1,0:T(8,128)(2,1)S(1)}, bf16[64,640]{1,0:T(8,128)(2,1)S(1)}, u32[]{:S(2)}, u32[]{:S(2)}) collective-permute-start(bf16[64,640]{1,0:T(8,128)(2,1)S(1)} %collective-permute-done.1.refs_2_), channel_id=1, source_target_pairs={{0,2},{1,7},{2,4},{3,1},{4,6},{5,3},{6,0},{7,5},{8,10},{9,15},{10,... | collective-permute-start | bytes 245768 | tf_op jit(solution)/shard_map/ppermute | solution.py:403
  24.5 7.0 %collective-permute-start.4 = (bf16[64,640]{1,0:T(8,128)(2,1)S(1)}, bf16[64,640]{1,0:T(8,128)(2,1)S(1)}, u32[]{:S(2)}, u32[]{:S(2)}) collective-permute-start(bf16[64,640]{1,0:T(8,128)(2,1)S(1)} %collective-permute-done.2.refs_3_), channel_id=1, source_target_pairs={{0,1},{1,0},{2,3},{3,2},{4,5},{5,4},{6,7},{7,6},{8,9},{9,8},{10,11... | collective-permute-start | bytes 245768 | tf_op jit(solution)/shard_map/ppermute | solution.py:406
  24.5 7.0 %collective-permute-start.6 = (bf16[64,640]{1,0:T(8,128)(2,1)S(1)}, bf16[64,640]{1,0:T(8,128)(2,1)S(1)}, u32[]{:S(2)}, u32[]{:S(2)}) collective-permute-start(bf16[64,640]{1,0:T(8,128)(2,1)S(1)} %collective-permute-done.2.refs_3_), channel_id=1, source_target_pairs={{0,2},{1,7},{2,4},{3,1},{4,6},{5,3},{6,0},{7,5},{8,10},{9,15},{10,... | collective-permute-start | bytes 245768 | tf_op jit(solution)/shard_map/ppermute | solution.py:404
  25.7 2.2 %copy-start.1 = (bf16[32,128,512]{2,1,0:T(8,128)(2,1)S(1)}, bf16[32,128,512]{2,1,0:T(8,128)(2,1)}, u32[]{:S(2)}) copy-start(bf16[32,128,512]{2,1,0:T(8,128)(2,1)} %weight_hbm.1) | copy-start | bytes 12582916
  27.9 1.0 %copy-start.2 = (bf16[1,64,4096]{2,1,0:T(8,128)(2,1)S(1)}, bf16[1,64,4096]{2,1,0:T(8,128)(2,1)}, u32[]{:S(2)}) copy-start(bf16[1,64,4096]{2,1,0:T(8,128)(2,1)} %param.14) | copy-start | bytes 1572868
  28.9 0.9 %copy-start.3 = (bf16[1,64,2048]{2,1,0:T(8,128)(2,1)S(1)}, bf16[1,64,2048]{2,1,0:T(8,128)(2,1)}, u32[]{:S(2)}) copy-start(bf16[1,64,2048]{2,1,0:T(8,128)(2,1)} %param.15) | copy-start | bytes 786436
  31.6 0.9 %copy-start.7 = (bf16[512,640]{1,0:T(8,128)(2,1)}, bf16[512,640]{1,0:T(8,128)(2,1)S(1)}, u32[]{:S(2)}) copy-start(bf16[512,640]{1,0:T(8,128)(2,1)S(1)} %get-tuple-element.34.refs_1_) | copy-start | bytes 1966084
  32.5 11.7 %collective-permute-start.10 = (bf16[256,640]{1,0:T(8,128)(2,1)S(1)}, bf16[256,640]{1,0:T(8,128)(2,1)S(1)}, u32[]{:S(2)}, u32[]{:S(2)}) collective-permute-start(bf16[256,640]{1,0:T(8,128)(2,1)S(1)} %shard_map.168.refs_1_), channel_id=1, source_target_pairs={{0,1},{1,0},{2,3},{3,2},{4,5},{5,4},{6,7},{7,6},{8,9},{9,8},{10,11... | collective-permute-start | bytes 983048 | tf_op jit(solution)/shard_map/ppermute | solution.py:431
  37.3 7.5 %collective-permute-start.7 = (bf16[256,640]{1,0:T(8,128)(2,1)S(1)}, bf16[256,640]{1,0:T(8,128)(2,1)S(1)}, u32[]{:S(2)}, u32[]{:S(2)}) collective-permute-start(bf16[256,640]{1,0:T(8,128)(2,1)S(1)} %shard_map.168.refs_1_), channel_id=1, source_target_pairs={{0,2},{1,7},{2,4},{3,1},{4,6},{5,3},{6,0},{7,5},{8,10},{9,15},{10,... | collective-permute-start | bytes 983048 | tf_op jit(solution)/shard_map/ppermute | solution.py:432
  40.0 1.1 %copy-start.8 = (bf16[512,640]{1,0:T(8,128)(2,1)S(1)}, bf16[512,640]{1,0:T(8,128)(2,1)}, u32[]{:S(2)}) copy-start(bf16[512,640]{1,0:T(8,128)(2,1)} %copy-done.7) | copy-start | bytes 1966084
  44.2 7.4 %collective-permute-start.12 = (bf16[256,640]{1,0:T(8,128)(2,1)S(1)}, bf16[256,640]{1,0:T(8,128)(2,1)S(1)}, u32[]{:S(2)}, u32[]{:S(2)}) collective-permute-start(bf16[256,640]{1,0:T(8,128)(2,1)S(1)} %collective-permute-done.10.refs_2_), channel_id=1, source_target_pairs={{0,2},{1,7},{2,4},{3,1},{4,6},{5,3},{6,0},{7,5},{8,10},{9,15},{10,... | collective-permute-start | bytes 983048 | tf_op jit(solution)/shard_map/ppermute | solution.py:433
  44.8 6.9 %collective-permute-start.9 = (bf16[256,640]{1,0:T(8,128)(2,1)S(1)}, bf16[256,640]{1,0:T(8,128)(2,1)S(1)}, u32[]{:S(2)}, u32[]{:S(2)}) collective-permute-start(bf16[256,640]{1,0:T(8,128)(2,1)S(1)} %shard_map.170.refs_1_), channel_id=1, source_target_pairs={{0,1},{1,0},{2,3},{3,2},{4,5},{5,4},{6,7},{7,6},{8,9},{9,8},{10,11... | collective-permute-start | bytes 983048 | tf_op jit(solution)/shard_map/ppermute | solution.py:436
  45.6 9.5 %collective-permute-start.8 = (bf16[256,640]{1,0:T(8,128)(2,1)S(1)}, bf16[256,640]{1,0:T(8,128)(2,1)S(1)}, u32[]{:S(2)}, u32[]{:S(2)}) collective-permute-start(bf16[256,640]{1,0:T(8,128)(2,1)S(1)} %shard_map.170.refs_1_), channel_id=1, source_target_pairs={{0,2},{1,7},{2,4},{3,1},{4,6},{5,3},{6,0},{7,5},{8,10},{9,15},{10,... | collective-permute-start | bytes 983048 | tf_op jit(solution)/shard_map/ppermute | solution.py:437
  47.1 3.4 %copy-start.4 = (s32[32,8,8]{0,2,1:T(8,128)S(1)}, s32[32,8,8]{0,2,1:T(8,128)}, u32[]{:S(2)}) copy-start(s32[32,8,8]{0,2,1:T(8,128)} %param.26) | copy-start | bytes 24580
  47.1 3.4 %copy-start.6 = (s32[32,8,8]{0,2,1:T(8,128)S(1)}, s32[32,8,8]{0,2,1:T(8,128)}, u32[]{:S(2)}) copy-start(s32[32,8,8]{0,2,1:T(8,128)} %param.27) | copy-start | bytes 24580
  51.7 4.3 %collective-permute-start.13 = (bf16[256,640]{1,0:T(8,128)(2,1)S(1)}, bf16[256,640]{1,0:T(8,128)(2,1)S(1)}, u32[]{:S(2)}, u32[]{:S(2)}) collective-permute-start(bf16[256,640]{1,0:T(8,128)(2,1)S(1)} %shard_map.175.refs_1_), channel_id=1, source_target_pairs={{0,1},{1,0},{2,3},{3,2},{4,5},{5,4},{6,7},{7,6},{8,9},{9,8},{10,11... | collective-permute-start | bytes 983048 | tf_op jit(solution)/shard_map/ppermute | solution.py:452
  55.1 4.8 %collective-permute-start.11 = (bf16[256,640]{1,0:T(8,128)(2,1)S(1)}, bf16[256,640]{1,0:T(8,128)(2,1)S(1)}, u32[]{:S(2)}, u32[]{:S(2)}) collective-permute-start(bf16[256,640]{1,0:T(8,128)(2,1)S(1)} %shard_map.173.refs_1_), channel_id=1, source_target_pairs={{0,1},{1,0},{2,3},{3,2},{4,5},{5,4},{6,7},{7,6},{8,9},{9,8},{10,11... | collective-permute-start | bytes 983048 | tf_op jit(solution)/shard_map/ppermute | solution.py:455
  55.9 4.0 %copy-start = (bf16[32,512,128]{2,1,0:T(8,128)(2,1)S(1)}, bf16[32,512,128]{2,1,0:T(8,128)(2,1)}, u32[]{:S(2)}) copy-start(bf16[32,512,128]{2,1,0:T(8,128)(2,1)} %refs_6_.3) | copy-start | bytes 12582916
